TPU v7x, 32 devices: a whole 2x2x4 slice. The times are simulated.
32 devices in a mesh: panel: 2 (over x), rad: 2 (over y), ang: 8 (over z, core).
Axes of the slice: x: 2, y: 2, z: 4, core: 2. Of those that a mesh axis runs over, the one named last changes fastest.
Arguments:
- adj_final: float32 [2, 7, 2, 64, 1536], P('panel', None, 'rad', 'ang'), may hold values from -6 to 6
- cond: float32 [2, 2, 64, 1536], P('panel', 'rad', 'ang'), may hold values from 0.5 to 1.5
- diffus: float32 [7], replicated, may hold values from 0.02 to 0.1
- couple: float32 [7, 7], replicated, may hold values from -0.1 to 0.1
- ghost_row: int32 [2, 4, 64], replicated, may hold values from 0 to 63
- ghost_col: int32 [2, 4, 64], replicated, may hold values from 0 to 1535
- ghost_wt: float32 [2, 4, 64], replicated, may hold values from 0.5 to 1.5
- obs_dest: int32 [2, 2, 2048, 1], P('panel', 'rad', 'ang'), may hold values from 0 to 7; in each aligned block of 256 rows (0 to 255, 256 to 511, ..., all dimensions but the last counted through in order) at most 64 rows name the same one
- obs_cell: int32 [2, 2, 4, 2048], P('panel', 'rad', None, 'ang'), may hold values from 0 to 12287
- obs_wt: float32 [2, 2, 4, 2048], P('panel', 'rad', None, 'ang'), may hold values from 0.2 to 1
- misfit: float32 [2, 2, 2, 2048], P('panel', 'rad', None, 'ang'), may hold values from -6 to 6
Outputs:
- adj_start: float32 [2, 7, 2, 64, 1536], P('panel', None, 'rad', 'ang')
Inputs may be any that keep to these rules, and one draw needn't show every extreme that they name: `obs_dest`: owner tile, within the observation's own panel, whose outermost layer holds it; among the 256 observations of one device at most 64 name one owner. `obs_cell`: row within the owner's tile times 1536 plus column.
All inputs are finite; a program needn't handle non-finite values.
Results may differ from a plain program's by a relative error of at most 0.000088.
Values sent between devices are 32-bit elements; how exact they have to be, the bound alone decides.
No kernel may reach another device: no remote copies, remote signals or barrier semaphores. Data moves between devices by JAX's collectives and lax.ppermute only.
A program may use at most 64 MiB of HBM per device.

v0:
```python
import jax
import jax.numpy as jnp
from jax import lax
from jax.sharding import PartitionSpec as P


def swapped(x, axis, apart):
    return lax.ppermute(x, axis, [(i, i ^ 1 << apart) for i in range(lax.axis_size(axis))])


def extended(block, sides, width):
    for axis, dim in sides:
        count = lax.axis_size(axis)
        forward = [(i, i + 1) for i in range(count - 1)]
        backward = [(target, source) for source, target in forward]
        low = lax.ppermute(
            lax.slice_in_dim(block, block.shape[dim] - width, None, axis=dim), axis, forward
        )
        high = lax.ppermute(lax.slice_in_dim(block, 0, width, axis=dim), axis, backward)
        block = jnp.concatenate([low, block, high], axis=dim)
    return block


def deposit(inbox, cells_total):
    values = inbox[:8].reshape(2, -1)
    cells = inbox[8:].astype(jnp.int32).reshape(-1)
    dense = jnp.zeros((2, cells_total), jnp.float32)
    return dense.at[:, cells].add(values, mode="drop")


def route_obs(obs_dest, obs_cell, obs_wt, misfit, cells_total):
    target = obs_dest[0, 0, :, 0]
    count = target.shape[0]
    owners = lax.axis_size("ang")
    slots = 2 * count // owners
    onehot = (target[:, None] == jnp.arange(owners, dtype=jnp.int32)[None]).astype(jnp.int32)
    before = jnp.cumsum(onehot, axis=0) - onehot
    ranking = jnp.sum(before * onehot, axis=1)
    position = target * slots + ranking
    values = (misfit[0, 0][:, None, :] * obs_wt[0, 0][None]).reshape(8, count)
    payload = jnp.concatenate([values, obs_cell[0, 0].astype(jnp.float32)], axis=0)
    blank = jnp.concatenate(
        [
            jnp.zeros((8, owners * slots), jnp.float32),
            jnp.full((4, owners * slots), cells_total, jnp.float32),
        ],
        axis=0,
    )
    outbox = blank.at[:, position].set(payload)
    inbox = lax.all_to_all(outbox, "ang", split_axis=1, concat_axis=1, tiled=True)
    dense = deposit(inbox, cells_total)
    return lax.psum(dense, "rad")


def other_edges(edges):
    across = swapped(edges, "panel", 0)
    return lax.all_gather(across, "ang", axis=3, tiled=True)


def ghost_terms(scaled_own, row_start, central_rows, ghost_row, ghost_col, ghost_wt):
    fields, layers, tile_rows, columns = scaled_own.shape
    edges = jnp.stack([scaled_own[..., 0], scaled_own[..., -1]], axis=2)
    gathered = other_edges(edges)
    values = gathered[:, :, :, None, :] * ghost_wt[None, None]
    local_row = ghost_row - row_start
    inside = (local_row >= 0) & (local_row < central_rows)
    flat_index = jnp.where(inside, local_row * columns + ghost_col, central_rows * columns).reshape(
        -1
    )
    target = jnp.zeros((fields, layers, central_rows * columns), jnp.float32)
    target = target.at[:, :, flat_index].add(values.reshape(fields, layers, -1), mode="drop")
    return target.reshape(fields, layers, central_rows, columns)


def finish(padded, centre, ghost_add, source, couple, row_start, total_rows):
    middle = padded[:, 1:-1, 1:-1]
    lap = padded[:, 2:, 1:-1] + padded[:, :-2, 1:-1] + padded[:, 1:-1, 2:] + padded[:, 1:-1, :-2]
    west = jnp.pad(middle[..., :-1], ((0, 0), (0, 0), (0, 0), (1, 0)))
    east = jnp.pad(middle[..., 1:], ((0, 0), (0, 0), (0, 0), (0, 1)))
    lap = lap + west + east - 6.0 * middle
    coupled = jnp.einsum("ec,elrk->clrk", couple, centre, precision=lax.Precision.HIGHEST)
    updated = centre + lap + ghost_add + coupled
    updated = updated.at[3].add(source)
    global_rows = row_start + jnp.arange(centre.shape[2], dtype=jnp.int32)
    inside = ((global_rows >= 0) & (global_rows < total_rows)).astype(jnp.float32)
    return updated * inside[None, None, :, None]


def shallow_step(
    adjoint, coeff, source, couple, row_start, total_rows, ghost_row, ghost_col, ghost_wt
):
    scaled = coeff * adjoint
    padded = extended(scaled, (("rad", 1), ("ang", 2)), 1)
    ghost_add = ghost_terms(scaled, row_start, adjoint.shape[2], ghost_row, ghost_col, ghost_wt)
    return finish(padded, adjoint, ghost_add, source, couple, row_start, total_rows)


def body(
    adj_final,
    cond,
    diffus,
    couple,
    ghost_row,
    ghost_col,
    ghost_wt,
    obs_dest,
    obs_cell,
    obs_wt,
    misfit,
):
    adjoint = adj_final[0]
    conduct = cond[0]
    fields, layers, tile_rows, columns = adjoint.shape
    total_rows = tile_rows * lax.axis_size("ang")
    row_start = lax.axis_index("ang") * tile_rows
    outer = (lax.axis_index("rad") == lax.axis_size("rad") - 1).astype(jnp.float32)
    forcing = route_obs(obs_dest, obs_cell, obs_wt, misfit, tile_rows * columns)
    sources = []
    for moment in range(2):
        blank = jnp.zeros((layers, tile_rows, columns), jnp.float32)
        sources.append(
            blank.at[layers - 1].set(forcing[moment].reshape(tile_rows, columns) * outer)
        )
    coeff = diffus[:, None, None, None] * conduct[None]
    first = shallow_step(
        adjoint, coeff, sources[1], couple, row_start, total_rows, ghost_row, ghost_col, ghost_wt
    )
    final = shallow_step(
        first, coeff, sources[0], couple, row_start, total_rows, ghost_row, ghost_col, ghost_wt
    )
    return final[None]


def solution(mesh):
    placed = (
        P("panel", None, "rad", "ang", None),
        P("panel", "rad", "ang", None),
        P(),
        P(),
        P(),
        P(),
        P(),
        P("panel", "rad", "ang", None),
        P("panel", "rad", None, "ang"),
        P("panel", "rad", None, "ang"),
        P("panel", "rad", None, "ang"),
    )
    return jax.shard_map(
        body,
        mesh=mesh,
        in_specs=placed,
        out_specs=P("panel", None, "rad", "ang", None),
        check_vma=False,
    )
```

profile of v0, /device:TPU:0, one launch (start us, length us, event | category | flops | bytes accessed | tf_op | source)
XLA Modules:
  0.0 289.1 jit_solution(18301925679141417289)
XLA Ops:
  6.5 1.2 multiply_multiply_fusion.1
  7.8 1.3 collective-permute-start
  9.1 4.9 %collective-permute-start.1 = (f32[7,1,8,1536]{3,0,2,1:T(8,128)S(1)}, f32[7,1,8,1536]{3,0,2,1:T(8,128)S(1)}, u32[]{:S(2)}, u32[]{:S(2)}) collective-permute-start(f32[7,1,8,1536]{3,0,2,1:T(8,128)S(1)} %multiply_multiply_fusion.1), channel_id=1, source_target_pairs={{0,8},{1,9},{2,10},{3,11},{4,12},{5,13},{6,14},{7,15},{16,24},{17,... | collective-permute-start | bytes 1032200 | tf_op jit(solution)/shard_map/ppermute | solution.py:16
  14.0 0.1 fusion.42
  14.1 0.1 copy.71
  14.2 0.1 copy.72
  14.4 2.7 collective-permute-start.4
  17.0 0.7 fusion.36
  17.7 0.6 reduce-window.6
  18.3 0.2 slice_reduce_fusion
  18.5 0.8 fusion.35
  19.3 0.7 compare_select_fusion.2
  20.0 0.9 copy.113
  20.9 0.7 broadcast_multiply_fusion
  21.7 0.7 convert_bitcast_fusion
  22.4 0.1 copy.79
  22.5 1.3 scatter_fusion
  23.8 0.1 copy.80
  23.9 0.7 reshape.458
  24.6 4.9 %all-to-all-start = ((f32[8,1,768]{2,1,0:T(1,128)}), f32[8,1,768]{2,1,0:T(1,128)S(1)}, u32[]{:S(2)}, u32[]{:S(2)}) async-start(f32[8,1,768]{2,1,0:T(1,128)} %reshape.458), calls=%async_computation | async-start | bytes 49152 | tf_op jit(solution)/shard_map/all_to_all | solution.py:50
  29.5 0.2 fusion.41
  29.7 0.7 add_select_fusion
  30.4 0.1 reshape.402
  30.5 0.8 mul.213
  31.3 0.1 copy.73
  31.4 14.4 %all_gather.6 = f32[7,1,2,64]{0,2,1,3:T(2,128)S(1)} all-gather(f32[7,1,2,8]{0,2,1,3:T(2,128)S(1)} %copy.73), channel_id=1, replica_groups=mesh['panel'=2,'rad'=2,'ang'=8] {'ang'}, dimensions={3}, use_global_device_ids=true | all-gather | bytes 4032 | tf_op jit(solution)/shard_map/all_gather | solution.py:57
  45.9 5.4 %scatter_custom_fusion = f32[7,12288]{0,1:T(8,128)} fusion(s32[512]{0:T(512)S(1)} %bitcast.103, f32[]{:T(128)} %constant.121.clone.1, f32[7,1,512]{0,2,1:T(8,128)S(1)} %bitcast.81, f32[512]{0:T(512)S(1)} %mul.213), kind=kCustom, calls=%fused_computation.10 | custom fusion | flops 7168 | bytes 608260 | tf_op jit(solution)/shard_map/scatter-add | solution.py:71
  51.2 4.4 %copy.76 = f32[7,1,8,1536]{3,0,2,1:T(8,128)S(1)} copy(f32[7,1,8,1536]{0,3,2,1:T(8,128)} %bitcast.77) | data formatting | bytes 688128 | tf_op jit(solution)/shard_map/reshape | solution.py:72
  55.7 0.5 broadcast.321
  56.2 0.7 reduce.14
  56.9 0.1 reshape.459
  57.0 0.1 reshape.428
  57.1 0.4 copy.83
  57.5 0.1 convert_element_type.51
  57.6 14.5 %scatter_custom_fusion.2 = f32[2,12288]{0,1:T(8,128)} fusion(s32[2048]{0:T(1024)S(1)} %bitcast.98, f32[2048,2]{1,0:T(8,128)S(1)} %copy.83, f32[]{:T(128)} %constant.121.clone.1), kind=kCustom, calls=%fused_computation.12 | custom fusion | flops 4096 | bytes 98308 | tf_op jit(solution)/shard_map/scatter-add | solution.py:28
  72.1 1.3 collective-permute-start.2
  73.5 3.4 %collective-permute-start.3 = (f32[7,3,1,1536]{3,0,2,1:T(8,128)S(1)}, f32[7,3,1,1536]{3,0,2,1:T(8,128)S(1)}, u32[]{:S(2)}, u32[]{:S(2)}) collective-permute-start(f32[7,3,1,1536]{3,0,2,1:T(8,128)S(1)} %get-tuple-element.58), channel_id=1, source_target_pairs={{0,1},{1,2},{2,3},{3,4},{4,5},{5,6},{6,7},{8,9},{9,10},{10,11},{11... | collective-permute-start | bytes 387080 | tf_op jit(solution)/shard_map/ppermute | solution.py:16
  76.8 147.7 %all-reduce.6.cloned.1.call-done = f32[2,12288]{0,1:T(8,128)} async-done(((f32[2,12288]{0,1:T(8,128)}), f32[2,12288]{0,1:T(8,128)}) %all-reduce.6.cloned.1.call-update) | async-done | bytes 98320 | tf_op jit(solution)/shard_map/psum | solution.py:52
  224.5 9.6 %fusion = (f32[12288]{0:T(1024)S(1)}, f32[12288]{0:T(1024)S(1)}) fusion(f32[2,12288]{0,1:T(8,128)} %all-reduce.6.cloned.1.call-done, f32[]{:T(128)S(6)} %convert_element_type.52), kind=kLoop, calls=%fused_computation.5 | loop fusion | flops 24576 | bytes 196612 | tf_op jit(solution)/shard_map/mul | solution.py:122
  234.2 1.1 fusion.9
  235.2 0.1 slice_add_fusion.1
  235.3 0.6 scatter-add.33
  235.9 0.8 multiply_multiply_fusion
  236.7 1.3 collective-permute-start.5
  238.0 4.6 %collective-permute-start.6 = (f32[7,1,8,1536]{3,0,2,1:T(8,128)S(1)}, f32[7,1,8,1536]{3,0,2,1:T(8,128)S(1)}, u32[]{:S(2)}, u32[]{:S(2)}) collective-permute-start(f32[7,1,8,1536]{3,0,2,1:T(8,128)S(1)} %multiply_multiply_fusion), channel_id=1, source_target_pairs={{0,8},{1,9},{2,10},{3,11},{4,12},{5,13},{6,14},{7,15},{16,24},{17,... | collective-permute-start | bytes 1032200 | tf_op jit(solution)/shard_map/ppermute | solution.py:16
  242.6 0.1 fusion.40
  242.6 0.1 copy.85
  242.8 0.1 copy.86
  242.9 1.5 collective-permute-start.9
  244.4 5.0 %collective-permute-done.5 = f32[7,1,8,1536]{3,0,2,1:T(8,128)S(1)} collective-permute-done((f32[7,1,8,1536]{3,0,2,1:T(8,128)S(1)}, f32[7,1,8,1536]{3,0,2,1:T(8,128)S(1)}, u32[]{:S(2)}, u32[]{:S(2)}) %collective-permute-start.5) | collective-permute-done | bytes 344096 | tf_op jit(solution)/shard_map/ppermute | solution.py:19
  249.4 1.2 collective-permute-done.6
  250.6 0.7 pad_maximum_fusion.14
  251.4 1.3 collective-permute-start.7
  252.6 3.0 %collective-permute-start.8 = (f32[7,3,1,1536]{3,0,2,1:T(8,128)}, f32[7,3,1,1536]{3,0,2,1:T(8,128)S(1)}, u32[]{:S(2)}, u32[]{:S(2)}) collective-permute-start(f32[7,3,1,1536]{3,0,2,1:T(8,128)} %get-tuple-element.56), channel_id=1, source_target_pairs={{0,1},{1,2},{2,3},{3,4},{4,5},{5,6},{6,7},{8,9},{9,10},{10,11},{11... | collective-permute-start | bytes 387080 | tf_op jit(solution)/shard_map/ppermute | solution.py:16
  255.7 0.2 fusion.39
  255.9 0.1 copy.87
  256.0 14.0 %all_gather.7 = f32[7,1,2,64]{0,2,1,3:T(2,128)S(1)} all-gather(f32[7,1,2,8]{0,2,1,3:T(2,128)S(1)} %copy.87), channel_id=1, replica_groups=mesh['panel'=2,'rad'=2,'ang'=8] {'ang'}, dimensions={3}, use_global_device_ids=true | all-gather | bytes 4032 | tf_op jit(solution)/shard_map/all_gather | solution.py:57
  270.0 5.4 %scatter_custom_fusion.3 = f32[7,12288]{0,1:T(8,128)} fusion(s32[512]{0:T(512)S(1)} %bitcast.104, f32[]{:T(128)} %constant.121.clone.1, f32[7,1,512]{0,2,1:T(8,128)S(1)} %bitcast.80, f32[512]{0:T(512)S(1)} %mul.213), kind=kCustom, calls=%fused_computation.8 | custom fusion | flops 7168 | bytes 608260 | tf_op jit(solution)/shard_map/scatter-add | solution.py:71
  275.4 4.4 %copy.90 = f32[7,1,8,1536]{3,0,2,1:T(8,128)S(1)} copy(f32[7,1,8,1536]{0,3,2,1:T(8,128)} %bitcast.76) | data formatting | bytes 688128 | tf_op jit(solution)/shard_map/reshape | solution.py:72
  279.8 0.7 fusion.8
  280.6 0.1 slice_add_fusion
  280.6 0.6 scatter-add.35
  281.2 0.1 multiply_bitcast_fusion
  281.3 0.9 copy.93
  (35 shorter events, 0.3 us)
Async XLA Ops:
  6.5 227.6 %copy-start = (f32[7,7]{1,0:T(8,128)S(1)}, f32[7,7]{1,0:T(8,128)}, u32[]{:S(2)}) copy-start(f32[7,7]{1,0:T(8,128)} %param.22) | copy-start | bytes 592
  7.8 64.3 %collective-permute-start = (f32[7,1,8,1536]{3,0,2,1:T(8,128)S(1)}, f32[7,1,8,1536]{3,0,2,1:T(8,128)S(1)}, u32[]{:S(2)}, u32[]{:S(2)}) collective-permute-start(f32[7,1,8,1536]{3,0,2,1:T(8,128)S(1)} %multiply_multiply_fusion.1), channel_id=1, source_target_pairs={{8,0},{9,1},{10,2},{11,3},{12,4},{13,5},{14,6},{15,7},{24,16},{25,... | collective-permute-start | bytes 1032200 | tf_op jit(solution)/shard_map/ppermute | solution.py:19
  9.1 63.0 %collective-permute-start.1 = (f32[7,1,8,1536]{3,0,2,1:T(8,128)S(1)}, f32[7,1,8,1536]{3,0,2,1:T(8,128)S(1)}, u32[]{:S(2)}, u32[]{:S(2)}) collective-permute-start(f32[7,1,8,1536]{3,0,2,1:T(8,128)S(1)} %multiply_multiply_fusion.1), channel_id=1, source_target_pairs={{0,8},{1,9},{2,10},{3,11},{4,12},{5,13},{6,14},{7,15},{16,24},{17,... | collective-permute-start | bytes 1032200 | tf_op jit(solution)/shard_map/ppermute | solution.py:16
  14.4 16.9 %collective-permute-start.4 = (f32[7,1,2,8]{3,2,0,1:T(2,128)S(1)}, f32[7,1,2,8]{3,2,0,1:T(2,128)S(1)}, u32[]{:S(2)}, u32[]{:S(2)}) collective-permute-start(f32[7,1,2,8]{3,2,0,1:T(2,128)S(1)} %pad_maximum_fusion.18), channel_id=1, source_target_pairs={{0,16},{16,0},{1,17},{17,1},{2,18},{18,2},{3,19},{19,3},{4,20},{20... | collective-permute-start | bytes 1352 | tf_op jit(solution)/shard_map/ppermute | solution.py:8
  24.6 31.1 %all-to-all-start = ((f32[8,1,768]{2,1,0:T(1,128)}), f32[8,1,768]{2,1,0:T(1,128)S(1)}, u32[]{:S(2)}, u32[]{:S(2)}) async-start(f32[8,1,768]{2,1,0:T(1,128)} %reshape.458), calls=%async_computation | async-start | bytes 49152 | tf_op jit(solution)/shard_map/all_to_all | solution.py:50
  29.5 195.0 %all-reduce.6.cloned.1.call-start = ((), (), s32[]{:S(2)}) async-start(), calls=%async_computation.1 | async-start | bytes 12582912 | tf_op jit(solution)/shard_map/psum | solution.py:52
  72.1 162.0 %collective-permute-start.2 = (f32[7,3,1,1536]{3,0,2,1:T(8,128)S(1)}, f32[7,3,1,1536]{3,0,2,1:T(8,128)S(1)}, u32[]{:S(2)}, u32[]{:S(2)}) collective-permute-start(f32[7,3,1,1536]{3,0,2,1:T(8,128)S(1)} %get-tuple-element.57), channel_id=1, source_target_pairs={{1,0},{2,1},{3,2},{4,3},{5,4},{6,5},{7,6},{9,8},{10,9},{11,10},{12... | collective-permute-start | bytes 387080 | tf_op jit(solution)/shard_map/ppermute | solution.py:19
  73.4 160.7 %copy-start.1 = (f32[1,7,1,8,1536]{4,3,2,1,0:T(8,128)S(1)}, f32[1,7,1,8,1536]{4,3,2,1,0:T(8,128)}, u32[]{:S(2)}) copy-start(f32[1,7,1,8,1536]{4,3,2,1,0:T(8,128)} %param.19) | copy-start | bytes 1032196
  73.5 162.4 %copy-start.2 = (f32[1,1,8,1536]{3,2,1,0:T(8,128)S(1)}, f32[1,1,8,1536]{3,2,1,0:T(8,128)}, u32[]{:S(2)}) copy-start(f32[1,1,8,1536]{3,2,1,0:T(8,128)} %param.20) | copy-start | bytes 147460
  73.5 160.7 %collective-permute-start.3 = (f32[7,3,1,1536]{3,0,2,1:T(8,128)S(1)}, f32[7,3,1,1536]{3,0,2,1:T(8,128)S(1)}, u32[]{:S(2)}, u32[]{:S(2)}) collective-permute-start(f32[7,3,1,1536]{3,0,2,1:T(8,128)S(1)} %get-tuple-element.58), channel_id=1, source_target_pairs={{0,1},{1,2},{2,3},{3,4},{4,5},{5,6},{6,7},{8,9},{9,10},{10,11},{11... | collective-permute-start | bytes 387080 | tf_op jit(solution)/shard_map/ppermute | solution.py:16
  236.7 12.7 %collective-permute-start.5 = (f32[7,1,8,1536]{3,0,2,1:T(8,128)S(1)}, f32[7,1,8,1536]{3,0,2,1:T(8,128)S(1)}, u32[]{:S(2)}, u32[]{:S(2)}) collective-permute-start(f32[7,1,8,1536]{3,0,2,1:T(8,128)S(1)} %multiply_multiply_fusion), channel_id=1, source_target_pairs={{8,0},{9,1},{10,2},{11,3},{12,4},{13,5},{14,6},{15,7},{24,16},{25,... | collective-permute-start | bytes 1032200 | tf_op jit(solution)/shard_map/ppermute | solution.py:19
  238.0 12.7 %collective-permute-start.6 = (f32[7,1,8,1536]{3,0,2,1:T(8,128)S(1)}, f32[7,1,8,1536]{3,0,2,1:T(8,128)S(1)}, u32[]{:S(2)}, u32[]{:S(2)}) collective-permute-start(f32[7,1,8,1536]{3,0,2,1:T(8,128)S(1)} %multiply_multiply_fusion), channel_id=1, source_target_pairs={{0,8},{1,9},{2,10},{3,11},{4,12},{5,13},{6,14},{7,15},{16,24},{17,... | collective-permute-start | bytes 1032200 | tf_op jit(solution)/shard_map/ppermute | solution.py:16
  242.9 12.9 %collective-permute-start.9 = (f32[7,1,2,8]{3,2,0,1:T(2,128)S(1)}, f32[7,1,2,8]{3,2,0,1:T(2,128)S(1)}, u32[]{:S(2)}, u32[]{:S(2)}) collective-permute-start(f32[7,1,2,8]{3,2,0,1:T(2,128)S(1)} %pad_maximum_fusion.19), channel_id=1, source_target_pairs={{0,16},{16,0},{1,17},{17,1},{2,18},{18,2},{3,19},{19,3},{4,20},{20... | collective-permute-start | bytes 1352 | tf_op jit(solution)/shard_map/ppermute | solution.py:8
  251.4 28.4 %collective-permute-start.7 = (f32[7,3,1,1536]{3,0,2,1:T(8,128)}, f32[7,3,1,1536]{3,0,2,1:T(8,128)S(1)}, u32[]{:S(2)}, u32[]{:S(2)}) collective-permute-start(f32[7,3,1,1536]{3,0,2,1:T(8,128)} %get-tuple-element.55), channel_id=1, source_target_pairs={{1,0},{2,1},{3,2},{4,3},{5,4},{6,5},{7,6},{9,8},{10,9},{11,10},{12... | collective-permute-start | bytes 387080 | tf_op jit(solution)/shard_map/ppermute | solution.py:19
  252.6 27.2 %collective-permute-start.8 = (f32[7,3,1,1536]{3,0,2,1:T(8,128)}, f32[7,3,1,1536]{3,0,2,1:T(8,128)S(1)}, u32[]{:S(2)}, u32[]{:S(2)}) collective-permute-start(f32[7,3,1,1536]{3,0,2,1:T(8,128)} %get-tuple-element.56), channel_id=1, source_target_pairs={{0,1},{1,2},{2,3},{3,4},{4,5},{5,6},{6,7},{8,9},{9,10},{10,11},{11... | collective-permute-start | bytes 387080 | tf_op jit(solution)/shard_map/ppermute | solution.py:16
Sparse Core Ops, SparseCore 0:
  72.2 152.2 all-reduce.5
where the time goes:
time: 290 us; the launch traced here: 289 us
  waiting for transfers between devices  154 us (53%)
  other arithmetic  43.5 us (15%)
  starting transfers between devices  30.2 us (10%)
  blocking collectives  28.4 us (10%)
  local copies, waits for them, and re-layouts  17.6 us (6%)
  between operations  13.7 us (5%)
    psum x1, waiting for transfers between devices, route_obs(): return lax.psum(dense, 'rad')  148 us
    all_gather x2, blocking collectives, other_edges(): return lax.all_gather(across, 'ang', axis=3, tiled=True)  28.4 us
    ppermute x4, starting transfers between devices, extended(): lax.ppermute(lax.slice_in_dim(block, block.shape[dim] - width, None, axis...  15.9 us
    scatter-add x1, other arithmetic, deposit(): return dense.at[:, cells].add(values, mode='drop')  14.5 us
    scatter-add x2, other arithmetic, ghost_terms(): target.at[:, :, flat_index]  10.8 us
    mul x1, other arithmetic, body(): forcing[moment].reshape(tile_rows, columns) * outer  9.58 us
    reshape x2, local copies, waits for them, and re-layouts, ghost_terms(): return target.reshape(fields, layers, central_rows, columns)  8.86 us
  transfers between devices with their start and end apart: 12, of which 3 were waited for; matrix products, arithmetic and copies ran while one was open for 20% of the time, Pallas kernels for 0%

commit v1 on v0

v1 whole, which is shorter than its diff:
```python
import functools

import jax
import jax.numpy as jnp
from jax import lax
from jax.experimental import pallas as pl
from jax.experimental.pallas import tpu as pltpu
from jax.sharding import PartitionSpec as P

LANES = 128
SUBL = 8
POINTS = 4
TIMES = 2
LOW = 256
F32 = jnp.float32
BF16 = jnp.bfloat16
NT_DIMS = (((1,), (1,)), ((), ()))


def parts_of(x, count):
    parts = []
    for _ in range(count):
        part = x.astype(BF16)
        parts.append(part)
        x = x - part.astype(F32)
    return parts


def split_dot(x, onehot, count, dims):
    total = None
    for part in parts_of(x, count):
        term = lax.dot_general(part, onehot, dims, preferred_element_type=F32)
        total = term if total is None else total + term
    return total


def iota(shape, dim):
    return lax.broadcasted_iota(jnp.int32, shape, dim)


class Sizes:
    def __init__(self, adj, obs_cell, ghost_row):
        self.fields, self.rows, self.cols = adj.shape[1], adj.shape[3], adj.shape[4]
        self.panels = lax.axis_size("panel")
        self.rads = lax.axis_size("rad")
        self.tiles = lax.axis_size("ang")
        self.devices = self.panels * self.rads * self.tiles
        self.total_rows = self.tiles * self.rows
        self.edge = 2 * self.total_rows
        self.count = obs_cell.shape[-1]
        self.slots = 2 * self.count // self.tiles
        self.spr = min(POINTS, LANES // self.slots)
        self.npr = POINTS // self.spr
        self.feat_rows = 2 * self.npr + 1
        self.edge_rows = self.edge // LANES
        self.strip = self.feat_rows + self.edge_rows
        self.block = -(-(self.strip + 2) // SUBL) * SUBL
        self.stencil = ghost_row.shape[1]
        self.hi = self.rows * self.cols // LOW
        self.pair = self.rads == 2


def rolled(x, shift, axis):
    size = x.shape[axis]
    shift = shift % size
    return x if shift == 0 else pltpu.roll(x, shift, axis)


def pack_kernel(z, adj, cond, diffus, dest, cell, wt, misfit, pay, up, down):
    for f in range(z.fields):
        s = adj[0, f, 0] * (cond[0, 0] * diffus[f])
        up[f : f + 1, :] = s[z.rows - 1 :, :]
        down[f : f + 1, :] = s[:1, :]
    up[z.fields :, :] = jnp.zeros((SUBL - z.fields, z.cols), F32)
    down[z.fields :, :] = jnp.zeros((SUBL - z.fields, z.cols), F32)

    owner = dest[...]
    height = max(16, z.tiles)
    mine = (iota((height, z.count), 0) == owner).astype(F32)
    earlier = (iota((z.count, z.count), 0) < iota((z.count, z.count), 1)).astype(F32)
    ranks = jnp.dot(mine.astype(BF16), earlier.astype(BF16), preferred_element_type=F32)
    rank = jnp.sum(ranks * mine, axis=0, keepdims=True)
    place = owner * LANES + rank.astype(jnp.int32)
    spread = (iota((z.tiles * LANES, z.count), 0) == place).astype(F32).astype(BF16)

    where = cell[0, 0]
    row = ((where.astype(F32) + 0.5) * (1.0 / z.cols)).astype(jnp.int32)
    col = where - row * z.cols
    code = ((col // LOW) * z.rows + row) * LOW + col % LOW
    code = code.astype(F32)
    weight = wt[0, 0]
    mis = misfit[0, 0]
    feats = []
    for g in range(z.spr):
        picked = [weight[h * z.spr + g : h * z.spr + g + 1] for h in range(z.npr)]
        picked += [code[h * z.spr + g : h * z.spr + g + 1] for h in range(z.npr)]
        picked.append(mis[g : g + 1] if g < TIMES else jnp.zeros((1, z.count), F32))
        feats += picked
    used = len(feats)
    padded = -(-used // 16) * 16
    if padded > used:
        feats.append(jnp.zeros((padded - used, z.count), F32))
    boxed = split_dot(jnp.concatenate(feats, axis=0), spread, 3, NT_DIMS)
    slots = boxed[: z.feat_rows]
    for g in range(1, z.spr):
        slots = slots + rolled(boxed[g * z.feat_rows : (g + 1) * z.feat_rows], g * z.slots, 1)

    full_row = owner * z.rows + row
    edge_at = jnp.where(col == 0, full_row, jnp.where(col == z.cols - 1, z.total_rows + full_row, -1))
    total = None
    for s in range(POINTS):
        value = mis[1:2] * weight[s : s + 1]
        value = jnp.concatenate([value, jnp.zeros((15, z.count), F32)], axis=0)
        hits = (iota((z.edge, z.count), 0) == edge_at[s : s + 1]).astype(F32).astype(BF16)
        term = split_dot(value, hits, 3, NT_DIMS)
        total = term if total is None else total + term
    edge_force = total[:1]

    lane = iota((z.rows, LANES), 1)
    sub = iota((z.rows, LANES), 0)
    strips = []
    for side in range(2):
        acc = jnp.zeros((z.rows, LANES), F32)
        for f in range(z.fields + 1):
            for inner in range(2):
                at = inner if side == 0 else z.cols - 1 - inner
                line = adj[0, f, 0, :, at : at + 1] if f < z.fields else cond[0, 0, :, at : at + 1]
                acc = jnp.where(lane == (f * 2 + inner) * z.rows + sub, line, acc)
        strips.append(jnp.sum(acc, axis=0, keepdims=True))

    common = [edge_force[:, k * LANES : (k + 1) * LANES] for k in range(z.edge_rows)] + strips
    spare = z.block - z.strip - 2
    if spare:
        common.append(jnp.zeros((spare, LANES), F32))
    common = jnp.concatenate(common, axis=0)
    for t in range(z.tiles):
        part = jnp.concatenate([slots[:, t * LANES : (t + 1) * LANES], common], axis=0)
        for group in range(z.panels * z.rads):
            pay[group * z.tiles + t] = part


def by_field(z, scalar, width):
    sub = iota((SUBL, width), 0)
    out = jnp.zeros((SUBL, width), F32)
    for f in range(z.fields):
        out = jnp.where(sub == f, scalar(f), out)
    return out


def unpack_strips(z, recv, sets):
    height = 2 * z.tiles
    stacked = []
    for panel, rad in sets:
        base = (panel * z.rads + rad) * z.tiles * z.block + z.strip
        for side in range(2):
            stacked.append(recv[pl.ds(base + side, z.tiles, stride=z.block), :])
    stacked = jnp.concatenate(stacked, axis=0)
    width = 2 * SUBL * z.edge
    lane = iota((LANES, width), 1)
    slot = lane // z.edge
    inner, plane = slot // SUBL, slot % SUBL
    picks = (iota((LANES, width), 0) == (plane * 2 + inner) * z.rows + lane % z.rows).astype(F32)
    moved = split_dot(stacked, picks.astype(BF16), 3, (((1,), (0,)), ((), ())))
    lane = iota((height, z.edge), 1)
    keep = lane // z.rows == iota((height, z.edge), 0)
    out = []
    for number in range(len(sets)):
        both = []
        for inner in range(2):
            rows = []
            for f in range(z.fields + 1):
                at = (inner * SUBL + f) * z.edge
                tile = moved[number * height : (number + 1) * height, at : at + z.edge]
                rows.append(jnp.sum(jnp.where(keep, tile, 0.0), axis=0, keepdims=True))
            both.append(jnp.concatenate(rows, axis=0))
        out.append(both)
    return out


def edge_scaled(z, values, dif):
    return values * values[z.fields : z.fields + 1] * dif


def coupled(z, couple, state, c):
    total = None
    for e in range(z.fields):
        term = state(e) * couple[e, c]
        total = term if total is None else total + term
    return total


def line_of(ref, s, q):
    return jnp.concatenate([ref[side, q : q + 1, :] for side in range(2)], axis=1) if s is None else ref[s, q : q + 1, :]


def deposit(z, recv, panel, spread_a, spread_b):
    sources = z.rads * z.tiles
    base = panel * sources * z.block
    feat = [recv[pl.ds(base + k, sources, stride=z.block), :] for k in range(z.feat_rows)]
    lane = iota((sources, LANES), 1)
    scaled = []
    for t in range(TIMES):
        mis = jnp.where(lane // z.slots == t, feat[2 * z.npr], 0.0)
        full = None
        for g in range(z.spr):
            term = rolled(mis, (g - t) * z.slots, 1)
            full = term if full is None else full + term
        scaled.append(full)
    sub_hi = iota((z.hi, LANES), 0)
    sub_lo = iota((LOW, LANES), 0)
    for h in range(z.npr):
        code = feat[z.npr + h].astype(jnp.int32)
        high, low = code // LOW, code % LOW
        parts = []
        for t in range(TIMES):
            parts += [p.astype(F32) for p in parts_of(scaled[t] * feat[h], 2)]
        for n in range(sources):
            at = (n * z.npr + h) * LANES
            hit = sub_hi == high[n : n + 1]
            for k, part in enumerate(parts):
                spread_a[k * z.hi : (k + 1) * z.hi, at : at + LANES] = jnp.where(hit, part[n : n + 1], 0.0).astype(BF16)
            spread_b[:, at : at + LANES] = (sub_lo == low[n : n + 1]).astype(F32).astype(BF16)
    grid = lax.dot_general(spread_a[...], spread_b[...], NT_DIMS, preferred_element_type=F32)
    out = []
    for t in range(TIMES):
        both = grid[2 * t * z.hi : (2 * t + 1) * z.hi] + grid[(2 * t + 1) * z.hi : (2 * t + 2) * z.hi]
        out.append(jnp.concatenate([both[k * z.rows : (k + 1) * z.rows] for k in range(z.cols // LOW)], axis=1))
    return out


def sideways(s):
    cols = s.shape[1]
    lane = iota(s.shape, 1)
    west = jnp.where(lane == 0, 0.0, pltpu.roll(s, 1, 1))
    east = jnp.where(lane == cols - 1, 0.0, pltpu.roll(s, cols - 1, 1))
    return west + east


def upright(s, above, below):
    rows = s.shape[0]
    sub = iota(s.shape, 0)
    north = jnp.where(sub == 0, above, pltpu.roll(s, 1, 0))
    south = jnp.where(sub == rows - 1, below, pltpu.roll(s, rows - 1, 0))
    return north + south


def first_kernel(z, adj, cond, *refs):
    if z.pair:
        adj2, cond2, *refs = refs
    else:
        beside, *refs = refs
    above, below, recv, diffus, couple, grow, gcol, gwt, *refs = refs
    first, base, up, down, spread_a, spread_b = refs
    panel, rad, tile = lax.axis_index("panel"), lax.axis_index("rad"), lax.axis_index("ang")
    other = 1 - panel
    outer = jnp.where(rad == z.rads - 1, 1.0, 0.0)

    sets = [(other, rad), (panel, rad)]
    if z.pair:
        sets.append((other, 1 - rad))
        near = [1.0]
    else:
        sets += [(other, jnp.maximum(rad - 1, 0)), (other, jnp.minimum(rad + 1, z.rads - 1))]
        near = [jnp.where(rad > 0, 1.0, 0.0), jnp.where(rad < z.rads - 1, 1.0, 0.0)]
    strips = unpack_strips(z, recv, sets)
    dif = by_field(z, lambda f: diffus[f], z.edge)
    rim, inside = strips[0]
    rim_s = edge_scaled(z, rim, dif)
    home_s = edge_scaled(z, strips[1][0], dif)
    layers_s = [edge_scaled(z, strips[2 + k][0], dif) for k in range(len(near))]
    lap = edge_scaled(z, inside, dif) - 6.0 * rim_s
    for k, one in enumerate(near):
        lap = lap + layers_s[k] * one
    spot = iota((SUBL, z.edge), 1) % z.total_rows
    lap = lap + jnp.where(spot == 0, 0.0, pltpu.roll(rim_s, 1, 1))
    lap = lap + jnp.where(spot == z.total_rows - 1, 0.0, pltpu.roll(rim_s, z.edge - 1, 1))
    rows = [coupled(z, couple, lambda e: rim[e : e + 1], c) for c in range(z.fields)]
    mixed = jnp.concatenate(rows + [jnp.zeros((SUBL - z.fields, z.edge), F32)], axis=0)

    g_row = [line_of(grow, None, q) for q in range(z.stencil)]
    g_col = [line_of(gcol, None, q) for q in range(z.stencil)]
    g_wt = [line_of(gwt, None, q) for q in range(z.stencil)]
    rim_ghost = None
    for q in range(z.stencil):
        target = jnp.where(
            g_col[q] == 0, g_row[q], jnp.where(g_col[q] == z.cols - 1, z.total_rows + g_row[q], -1)
        )
        hits = (iota((z.edge, z.edge), 0) == target).astype(F32).astype(BF16)
        values = jnp.concatenate([home_s * g_wt[q], jnp.zeros((SUBL, z.edge), F32)], axis=0)
        term = split_dot(values, hits, 3, NT_DIMS)
        rim_ghost = term if rim_ghost is None else rim_ghost + term
    sources = z.rads * z.tiles
    force = []
    for k in range(z.edge_rows):
        at = other * sources * z.block + z.feat_rows + k
        force.append(jnp.sum(recv[pl.ds(at, sources, stride=z.block), :], axis=0, keepdims=True))
    force = jnp.concatenate(force, axis=1) * outer
    rim_first = rim + lap + mixed + rim_ghost[:SUBL]
    rim_first = rim_first + jnp.where(iota((SUBL, z.edge), 0) == 3, force, 0.0)
    rim_second = rim_first * rim[z.fields : z.fields + 1] * dif

    row0 = tile * z.rows
    aimed = [jnp.where(iota((z.rows, z.edge), 0) == g_row[q] - row0, g_wt[q], 0.0) for q in range(z.stencil)]
    loads = [rim_s, rim_second] + ([layers_s[0]] if z.pair else [])
    stacked = []
    for load in loads:
        for f in range(z.fields):
            stacked.append(jnp.concatenate([load[f : f + 1] * aimed[q] for q in range(z.stencil)], axis=1))
    height = len(stacked) * z.rows
    if height % 16:
        stacked.append(jnp.zeros((16 - height % 16, z.stencil * z.edge), F32))
    stacked = jnp.concatenate(stacked, axis=0)
    spots = jnp.concatenate(g_col, axis=1)
    columns = (iota((z.cols, z.stencil * z.edge), 0) == spots).astype(F32).astype(BF16)
    ghost = split_dot(stacked, columns, 2, NT_DIMS)

    def ghost_of(step, f):
        at = (step * z.fields + f) * z.rows
        return ghost[at : at + z.rows]

    force0, force1 = deposit(z, recv, panel, spread_a, spread_b)

    own_c = cond[0, 0]
    far_c = cond2[0, 0] if z.pair else None
    for f in range(z.fields):
        s = adj[0, f, 0] * (own_c * diffus[f])
        new = adj[0, f, 0] - 6.0 * s + sideways(s) + upright(s, above[f : f + 1], below[f : f + 1])
        new = new + coupled(z, couple, lambda e: adj[0, e, 0], f) + ghost_of(0, f)
        second = ghost_of(1, f)
        if z.pair:
            far = adj2[0, f, 0] * (far_c * diffus[f])
            new = new + far
            part = adj2[0, f, 0] - 6.0 * far + sideways(far) + upright(far, 0.0, 0.0) + s
            part = part + coupled(z, couple, lambda e: adj2[0, e, 0], f) + ghost_of(2, f)
            if f == 3:
                part = part + force1 * (1.0 - outer)
            second = second + part * (far_c * diffus[f])
            up[SUBL + f : SUBL + f + 1, :] = far[z.rows - 1 :]
            down[SUBL + f : SUBL + f + 1, :] = far[:1]
        else:
            new = new + beside[f]
        if f == 3:
            new = new + force1 * outer
            second = second + force0 * outer
        first[f] = new
        base[f] = second
        s = new * (own_c * diffus[f])
        up[f : f + 1, :] = s[z.rows - 1 :]
        down[f : f + 1, :] = s[:1]
    for half in range(2 if z.pair else 1):
        for ref in (up, down):
            ref[half * SUBL + z.fields : (half + 1) * SUBL, :] = jnp.zeros((SUBL - z.fields, z.cols), F32)


def second_kernel(z, first, base, cond, *refs):
    if z.pair:
        cond2, *refs = refs
    else:
        beside, *refs = refs
    above, below, diffus, couple, out = refs
    own_c = cond[0, 0]
    for f in range(z.fields):
        s = first[f] * (own_c * diffus[f])
        new = first[f] - 6.0 * s + sideways(s) + base[f]
        high, low = above[f : f + 1], below[f : f + 1]
        if z.pair:
            far_c = cond2[0, 0]
            high = high + above[SUBL + f : SUBL + f + 1] * (far_c[:1] * diffus[f])
            low = low + below[SUBL + f : SUBL + f + 1] * (far_c[z.rows - 1 :] * diffus[f])
        else:
            new = new + beside[f]
        new = new + upright(s, high, low)
        out[0, f, 0] = new + coupled(z, couple, lambda e: first[e], f)


def shifted(x, axis, step):
    count = lax.axis_size(axis)
    pairs = [(i, i + step) for i in range(count) if 0 <= i + step < count]
    return lax.ppermute(x, axis, pairs)


def both_sides(x, axis):
    return shifted(x, axis, 1) + shifted(x, axis, -1)


def call(kernel, shapes, scratch, args, scalars):
    specs = [
        pl.BlockSpec(memory_space=pltpu.SMEM if n in scalars else pltpu.VMEM) for n in range(len(args))
    ]
    return pl.pallas_call(
        kernel,
        out_shape=[jax.ShapeDtypeStruct(shape, F32) for shape in shapes],
        in_specs=specs,
        out_specs=[pl.BlockSpec(memory_space=pltpu.VMEM)] * len(shapes),
        scratch_shapes=scratch,
        compiler_params=pltpu.CompilerParams(vmem_limit_bytes=48 << 20),
    )(*args)


def body(adj, cond, diffus, couple, ghost_row, ghost_col, ghost_wt, obs_dest, obs_cell, obs_wt, misfit):
    z = Sizes(adj, obs_cell, ghost_row)
    state = (z.fields, z.rows, z.cols)
    if z.pair:
        swap = [(0, 1), (1, 0)]
        adj2 = lax.ppermute(adj, "rad", swap)
        cond2 = lax.ppermute(cond, "rad", swap)
    else:
        scaled = diffus[:, None, None] * cond[0, 0][None] * adj[0, :, 0]
        beside = both_sides(scaled, "rad")
    pay, up, down = call(
        functools.partial(pack_kernel, z),
        [(z.devices, z.block, LANES), (SUBL, z.cols), (SUBL, z.cols)],
        [],
        [adj, cond, diffus, obs_dest.reshape(1, z.count), obs_cell, obs_wt, misfit],
        (2,),
    )
    recv = lax.all_to_all(pay, ("panel", "rad", "ang"), split_axis=0, concat_axis=0, tiled=True)
    above, below = shifted(up, "ang", 1), shifted(down, "ang", -1)
    points = z.rads * z.tiles * z.npr * LANES
    lines = (SUBL * (2 if z.pair else 1), z.cols)
    args = [adj, cond] + ([adj2, cond2] if z.pair else [beside])
    args += [above, below, recv.reshape(z.devices * z.block, LANES), diffus, couple]
    scalars = (len(args) - 2, len(args) - 1)
    first, base, up, down = call(
        functools.partial(first_kernel, z),
        [state, state, lines, lines],
        [pltpu.VMEM((2 * TIMES * z.hi, points), BF16), pltpu.VMEM((LOW, points), BF16)],
        args + [ghost_row, ghost_col, ghost_wt],
        scalars,
    )
    above, below = shifted(up, "ang", 1), shifted(down, "ang", -1)
    if z.pair:
        args = [first, base, cond, cond2]
    else:
        scaled = diffus[:, None, None] * cond[0, 0][None] * first
        args = [first, base, cond, both_sides(scaled, "rad")]
    args += [above, below, diffus, couple]
    (out,) = call(functools.partial(second_kernel, z), [adj.shape], [], args, (6, 7))
    return out


def solution(mesh):
    placed = (
        P("panel", None, "rad", "ang", None),
        P("panel", "rad", "ang", None),
        P(),
        P(),
        P(),
        P(),
        P(),
        P("panel", "rad", "ang", None),
        P("panel", "rad", None, "ang"),
        P("panel", "rad", None, "ang"),
        P("panel", "rad", None, "ang"),
    )
    return jax.shard_map(
        body,
        mesh=mesh,
        in_specs=placed,
        out_specs=P("panel", None, "rad", "ang", None),
        check_vma=False,
    )
```

time: 290 us -> 38.5 us (0.13)
  the two profiles are of different devices: /device:TPU:0 before, /device:TPU:1 now
where the time goes in v1:
time: 38.5 us; the launch traced here: 38.1 us
  starting transfers between devices  19.1 us (50%)
  Pallas kernels  7.98 us (21%)
  waiting for transfers between devices  6.98 us (18%)
  local copies, waits for them, and re-layouts  3.89 us (10%)
    ppermute x4, starting transfers between devices, shifted(): return lax.ppermute(x, axis, pairs)  9.86 us
    pallas_call x3, Pallas kernels, call(): pl.pallas_call(kernel, out_shape=[jax.ShapeDtypeStruct(shape, F32) for sh...  7.98 us
    ppermute x4, waiting for transfers between devices, shifted(): return lax.ppermute(x, axis, pairs)  6.97 us
    all_to_all x1, starting transfers between devices, body(): lax.all_to_all(pay, ('panel', 'rad', 'ang'), split_axis=0, concat_axis=0,...  5.69 us
    unnamed x26, local copies, waits for them, and re-layouts  3.89 us
    ppermute x1, starting transfers between devices, body(): adj2 = lax.ppermute(adj, 'rad', swap)  2.07 us
    ppermute x1, starting transfers between devices, body(): cond2 = lax.ppermute(cond, 'rad', swap)  1.45 us
  transfers between devices with their start and end apart: 7, of which 2 were waited for; matrix products, arithmetic and copies ran while one was open for 0% of the time, Pallas kernels for 6%

profile of v1, /device:TPU:1, one launch (start us, length us, event | category | flops | bytes accessed | tf_op | source)
XLA Modules:
  0.0 38.1 jit_solution(11321362984446404911)
XLA Ops:
  0.0 0.0 copy-start.5
  0.0 0.0 copy-start.12
  0.0 2.1 %collective-permute-start = (f32[1,7,1,8,1536]{4,3,2,1,0:T(8,128)}, f32[1,7,1,8,1536]{4,3,2,1,0:T(8,128)S(1)}, u32[]{:S(2)}, u32[]{:S(2)}) collective-permute-start(f32[1,7,1,8,1536]{4,3,2,1,0:T(8,128)} %adj.3), channel_id=1, source_target_pairs={{0,8},{8,0},{1,9},{9,1},{2,10},{10,2},{3,11},{11,3},{4,12},{12,4},... | collective-permute-start | bytes 1032200 | tf_op jit(solution)/shard_map/ppermute | solution.py:405
  2.1 0.0 copy-done.5
  2.1 0.0 copy-done.12
  2.1 0.0 copy-start
  2.1 1.0 %copy-done = f32[1,7,1,8,1536]{4,3,2,1,0:T(8,128)S(1)} copy-done((f32[1,7,1,8,1536]{4,3,2,1,0:T(8,128)S(1)}, f32[1,7,1,8,1536]{4,3,2,1,0:T(8,128)}, u32[]{:S(2)}) %copy-start) | copy-done | bytes 344088
  3.1 0.0 copy-start.2
  3.1 0.8 %copy-done.2 = f32[1,1,8,1536]{3,2,1,0:T(8,128)S(1)} copy-done((f32[1,1,8,1536]{3,2,1,0:T(8,128)S(1)}, f32[1,1,8,1536]{3,2,1,0:T(8,128)}, u32[]{:S(2)}) %copy-start.2) | copy-done | bytes 49176
  3.9 0.0 copy-start.6
  3.9 0.7 %copy-done.6 = s32[1,1,4,256]{3,2,1,0:T(4,128)S(1)} copy-done((s32[1,1,4,256]{3,2,1,0:T(4,128)S(1)}, s32[1,1,4,256]{3,2,1,0:T(4,128)}, u32[]{:S(2)}) %copy-start.6) | copy-done | bytes 4120
  4.6 0.0 copy-start.7
  4.6 0.7 %copy-done.7 = f32[1,1,4,256]{3,2,1,0:T(4,128)S(1)} copy-done((f32[1,1,4,256]{3,2,1,0:T(4,128)S(1)}, f32[1,1,4,256]{3,2,1,0:T(4,128)}, u32[]{:S(2)}) %copy-start.7) | copy-done | bytes 4120
  5.3 0.0 copy-start.11
  5.3 0.7 %copy-done.11 = f32[1,1,2,256]{3,2,1,0:T(2,128)S(1)} copy-done((f32[1,1,2,256]{3,2,1,0:T(2,128)S(1)}, f32[1,1,2,256]{3,2,1,0:T(2,128)}, u32[]{:S(2)}) %copy-start.11) | copy-done | bytes 2072
  5.9 0.0 copy-start.1
  5.9 2.2 %shard_map.109 = (f32[32,8,128]{2,1,0:T(8,128)}, f32[8,1536]{1,0:T(8,128)S(1)}, f32[8,1536]{1,0:T(8,128)S(1)}) custom-call(f32[1,7,1,8,1536]{4,3,2,1,0:T(8,128)S(1)} %copy-done, f32[1,1,8,1536]{3,2,1,0:T(8,128)S(1)} %copy-done.2, f32[7]{0:T(128)S(1)} %copy-done.5, s32[1,256]{1,0:T(1,128)S(1)} %bitcast.3, s32[1,1,4,256]{3,2,1,0:T(4,128)S(1)} %copy-done.6, ...), custom_call_target="tpu_custom_call" | custom-call | tf_op jit(solution)/shard_map/pallas_call | solution.py:390
  8.2 0.0 copy-start.3
  8.2 0.0 copy-start.8
  8.2 0.0 copy-start.9
  8.2 0.0 copy-start.10
  8.2 5.7 %all-to-all-start = ((f32[32,8,128]{2,1,0:T(8,128)}), f32[32,8,128]{2,1,0:T(8,128)S(1)}, u32[]{:S(2)}, u32[]{:S(2)}) async-start(f32[32,8,128]{2,1,0:T(8,128)} %get-tuple-element.14), calls=%async_computation | async-start | bytes 262144 | tf_op jit(solution)/shard_map/all_to_all | solution.py:417
  13.9 0.0 copy-done.3
  13.9 0.0 copy-start.4
  13.9 1.5 %collective-permute-start.1 = (f32[1,1,8,1536]{3,2,1,0:T(8,128)S(1)}, f32[1,1,8,1536]{3,2,1,0:T(8,128)S(1)}, u32[]{:S(2)}, u32[]{:S(2)}) collective-permute-start(f32[1,1,8,1536]{3,2,1,0:T(8,128)S(1)} %copy-done.3), channel_id=1, source_target_pairs={{0,8},{8,0},{1,9},{9,1},{2,10},{10,2},{3,11},{11,3},{4,12},{12,4},... | collective-permute-start | bytes 147464 | tf_op jit(solution)/shard_map/ppermute | solution.py:406
  15.4 3.6 %collective-permute-start.2 = (f32[8,1536]{1,0:T(8,128)S(1)}, f32[8,1536]{1,0:T(8,128)S(1)}, u32[]{:S(2)}, u32[]{:S(2)}) collective-permute-start(f32[8,1536]{1,0:T(8,128)S(1)} %get-tuple-element.12), channel_id=1, source_target_pairs={{0,1},{1,2},{2,3},{3,4},{4,5},{5,6},{6,7},{8,9},{9,10},{10,11},{11... | collective-permute-start | bytes 147464 | tf_op jit(solution)/shard_map/ppermute | solution.py:379
  19.0 1.9 %collective-permute-start.3 = (f32[8,1536]{1,0:T(8,128)S(1)}, f32[8,1536]{1,0:T(8,128)S(1)}, u32[]{:S(2)}, u32[]{:S(2)}) collective-permute-start(f32[8,1536]{1,0:T(8,128)S(1)} %get-tuple-element.13), channel_id=1, source_target_pairs={{1,0},{2,1},{3,2},{4,3},{5,4},{6,5},{7,6},{9,8},{10,9},{11,10},{12... | collective-permute-start | bytes 147464 | tf_op jit(solution)/shard_map/ppermute | solution.py:379
  20.9 0.0 collective-permute-done.1.refs_1_.refs_0_
  20.9 0.0 collective-permute-done.2.refs_2_
  20.9 3.5 %collective-permute-done.3.refs_3_ = f32[8,1536]{1,0:T(8,128)S(1)} collective-permute-done((f32[8,1536]{1,0:T(8,128)S(1)}, f32[8,1536]{1,0:T(8,128)S(1)}, u32[]{:S(2)}, u32[]{:S(2)}) %collective-permute-start.3) | collective-permute-done | bytes 49184 | tf_op jit(solution)/shard_map/ppermute | solution.py:379
  24.4 0.0 all-to-all-done
  24.4 0.0 collective-permute-done.refs_0_
  24.4 0.0 copy-done.1
  24.4 0.0 copy-done.8
  24.4 0.0 copy-done.9
  24.4 0.0 copy-done.10
  24.4 0.0 copy-done.4
  24.4 4.0 %shard_map.110 = (f32[7,8,1536]{2,1,0:T(8,128)S(1)}, f32[7,8,1536]{2,1,0:T(8,128)S(1)}, f32[16,1536]{1,0:T(8,128)S(1)}, f32[16,1536]{1,0:T(8,128)S(1)}) custom-call(f32[1,7,1,8,1536]{4,3,2,1,0:T(8,128)S(1)} %copy-done.1, f32[1,1,8,1536]{3,2,1,0:T(8,128)S(1)} %copy-done.3, f32[1,7,1,8,1536]{4,3,2,1,0:T(8,128)S(1)} %collective-permute-done.refs_0_, ...), custom_call_target="tpu_custom_call" | custom-call | tf_op jit(solution)/shard_map/pallas_call | solution.py:390
  28.4 1.9 %collective-permute-start.4 = (f32[16,1536]{1,0:T(8,128)S(1)}, f32[16,1536]{1,0:T(8,128)S(1)}, u32[]{:S(2)}, u32[]{:S(2)}) collective-permute-start(f32[16,1536]{1,0:T(8,128)S(1)} %get-tuple-element.17), channel_id=1, source_target_pairs={{0,1},{1,2},{2,3},{3,4},{4,5},{5,6},{6,7},{8,9},{9,10},{10,11},{11... | collective-permute-start | bytes 294920 | tf_op jit(solution)/shard_map/ppermute | solution.py:379
  30.3 2.4 %collective-permute-start.5 = (f32[16,1536]{1,0:T(8,128)S(1)}, f32[16,1536]{1,0:T(8,128)S(1)}, u32[]{:S(2)}, u32[]{:S(2)}) collective-permute-start(f32[16,1536]{1,0:T(8,128)S(1)} %get-tuple-element.18), channel_id=1, source_target_pairs={{1,0},{2,1},{3,2},{4,3},{5,4},{6,5},{7,6},{9,8},{10,9},{11,10},{12... | collective-permute-start | bytes 294920 | tf_op jit(solution)/shard_map/ppermute | solution.py:379
  32.7 0.0 collective-permute-done.4.refs_1_
  32.8 3.5 %collective-permute-done.5.refs_2_ = f32[16,1536]{1,0:T(8,128)S(1)} collective-permute-done((f32[16,1536]{1,0:T(8,128)S(1)}, f32[16,1536]{1,0:T(8,128)S(1)}, u32[]{:S(2)}, u32[]{:S(2)}) %collective-permute-start.5) | collective-permute-done | bytes 98336 | tf_op jit(solution)/shard_map/ppermute | solution.py:379
  36.3 1.8 %shard_map.111 = f32[1,7,1,8,1536]{4,3,2,1,0:T(8,128)} custom-call(f32[7,8,1536]{2,1,0:T(8,128)S(1)} %get-tuple-element.15.first, f32[7,8,1536]{2,1,0:T(8,128)S(1)} %get-tuple-element.16.base, f32[1,1,8,1536]{3,2,1,0:T(8,128)S(1)} %copy-done.3, f32[1,1,8,1536]{3,2,1,0:T(8,128)S(1)} %collective-permute-done.1.refs_1_.refs_0_, ...), custom_call_target="tpu_custom_call" | custom-call | tf_op jit(solution)/shard_map/pallas_call | solution.py:390
Async XLA Ops:
  0.0 2.1 %copy-start.5 = (f32[7]{0:T(128)S(1)}, f32[7]{0:T(128)}, u32[]{:S(2)}) copy-start(f32[7]{0:T(128)} %refs_3_.1) | copy-start | bytes 88
  0.0 2.1 %copy-start.12 = (s32[1,1,256,1]{2,3,1,0:T(1,128)S(1)}, s32[1,1,256,1]{2,3,1,0:T(1,128)}, u32[]{:S(2)}) copy-start(s32[1,1,256,1]{2,3,1,0:T(1,128)} %param.18) | copy-start | bytes 3076
  0.0 24.4 %collective-permute-start = (f32[1,7,1,8,1536]{4,3,2,1,0:T(8,128)}, f32[1,7,1,8,1536]{4,3,2,1,0:T(8,128)S(1)}, u32[]{:S(2)}, u32[]{:S(2)}) collective-permute-start(f32[1,7,1,8,1536]{4,3,2,1,0:T(8,128)} %adj.3), channel_id=1, source_target_pairs={{0,8},{8,0},{1,9},{9,1},{2,10},{10,2},{3,11},{11,3},{4,12},{12,4},... | collective-permute-start | bytes 1032200 | tf_op jit(solution)/shard_map/ppermute | solution.py:405
  2.1 1.0 %copy-start = (f32[1,7,1,8,1536]{4,3,2,1,0:T(8,128)S(1)}, f32[1,7,1,8,1536]{4,3,2,1,0:T(8,128)}, u32[]{:S(2)}) copy-start(f32[1,7,1,8,1536]{4,3,2,1,0:T(8,128)} %adj.3) | copy-start | bytes 1032196
  3.1 0.8 %copy-start.2 = (f32[1,1,8,1536]{3,2,1,0:T(8,128)S(1)}, f32[1,1,8,1536]{3,2,1,0:T(8,128)}, u32[]{:S(2)}) copy-start(f32[1,1,8,1536]{3,2,1,0:T(8,128)} %cond.5) | copy-start | bytes 147460
  3.9 0.7 %copy-start.6 = (s32[1,1,4,256]{3,2,1,0:T(4,128)S(1)}, s32[1,1,4,256]{3,2,1,0:T(4,128)}, u32[]{:S(2)}) copy-start(s32[1,1,4,256]{3,2,1,0:T(4,128)} %cell.1) | copy-start | bytes 12292
  4.6 0.7 %copy-start.7 = (f32[1,1,4,256]{3,2,1,0:T(4,128)S(1)}, f32[1,1,4,256]{3,2,1,0:T(4,128)}, u32[]{:S(2)}) copy-start(f32[1,1,4,256]{3,2,1,0:T(4,128)} %wt.1) | copy-start | bytes 12292
  5.3 0.7 %copy-start.11 = (f32[1,1,2,256]{3,2,1,0:T(2,128)S(1)}, f32[1,1,2,256]{3,2,1,0:T(2,128)}, u32[]{:S(2)}) copy-start(f32[1,1,2,256]{3,2,1,0:T(2,128)} %misfit.1) | copy-start | bytes 6148
  5.9 18.5 %copy-start.1 = (f32[1,7,1,8,1536]{4,3,2,1,0:T(8,128)S(1)}, f32[1,7,1,8,1536]{4,3,2,1,0:T(8,128)}, u32[]{:S(2)}) copy-start(f32[1,7,1,8,1536]{4,3,2,1,0:T(8,128)} %adj.3) | copy-start | bytes 1032196
  8.2 5.7 %copy-start.3 = (f32[1,1,8,1536]{3,2,1,0:T(8,128)S(1)}, f32[1,1,8,1536]{3,2,1,0:T(8,128)}, u32[]{:S(2)}) copy-start(f32[1,1,8,1536]{3,2,1,0:T(8,128)} %cond.5) | copy-start | bytes 147460
  8.2 16.2 %copy-start.8 = (s32[2,4,64]{2,1,0:T(4,128)S(1)}, s32[2,4,64]{2,1,0:T(4,128)}, u32[]{:S(2)}) copy-start(s32[2,4,64]{2,1,0:T(4,128)} %refs_7_.1) | copy-start | bytes 6148
  8.2 16.2 %copy-start.9 = (s32[2,4,64]{2,1,0:T(4,128)S(1)}, s32[2,4,64]{2,1,0:T(4,128)}, u32[]{:S(2)}) copy-start(s32[2,4,64]{2,1,0:T(4,128)} %refs_8_.1) | copy-start | bytes 6148
  8.2 16.2 %copy-start.10 = (f32[2,4,64]{2,1,0:T(4,128)S(1)}, f32[2,4,64]{2,1,0:T(4,128)}, u32[]{:S(2)}) copy-start(f32[2,4,64]{2,1,0:T(4,128)} %refs_9_.1) | copy-start | bytes 6148
  8.2 16.2 %all-to-all-start = ((f32[32,8,128]{2,1,0:T(8,128)}), f32[32,8,128]{2,1,0:T(8,128)S(1)}, u32[]{:S(2)}, u32[]{:S(2)}) async-start(f32[32,8,128]{2,1,0:T(8,128)} %get-tuple-element.14), calls=%async_computation | async-start | bytes 262144 | tf_op jit(solution)/shard_map/all_to_all | solution.py:417
  13.9 10.5 %copy-start.4 = (f32[7,7]{1,0:T(8,128)S(1)}, f32[7,7]{1,0:T(8,128)}, u32[]{:S(2)}) copy-start(f32[7,7]{1,0:T(8,128)} %refs_4_.1) | copy-start | bytes 592
  13.9 7.0 %collective-permute-start.1 = (f32[1,1,8,1536]{3,2,1,0:T(8,128)S(1)}, f32[1,1,8,1536]{3,2,1,0:T(8,128)S(1)}, u32[]{:S(2)}, u32[]{:S(2)}) collective-permute-start(f32[1,1,8,1536]{3,2,1,0:T(8,128)S(1)} %copy-done.3), channel_id=1, source_target_pairs={{0,8},{8,0},{1,9},{9,1},{2,10},{10,2},{3,11},{11,3},{4,12},{12,4},... | collective-permute-start | bytes 147464 | tf_op jit(solution)/shard_map/ppermute | solution.py:406
  15.4 5.6 %collective-permute-start.2 = (f32[8,1536]{1,0:T(8,128)S(1)}, f32[8,1536]{1,0:T(8,128)S(1)}, u32[]{:S(2)}, u32[]{:S(2)}) collective-permute-start(f32[8,1536]{1,0:T(8,128)S(1)} %get-tuple-element.12), channel_id=1, source_target_pairs={{0,1},{1,2},{2,3},{3,4},{4,5},{5,6},{6,7},{8,9},{9,10},{10,11},{11... | collective-permute-start | bytes 147464 | tf_op jit(solution)/shard_map/ppermute | solution.py:379
  19.0 5.4 %collective-permute-start.3 = (f32[8,1536]{1,0:T(8,128)S(1)}, f32[8,1536]{1,0:T(8,128)S(1)}, u32[]{:S(2)}, u32[]{:S(2)}) collective-permute-start(f32[8,1536]{1,0:T(8,128)S(1)} %get-tuple-element.13), channel_id=1, source_target_pairs={{1,0},{2,1},{3,2},{4,3},{5,4},{6,5},{7,6},{9,8},{10,9},{11,10},{12... | collective-permute-start | bytes 147464 | tf_op jit(solution)/shard_map/ppermute | solution.py:379
  28.4 4.3 %collective-permute-start.4 = (f32[16,1536]{1,0:T(8,128)S(1)}, f32[16,1536]{1,0:T(8,128)S(1)}, u32[]{:S(2)}, u32[]{:S(2)}) collective-permute-start(f32[16,1536]{1,0:T(8,128)S(1)} %get-tuple-element.17), channel_id=1, source_target_pairs={{0,1},{1,2},{2,3},{3,4},{4,5},{5,6},{6,7},{8,9},{9,10},{10,11},{11... | collective-permute-start | bytes 294920 | tf_op jit(solution)/shard_map/ppermute | solution.py:379
  30.3 5.9 %collective-permute-start.5 = (f32[16,1536]{1,0:T(8,128)S(1)}, f32[16,1536]{1,0:T(8,128)S(1)}, u32[]{:S(2)}, u32[]{:S(2)}) collective-permute-start(f32[16,1536]{1,0:T(8,128)S(1)} %get-tuple-element.18), channel_id=1, source_target_pairs={{1,0},{2,1},{3,2},{4,3},{5,4},{6,5},{7,6},{9,8},{10,9},{11,10},{12... | collective-permute-start | bytes 294920 | tf_op jit(solution)/shard_map/ppermute | solution.py:379

commit v2 on v1

--- a/solution.py
+++ b/solution.py
@@ -66,13 +66,16 @@
     return x if shift == 0 else pltpu.roll(x, shift, axis)
 
 
-def pack_kernel(z, adj, cond, diffus, dest, cell, wt, misfit, pay, up, down):
-    for f in range(z.fields):
-        s = adj[0, f, 0] * (cond[0, 0] * diffus[f])
-        up[f : f + 1, :] = s[z.rows - 1 :, :]
-        down[f : f + 1, :] = s[:1, :]
-    up[z.fields :, :] = jnp.zeros((SUBL - z.fields, z.cols), F32)
-    down[z.fields :, :] = jnp.zeros((SUBL - z.fields, z.cols), F32)
+def pack_kernel(z, *refs):
+    count = 7
+    given, (pay, mate, next_), held, sems = refs[:count], refs[count : count + 3], refs[count + 3 : -1], refs[-1]
+    order = (3, 4, 5, 6, 2, 1, 0)
+    copies = [pltpu.make_async_copy(given[n], held[n], sems.at[n]) for n in range(count)]
+    for n in order:
+        copies[n].start()
+    adj, cond, diffus, dest, cell, wt, misfit = held
+    for n in order[:4]:
+        copies[n].wait()
 
     owner = dest[...]
     height = max(16, z.tiles)
@@ -116,6 +119,9 @@
         total = term if total is None else total + term
     edge_force = total[:1]
 
+    for n in order[4:]:
+        copies[n].wait()
+
     lane = iota((z.rows, LANES), 1)
     sub = iota((z.rows, LANES), 0)
     strips = []
@@ -137,6 +143,29 @@
         part = jnp.concatenate([slots[:, t * LANES : (t + 1) * LANES], common], axis=0)
         for group in range(z.panels * z.rads):
             pay[group * z.tiles + t] = part
+
+    for f in range(z.fields):
+        s = adj[0, f, 0] * (cond[0, 0] * diffus[f])
+        mate[f : f + 1, :], next_[f : f + 1, :] = facing(s)
+    for ref in (mate, next_):
+        ref[z.fields :, :] = jnp.zeros((SUBL - z.fields, z.cols), F32)
+
+
+def even_tile():
+    return lax.axis_index("ang") % 2 == 0
+
+
+def facing(s):
+    top, bottom = s[:1], s[s.shape[0] - 1 :]
+    even = even_tile()
+    return jnp.where(even, bottom, top), jnp.where(even, top, bottom)
+
+
+def around(z, mate, next_):
+    even = even_tile()
+    tile = lax.axis_index("ang")
+    next_ = jnp.where((tile == 0) | (tile == z.tiles - 1), 0.0, next_)
+    return jnp.where(even, next_, mate), jnp.where(even, mate, next_)
 
 
 def by_field(z, scalar, width):
@@ -249,8 +278,9 @@
         adj2, cond2, *refs = refs
     else:
         beside, *refs = refs
-    above, below, recv, diffus, couple, grow, gcol, gwt, *refs = refs
-    first, base, up, down, spread_a, spread_b = refs
+    mate_in, next_in, recv, diffus, couple, grow, gcol, gwt, *refs = refs
+    first, base, mate, next_, spread_a, spread_b = refs
+    above, below = around(z, mate_in[...], next_in[...])
     panel, rad, tile = lax.axis_index("panel"), lax.axis_index("rad"), lax.axis_index("ang")
     other = 1 - panel
     outer = jnp.where(rad == z.rads - 1, 1.0, 0.0)
@@ -335,8 +365,8 @@
             if f == 3:
                 part = part + force1 * (1.0 - outer)
             second = second + part * (far_c * diffus[f])
-            up[SUBL + f : SUBL + f + 1, :] = far[z.rows - 1 :]
-            down[SUBL + f : SUBL + f + 1, :] = far[:1]
+            at = SUBL + f
+            mate[at : at + 1, :], next_[at : at + 1, :] = facing(far)
         else:
             new = new + beside[f]
         if f == 3:
@@ -345,10 +375,9 @@
         first[f] = new
         base[f] = second
         s = new * (own_c * diffus[f])
-        up[f : f + 1, :] = s[z.rows - 1 :]
-        down[f : f + 1, :] = s[:1]
+        mate[f : f + 1, :], next_[f : f + 1, :] = facing(s)
     for half in range(2 if z.pair else 1):
-        for ref in (up, down):
+        for ref in (mate, next_):
             ref[half * SUBL + z.fields : (half + 1) * SUBL, :] = jnp.zeros((SUBL - z.fields, z.cols), F32)
 
 
@@ -357,7 +386,8 @@
         cond2, *refs = refs
     else:
         beside, *refs = refs
-    above, below, diffus, couple, out = refs
+    mate_in, next_in, diffus, couple, out = refs
+    above, below = around(z, mate_in[...], next_in[...])
     own_c = cond[0, 0]
     for f in range(z.fields):
         s = first[f] * (own_c * diffus[f])
@@ -383,9 +413,25 @@
     return shifted(x, axis, 1) + shifted(x, axis, -1)
 
 
-def call(kernel, shapes, scratch, args, scalars):
+def beside_rows(z, mate, next_):
+    pairs, links = [], []
+    for rad in range(z.rads):
+        at = rad * z.tiles
+        other = (rad ^ 1) * z.tiles
+        for i in range(z.tiles):
+            pairs.append((at + i, at + (i ^ 1)))
+            if 0 < i < z.tiles - 1:
+                links.append((at + i, at + (i + 1 if i % 2 else i - 1)))
+            else:
+                links.append((at + i, other + i))
+    axes = ("rad", "ang")
+    return lax.ppermute(mate, axes, pairs), lax.ppermute(next_, axes, links)
+
+
+def call(kernel, shapes, scratch, args, scalars=(), spaces=None, room=48):
     specs = [
-        pl.BlockSpec(memory_space=pltpu.SMEM if n in scalars else pltpu.VMEM) for n in range(len(args))
+        pl.BlockSpec(memory_space=spaces or (pltpu.SMEM if n in scalars else pltpu.VMEM))
+        for n in range(len(args))
     ]
     return pl.pallas_call(
         kernel,
@@ -393,7 +439,7 @@
         in_specs=specs,
         out_specs=[pl.BlockSpec(memory_space=pltpu.VMEM)] * len(shapes),
         scratch_shapes=scratch,
-        compiler_params=pltpu.CompilerParams(vmem_limit_bytes=48 << 20),
+        compiler_params=pltpu.CompilerParams(vmem_limit_bytes=room << 20),
     )(*args)
 
 
@@ -407,34 +453,37 @@
     else:
         scaled = diffus[:, None, None] * cond[0, 0][None] * adj[0, :, 0]
         beside = both_sides(scaled, "rad")
-    pay, up, down = call(
+    given = [adj, cond, diffus, obs_dest.reshape(1, z.count), obs_cell, obs_wt, misfit]
+    held = [pltpu.SMEM(x.shape, x.dtype) if x is diffus else pltpu.VMEM(x.shape, x.dtype) for x in given]
+    pay, mate, next_ = call(
         functools.partial(pack_kernel, z),
         [(z.devices, z.block, LANES), (SUBL, z.cols), (SUBL, z.cols)],
-        [],
-        [adj, cond, diffus, obs_dest.reshape(1, z.count), obs_cell, obs_wt, misfit],
-        (2,),
+        held + [pltpu.SemaphoreType.DMA((len(given),))],
+        given,
+        spaces=pltpu.HBM,
+        room=64,
     )
     recv = lax.all_to_all(pay, ("panel", "rad", "ang"), split_axis=0, concat_axis=0, tiled=True)
-    above, below = shifted(up, "ang", 1), shifted(down, "ang", -1)
+    mate, next_ = beside_rows(z, mate, next_)
     points = z.rads * z.tiles * z.npr * LANES
     lines = (SUBL * (2 if z.pair else 1), z.cols)
     args = [adj, cond] + ([adj2, cond2] if z.pair else [beside])
-    args += [above, below, recv.reshape(z.devices * z.block, LANES), diffus, couple]
+    args += [mate, next_, recv.reshape(z.devices * z.block, LANES), diffus, couple]
     scalars = (len(args) - 2, len(args) - 1)
-    first, base, up, down = call(
+    first, base, mate, next_ = call(
         functools.partial(first_kernel, z),
         [state, state, lines, lines],
         [pltpu.VMEM((2 * TIMES * z.hi, points), BF16), pltpu.VMEM((LOW, points), BF16)],
         args + [ghost_row, ghost_col, ghost_wt],
         scalars,
     )
-    above, below = shifted(up, "ang", 1), shifted(down, "ang", -1)
+    mate, next_ = beside_rows(z, mate, next_)
     if z.pair:
         args = [first, base, cond, cond2]
     else:
         scaled = diffus[:, None, None] * cond[0, 0][None] * first
         args = [first, base, cond, both_sides(scaled, "rad")]
-    args += [above, below, diffus, couple]
+    args += [mate, next_, diffus, couple]
     (out,) = call(functools.partial(second_kernel, z), [adj.shape], [], args, (6, 7))
     return out
 

time: 38.5 us -> 31.4 us (0.82)
  the two profiles are of different devices: /device:TPU:1 before, /device:TPU:0 now
where the time goes in v2:
time: 31.4 us; the launch traced here: 31.1 us
  starting transfers between devices  11 us (35%)
  waiting for transfers between devices  10 us (32%)
  Pallas kernels  8.89 us (28%)
  local copies, waits for them, and re-layouts  1.02 us (3%)
    pallas_call x3, Pallas kernels, call(): pl.pallas_call(kernel, out_shape=[jax.ShapeDtypeStruct(shape, F32) for sh...  8.89 us
    ppermute x4, waiting for transfers between devices, beside_rows(): return (lax.ppermute(mate, axes, pairs), lax.ppermute(next_, axes, links))  5.83 us
    all_to_all x1, starting transfers between devices, body(): lax.all_to_all(pay, ('panel', 'rad', 'ang'), split_axis=0, concat_axis=0,...  4.9 us
    ppermute x1, starting transfers between devices, body(): adj2 = lax.ppermute(adj, 'rad', swap)  2.97 us
    ppermute x1, waiting for transfers between devices, body(): cond2 = lax.ppermute(cond, 'rad', swap)  2.19 us
    all_to_all x1, waiting for transfers between devices, body(): lax.all_to_all(pay, ('panel', 'rad', 'ang'), split_axis=0, concat_axis=0,...  2.02 us
    ppermute x1, starting transfers between devices, body(): cond2 = lax.ppermute(cond, 'rad', swap)  1.83 us
    ppermute x4, starting transfers between devices, beside_rows(): return (lax.ppermute(mate, axes, pairs), lax.ppermute(next_, axes, links))  1.27 us
  transfers between devices with their start and end apart: 7, of which 5 were waited for; matrix products, arithmetic and copies ran while one was open for 0% of the time, Pallas kernels for 8%

profile of v2, /device:TPU:0, one launch (start us, length us, event | category | flops | bytes accessed | tf_op | source)
XLA Modules:
  0.0 31.1 jit_solution(9559182922917924542)
XLA Ops:
  0.0 3.0 %collective-permute-start = (f32[1,7,1,8,1536]{4,3,2,1,0:T(8,128)}, f32[1,7,1,8,1536]{4,3,2,1,0:T(8,128)}, u32[]{:S(2)}, u32[]{:S(2)}) collective-permute-start(f32[1,7,1,8,1536]{4,3,2,1,0:T(8,128)} %adj.1), channel_id=1, source_target_pairs={{0,8},{8,0},{1,9},{9,1},{2,10},{10,2},{3,11},{11,3},{4,12},{12,4},... | collective-permute-start | bytes 1032200 | tf_op jit(solution)/shard_map/ppermute | solution.py:451
  3.0 2.6 %shard_map.109 = (f32[32,8,128]{2,1,0:T(8,128)}, f32[8,1536]{1,0:T(8,128)}, f32[8,1536]{1,0:T(8,128)}) custom-call(f32[1,7,1,8,1536]{4,3,2,1,0:T(8,128)} %adj.1, f32[1,1,8,1536]{3,2,1,0:T(8,128)} %cond.3, f32[7]{0:T(128)} %refs_3_.1, s32[1,256]{1,0:T(1,128)} %bitcast.3, s32[1,1,4,256]{3,2,1,0:T(4,128)} %refs_4_.2, f32[1,1,4,256]{3,2,1,0:T(4,128)} %refs_5_.2, ...), custom_call_target="tpu_custom_call" | custom-call | tf_op jit(solution)/shard_map/pallas_call | solution.py:436
  5.6 0.0 copy-start.1
  5.6 0.0 copy-start.8
  5.6 0.0 copy-start.7
  5.6 0.0 copy-start.4
  5.6 0.0 copy-start.5
  5.6 0.0 copy-start.6
  5.6 4.9 %all-to-all-start = ((f32[32,8,128]{2,1,0:T(8,128)}), f32[32,8,128]{2,1,0:T(8,128)S(1)}, u32[]{:S(2)}, u32[]{:S(2)}) async-start(f32[32,8,128]{2,1,0:T(8,128)} %get-tuple-element.14), calls=%async_computation | async-start | bytes 262144 | tf_op jit(solution)/shard_map/all_to_all | solution.py:466
  10.5 0.0 copy-done.1
  10.5 0.0 copy-start.2
  10.6 1.8 %collective-permute-start.1 = (f32[1,1,8,1536]{3,2,1,0:T(8,128)S(1)}, f32[1,1,8,1536]{3,2,1,0:T(8,128)S(1)}, u32[]{:S(2)}, u32[]{:S(2)}) collective-permute-start(f32[1,1,8,1536]{3,2,1,0:T(8,128)S(1)} %copy-done.1), channel_id=1, source_target_pairs={{0,8},{8,0},{1,9},{9,1},{2,10},{10,2},{3,11},{11,3},{4,12},{12,4},... | collective-permute-start | bytes 147464 | tf_op jit(solution)/shard_map/ppermute | solution.py:452
  12.4 0.0 copy-done.8
  12.4 0.0 collective-permute-start.2
  12.4 0.0 copy-done.7
  12.4 0.0 copy-start.3
  12.4 0.3 %collective-permute-start.3 = (f32[8,1536]{1,0:T(8,128)S(1)}, f32[8,1536]{1,0:T(8,128)S(1)}, u32[]{:S(2)}, u32[]{:S(2)}) collective-permute-start(f32[8,1536]{1,0:T(8,128)S(1)} %copy-done.7), channel_id=1, source_target_pairs={{0,8},{1,2},{2,1},{3,4},{4,3},{5,6},{6,5},{7,15},{8,0},{9,10},{10,... | collective-permute-start | bytes 147464 | tf_op jit(solution)/shard_map/ppermute | solution.py:428
  12.7 2.2 %collective-permute-done.1.refs_1_.refs_0_ = f32[1,1,8,1536]{3,2,1,0:T(8,128)S(1)} collective-permute-done((f32[1,1,8,1536]{3,2,1,0:T(8,128)S(1)}, f32[1,1,8,1536]{3,2,1,0:T(8,128)S(1)}, u32[]{:S(2)}, u32[]{:S(2)}) %collective-permute-start.1) | collective-permute-done | bytes 49184 | tf_op jit(solution)/shard_map/ppermute | solution.py:452
  14.9 0.0 collective-permute-done.2.refs_2_
  14.9 1.8 %collective-permute-done.3.refs_3_ = f32[8,1536]{1,0:T(8,128)S(1)} collective-permute-done((f32[8,1536]{1,0:T(8,128)S(1)}, f32[8,1536]{1,0:T(8,128)S(1)}, u32[]{:S(2)}, u32[]{:S(2)}) %collective-permute-start.3) | collective-permute-done | bytes 49184 | tf_op jit(solution)/shard_map/ppermute | solution.py:428
  16.7 2.0 %all-to-all-done = f32[32,8,128]{2,1,0:T(8,128)S(1)} async-done(((f32[32,8,128]{2,1,0:T(8,128)}), f32[32,8,128]{2,1,0:T(8,128)S(1)}, u32[]{:S(2)}, u32[]{:S(2)}) %all-to-all-start) | async-done | bytes 131104 | tf_op jit(solution)/shard_map/all_to_all | solution.py:466
  18.7 0.0 collective-permute-done.refs_0_
  18.7 0.0 copy-done.4
  18.7 0.0 copy-done.5
  18.7 0.0 copy-done.6
  18.7 0.0 copy-done.2
  18.7 0.0 copy-done.3
  18.8 0.0 copy-start
  18.8 1.0 %copy-done = f32[1,7,1,8,1536]{4,3,2,1,0:T(8,128)S(1)} copy-done((f32[1,7,1,8,1536]{4,3,2,1,0:T(8,128)S(1)}, f32[1,7,1,8,1536]{4,3,2,1,0:T(8,128)}, u32[]{:S(2)}) %copy-start) | copy-done | bytes 344088
  19.7 4.5 %shard_map.110 = (f32[7,8,1536]{2,1,0:T(8,128)S(1)}, f32[7,8,1536]{2,1,0:T(8,128)S(1)}, f32[16,1536]{1,0:T(8,128)S(1)}, f32[16,1536]{1,0:T(8,128)S(1)}) custom-call(f32[1,7,1,8,1536]{4,3,2,1,0:T(8,128)S(1)} %copy-done, f32[1,1,8,1536]{3,2,1,0:T(8,128)S(1)} %copy-done.1, f32[1,7,1,8,1536]{4,3,2,1,0:T(8,128)} %collective-permute-done.refs_0_, ...), custom_call_target="tpu_custom_call" | custom-call | tf_op jit(solution)/shard_map/pallas_call | solution.py:436
  24.2 0.4 %collective-permute-start.4 = (f32[16,1536]{1,0:T(8,128)S(1)}, f32[16,1536]{1,0:T(8,128)S(1)}, u32[]{:S(2)}, u32[]{:S(2)}) collective-permute-start(f32[16,1536]{1,0:T(8,128)S(1)} %get-tuple-element.17), channel_id=1, source_target_pairs={{0,1},{1,0},{2,3},{3,2},{4,5},{5,4},{6,7},{7,6},{8,9},{9,8},{10,11... | collective-permute-start | bytes 294920 | tf_op jit(solution)/shard_map/ppermute | solution.py:428
  24.6 0.6 %collective-permute-start.5 = (f32[16,1536]{1,0:T(8,128)S(1)}, f32[16,1536]{1,0:T(8,128)S(1)}, u32[]{:S(2)}, u32[]{:S(2)}) collective-permute-start(f32[16,1536]{1,0:T(8,128)S(1)} %get-tuple-element.18), channel_id=1, source_target_pairs={{0,8},{1,2},{2,1},{3,4},{4,3},{5,6},{6,5},{7,15},{8,0},{9,10},{10,... | collective-permute-start | bytes 294920 | tf_op jit(solution)/shard_map/ppermute | solution.py:428
  25.2 0.4 %collective-permute-done.4.refs_1_ = f32[16,1536]{1,0:T(8,128)S(1)} collective-permute-done((f32[16,1536]{1,0:T(8,128)S(1)}, f32[16,1536]{1,0:T(8,128)S(1)}, u32[]{:S(2)}, u32[]{:S(2)}) %collective-permute-start.4) | collective-permute-done | bytes 98336 | tf_op jit(solution)/shard_map/ppermute | solution.py:428
  25.6 3.6 %collective-permute-done.5.refs_2_ = f32[16,1536]{1,0:T(8,128)S(1)} collective-permute-done((f32[16,1536]{1,0:T(8,128)S(1)}, f32[16,1536]{1,0:T(8,128)S(1)}, u32[]{:S(2)}, u32[]{:S(2)}) %collective-permute-start.5) | collective-permute-done | bytes 98336 | tf_op jit(solution)/shard_map/ppermute | solution.py:428
  29.2 1.8 %shard_map.111 = f32[1,7,1,8,1536]{4,3,2,1,0:T(8,128)} custom-call(f32[7,8,1536]{2,1,0:T(8,128)S(1)} %get-tuple-element.15.first, f32[7,8,1536]{2,1,0:T(8,128)S(1)} %get-tuple-element.16.base, f32[1,1,8,1536]{3,2,1,0:T(8,128)S(1)} %copy-done.1, f32[1,1,8,1536]{3,2,1,0:T(8,128)S(1)} %collective-permute-done.1.refs_1_.refs_0_, ...), custom_call_target="tpu_custom_call" | custom-call | tf_op jit(solution)/shard_map/pallas_call | solution.py:436
Async XLA Ops:
  0.0 18.7 %collective-permute-start = (f32[1,7,1,8,1536]{4,3,2,1,0:T(8,128)}, f32[1,7,1,8,1536]{4,3,2,1,0:T(8,128)}, u32[]{:S(2)}, u32[]{:S(2)}) collective-permute-start(f32[1,7,1,8,1536]{4,3,2,1,0:T(8,128)} %adj.1), channel_id=1, source_target_pairs={{0,8},{8,0},{1,9},{9,1},{2,10},{10,2},{3,11},{11,3},{4,12},{12,4},... | collective-permute-start | bytes 1032200 | tf_op jit(solution)/shard_map/ppermute | solution.py:451
  5.6 5.0 %copy-start.1 = (f32[1,1,8,1536]{3,2,1,0:T(8,128)S(1)}, f32[1,1,8,1536]{3,2,1,0:T(8,128)}, u32[]{:S(2)}) copy-start(f32[1,1,8,1536]{3,2,1,0:T(8,128)} %cond.3) | copy-start | bytes 147460
  5.6 6.8 %copy-start.8 = (f32[8,1536]{1,0:T(8,128)S(1)}, f32[8,1536]{1,0:T(8,128)}, u32[]{:S(2)}) copy-start(f32[8,1536]{1,0:T(8,128)} %get-tuple-element.12) | copy-start | bytes 147460
  5.6 6.8 %copy-start.7 = (f32[8,1536]{1,0:T(8,128)S(1)}, f32[8,1536]{1,0:T(8,128)}, u32[]{:S(2)}) copy-start(f32[8,1536]{1,0:T(8,128)} %get-tuple-element.13) | copy-start | bytes 147460
  5.6 13.1 %copy-start.4 = (s32[2,4,64]{2,1,0:T(4,128)S(1)}, s32[2,4,64]{2,1,0:T(4,128)}, u32[]{:S(2)}) copy-start(s32[2,4,64]{2,1,0:T(4,128)} %refs_7_.1) | copy-start | bytes 6148
  5.6 13.1 %copy-start.5 = (s32[2,4,64]{2,1,0:T(4,128)S(1)}, s32[2,4,64]{2,1,0:T(4,128)}, u32[]{:S(2)}) copy-start(s32[2,4,64]{2,1,0:T(4,128)} %refs_8_.1) | copy-start | bytes 6148
  5.6 13.1 %copy-start.6 = (f32[2,4,64]{2,1,0:T(4,128)S(1)}, f32[2,4,64]{2,1,0:T(4,128)}, u32[]{:S(2)}) copy-start(f32[2,4,64]{2,1,0:T(4,128)} %refs_9_.1) | copy-start | bytes 6148
  5.6 13.1 %all-to-all-start = ((f32[32,8,128]{2,1,0:T(8,128)}), f32[32,8,128]{2,1,0:T(8,128)S(1)}, u32[]{:S(2)}, u32[]{:S(2)}) async-start(f32[32,8,128]{2,1,0:T(8,128)} %get-tuple-element.14), calls=%async_computation | async-start | bytes 262144 | tf_op jit(solution)/shard_map/all_to_all | solution.py:466
  10.5 8.2 %copy-start.2 = (f32[7,7]{1,0:T(8,128)S(1)}, f32[7,7]{1,0:T(8,128)}, u32[]{:S(2)}) copy-start(f32[7,7]{1,0:T(8,128)} %refs_4_.3) | copy-start | bytes 592
  10.6 4.4 %collective-permute-start.1 = (f32[1,1,8,1536]{3,2,1,0:T(8,128)S(1)}, f32[1,1,8,1536]{3,2,1,0:T(8,128)S(1)}, u32[]{:S(2)}, u32[]{:S(2)}) collective-permute-start(f32[1,1,8,1536]{3,2,1,0:T(8,128)S(1)} %copy-done.1), channel_id=1, source_target_pairs={{0,8},{8,0},{1,9},{9,1},{2,10},{10,2},{3,11},{11,3},{4,12},{12,4},... | collective-permute-start | bytes 147464 | tf_op jit(solution)/shard_map/ppermute | solution.py:452
  12.4 2.5 %collective-permute-start.2 = (f32[8,1536]{1,0:T(8,128)S(1)}, f32[8,1536]{1,0:T(8,128)S(1)}, u32[]{:S(2)}, u32[]{:S(2)}) collective-permute-start(f32[8,1536]{1,0:T(8,128)S(1)} %copy-done.8), channel_id=1, source_target_pairs={{0,1},{1,0},{2,3},{3,2},{4,5},{5,4},{6,7},{7,6},{8,9},{9,8},{10,11... | collective-permute-start | bytes 147464 | tf_op jit(solution)/shard_map/ppermute | solution.py:428
  12.4 6.3 %copy-start.3 = (f32[7]{0:T(128)S(1)}, f32[7]{0:T(128)}, u32[]{:S(2)}) copy-start(f32[7]{0:T(128)} %refs_3_.1) | copy-start | bytes 88
  12.4 4.3 %collective-permute-start.3 = (f32[8,1536]{1,0:T(8,128)S(1)}, f32[8,1536]{1,0:T(8,128)S(1)}, u32[]{:S(2)}, u32[]{:S(2)}) collective-permute-start(f32[8,1536]{1,0:T(8,128)S(1)} %copy-done.7), channel_id=1, source_target_pairs={{0,8},{1,2},{2,1},{3,4},{4,3},{5,6},{6,5},{7,15},{8,0},{9,10},{10,... | collective-permute-start | bytes 147464 | tf_op jit(solution)/shard_map/ppermute | solution.py:428
  18.8 1.0 %copy-start = (f32[1,7,1,8,1536]{4,3,2,1,0:T(8,128)S(1)}, f32[1,7,1,8,1536]{4,3,2,1,0:T(8,128)}, u32[]{:S(2)}) copy-start(f32[1,7,1,8,1536]{4,3,2,1,0:T(8,128)} %adj.1) | copy-start | bytes 1032196
  24.2 1.4 %collective-permute-start.4 = (f32[16,1536]{1,0:T(8,128)S(1)}, f32[16,1536]{1,0:T(8,128)S(1)}, u32[]{:S(2)}, u32[]{:S(2)}) collective-permute-start(f32[16,1536]{1,0:T(8,128)S(1)} %get-tuple-element.17), channel_id=1, source_target_pairs={{0,1},{1,0},{2,3},{3,2},{4,5},{5,4},{6,7},{7,6},{8,9},{9,8},{10,11... | collective-permute-start | bytes 294920 | tf_op jit(solution)/shard_map/ppermute | solution.py:428
  24.6 4.6 %collective-permute-start.5 = (f32[16,1536]{1,0:T(8,128)S(1)}, f32[16,1536]{1,0:T(8,128)S(1)}, u32[]{:S(2)}, u32[]{:S(2)}) collective-permute-start(f32[16,1536]{1,0:T(8,128)S(1)} %get-tuple-element.18), channel_id=1, source_target_pairs={{0,8},{1,2},{2,1},{3,4},{4,3},{5,6},{6,5},{7,15},{8,0},{9,10},{10,... | collective-permute-start | bytes 294920 | tf_op jit(solution)/shard_map/ppermute | solution.py:428

commit v3 on v2

--- a/solution.py
+++ b/solution.py
@@ -32,6 +32,17 @@
         term = lax.dot_general(part, onehot, dims, preferred_element_type=F32)
         total = term if total is None else total + term
     return total
+
+
+def joint_dot(x, onehot, count, dims):
+    rows = x.shape[0]
+    parts = [part.astype(F32) for part in parts_of(x, count)]
+    spare = -(rows * count) % 16
+    if spare:
+        parts.append(jnp.zeros((spare, x.shape[1]), F32))
+    joined = jnp.concatenate(parts, axis=0).astype(BF16)
+    out = lax.dot_general(joined, onehot, dims, preferred_element_type=F32)
+    return sum(out[k * rows : (k + 1) * rows] for k in range(1, count)) + out[:rows]
 
 
 def iota(shape, dim):
@@ -82,42 +93,35 @@
     mine = (iota((height, z.count), 0) == owner).astype(F32)
     earlier = (iota((z.count, z.count), 0) < iota((z.count, z.count), 1)).astype(F32)
     ranks = jnp.dot(mine.astype(BF16), earlier.astype(BF16), preferred_element_type=F32)
+
+    where = cell[0, 0]
+    weight = wt[0, 0]
+    mis = misfit[0, 0]
+    row = ((where.astype(F32) + 0.5) * (1.0 / z.cols)).astype(jnp.int32)
+    col = where - row * z.cols
+    full_row = owner * z.rows + row
+    edge_at = jnp.where(col == 0, full_row, jnp.where(col == z.cols - 1, z.total_rows + full_row, -1))
+    hits = jnp.concatenate(
+        [(iota((z.edge, z.count), 0) == edge_at[s : s + 1]).astype(F32) for s in range(POINTS)], axis=1
+    )
+    value = jnp.concatenate([mis[1:2] * weight[s : s + 1] for s in range(POINTS)], axis=1)
+    edge_force = joint_dot(value, hits.astype(BF16), 3, NT_DIMS)
+
     rank = jnp.sum(ranks * mine, axis=0, keepdims=True)
     place = owner * LANES + rank.astype(jnp.int32)
     spread = (iota((z.tiles * LANES, z.count), 0) == place).astype(F32).astype(BF16)
-
-    where = cell[0, 0]
-    row = ((where.astype(F32) + 0.5) * (1.0 / z.cols)).astype(jnp.int32)
-    col = where - row * z.cols
     code = ((col // LOW) * z.rows + row) * LOW + col % LOW
     code = code.astype(F32)
-    weight = wt[0, 0]
-    mis = misfit[0, 0]
     feats = []
     for g in range(z.spr):
         picked = [weight[h * z.spr + g : h * z.spr + g + 1] for h in range(z.npr)]
         picked += [code[h * z.spr + g : h * z.spr + g + 1] for h in range(z.npr)]
         picked.append(mis[g : g + 1] if g < TIMES else jnp.zeros((1, z.count), F32))
         feats += picked
-    used = len(feats)
-    padded = -(-used // 16) * 16
-    if padded > used:
-        feats.append(jnp.zeros((padded - used, z.count), F32))
-    boxed = split_dot(jnp.concatenate(feats, axis=0), spread, 3, NT_DIMS)
+    boxed = joint_dot(jnp.concatenate(feats, axis=0), spread, 3, NT_DIMS)
     slots = boxed[: z.feat_rows]
     for g in range(1, z.spr):
         slots = slots + rolled(boxed[g * z.feat_rows : (g + 1) * z.feat_rows], g * z.slots, 1)
-
-    full_row = owner * z.rows + row
-    edge_at = jnp.where(col == 0, full_row, jnp.where(col == z.cols - 1, z.total_rows + full_row, -1))
-    total = None
-    for s in range(POINTS):
-        value = mis[1:2] * weight[s : s + 1]
-        value = jnp.concatenate([value, jnp.zeros((15, z.count), F32)], axis=0)
-        hits = (iota((z.edge, z.count), 0) == edge_at[s : s + 1]).astype(F32).astype(BF16)
-        term = split_dot(value, hits, 3, NT_DIMS)
-        total = term if total is None else total + term
-    edge_force = total[:1]
 
     for n in order[4:]:
         copies[n].wait()
@@ -145,10 +149,8 @@
             pay[group * z.tiles + t] = part
 
     for f in range(z.fields):
-        s = adj[0, f, 0] * (cond[0, 0] * diffus[f])
-        mate[f : f + 1, :], next_[f : f + 1, :] = facing(s)
-    for ref in (mate, next_):
-        ref[z.fields :, :] = jnp.zeros((SUBL - z.fields, z.cols), F32)
+        mate[f : f + 1, :], next_[f : f + 1, :] = facing(adj[0, f, 0] * (cond[0, 0] * diffus[f]))
+    mate[z.fields :, :], next_[z.fields :, :] = facing(cond[0, 0])
 
 
 def even_tile():
@@ -218,43 +220,73 @@
     return total
 
 
-def line_of(ref, s, q):
-    return jnp.concatenate([ref[side, q : q + 1, :] for side in range(2)], axis=1) if s is None else ref[s, q : q + 1, :]
-
-
-def deposit(z, recv, panel, spread_a, spread_b):
+def line_of(ref, q):
+    return jnp.concatenate([ref[side, q : q + 1, :] for side in range(2)], axis=1)
+
+
+def observed(z, recv, panel):
     sources = z.rads * z.tiles
     base = panel * sources * z.block
     feat = [recv[pl.ds(base + k, sources, stride=z.block), :] for k in range(z.feat_rows)]
     lane = iota((sources, LANES), 1)
-    scaled = []
+    misfits = []
     for t in range(TIMES):
         mis = jnp.where(lane // z.slots == t, feat[2 * z.npr], 0.0)
         full = None
         for g in range(z.spr):
             term = rolled(mis, (g - t) * z.slots, 1)
             full = term if full is None else full + term
-        scaled.append(full)
-    sub_hi = iota((z.hi, LANES), 0)
-    sub_lo = iota((LOW, LANES), 0)
+        misfits.append(full)
+    return feat[: z.npr], [code.astype(jnp.int32) for code in feat[z.npr : 2 * z.npr]], misfits
+
+
+def dealt(z, values, highs, lows, height, spread_a, spread_b):
+    width = spread_b.shape[0]
+    sources = highs[0].shape[0]
+    sub_high = iota((height, LANES), 0)
+    sub_low = iota((width, LANES), 0)
     for h in range(z.npr):
-        code = feat[z.npr + h].astype(jnp.int32)
-        high, low = code // LOW, code % LOW
         parts = []
-        for t in range(TIMES):
-            parts += [p.astype(F32) for p in parts_of(scaled[t] * feat[h], 2)]
+        for value in values[h]:
+            parts += [part.astype(F32) for part in parts_of(value, 2)]
         for n in range(sources):
             at = (n * z.npr + h) * LANES
-            hit = sub_hi == high[n : n + 1]
+            hit = sub_high == highs[h][n : n + 1]
             for k, part in enumerate(parts):
-                spread_a[k * z.hi : (k + 1) * z.hi, at : at + LANES] = jnp.where(hit, part[n : n + 1], 0.0).astype(BF16)
-            spread_b[:, at : at + LANES] = (sub_lo == low[n : n + 1]).astype(F32).astype(BF16)
+                spread_a[k * height : (k + 1) * height, at : at + LANES] = jnp.where(hit, part[n : n + 1], 0.0).astype(BF16)
+            spread_b[:, at : at + LANES] = (sub_low == lows[h][n : n + 1]).astype(F32).astype(BF16)
     grid = lax.dot_general(spread_a[...], spread_b[...], NT_DIMS, preferred_element_type=F32)
+    return [
+        grid[2 * k * height : (2 * k + 1) * height] + grid[(2 * k + 1) * height : (2 * k + 2) * height]
+        for k in range(len(values[0]))
+    ]
+
+
+def deposit(z, recv, panel, spread_a, spread_b):
+    weights, codes, misfits = observed(z, recv, panel)
+    values = [[mis * weight for mis in misfits] for weight in weights]
+    highs = [code // LOW for code in codes]
+    lows = [code % LOW for code in codes]
     out = []
-    for t in range(TIMES):
-        both = grid[2 * t * z.hi : (2 * t + 1) * z.hi] + grid[(2 * t + 1) * z.hi : (2 * t + 2) * z.hi]
+    for both in dealt(z, values, highs, lows, z.hi, spread_a, spread_b):
         out.append(jnp.concatenate([both[k * z.rows : (k + 1) * z.rows] for k in range(z.cols // LOW)], axis=1))
     return out
+
+
+def deposit_ends(z, recv, panel, spread_a, spread_b):
+    weights, codes, misfits = observed(z, recv, panel)
+    values = [[misfits[1] * weight] for weight in weights]
+    chunks = z.cols // LANES
+    highs, lows = [], []
+    for code in codes:
+        row = (code // LOW) % z.rows
+        chunk = (code // LOW) // z.rows * (LOW // LANES) + (code % LOW) // LANES
+        end = jnp.where(row == z.rows - 1, chunk + chunks, -1)
+        highs.append(jnp.where(row == 0, chunk, end))
+        lows.append(code % LANES)
+    (both,) = dealt(z, values, highs, lows, 2 * chunks, spread_a, spread_b)
+    ends = [[both[e * chunks + k : e * chunks + k + 1] for k in range(chunks)] for e in range(2)]
+    return [jnp.concatenate(end, axis=1) for end in ends]
 
 
 def sideways(s):
@@ -273,17 +305,66 @@
     return north + south
 
 
-def first_kernel(z, adj, cond, *refs):
+def early_kernel(z, adj, cond, *refs):
     if z.pair:
-        adj2, cond2, *refs = refs
+        adj2, cond2, diffus, couple, out, mate, next_, own, far = refs
     else:
-        beside, *refs = refs
-    mate_in, next_in, recv, diffus, couple, grow, gcol, gwt, *refs = refs
-    first, base, mate, next_, spread_a, spread_b = refs
-    above, below = around(z, mate_in[...], next_in[...])
+        beside, diffus, couple, out, mate, next_, own = refs
+    own_c = cond[0, 0]
+    far_c = cond2[0, 0] if z.pair else None
+    for f in range(z.fields):
+        s = adj[0, f, 0] * (own_c * diffus[f])
+        new = adj[0, f, 0] - 6.0 * s + sideways(s) + upright(s, 0.0, 0.0)
+        new = new + coupled(z, couple, lambda e: adj[0, e, 0], f)
+        if z.pair:
+            other = adj2[0, f, 0] * (far_c * diffus[f])
+            new = new + other
+            part = adj2[0, f, 0] - 6.0 * other + sideways(other) + upright(other, 0.0, 0.0) + s
+            far[f] = part + coupled(z, couple, lambda e: adj2[0, e, 0], f)
+            at = SUBL + f
+            mate[at : at + 1, :], next_[at : at + 1, :] = facing(other)
+        else:
+            new = new + beside[f]
+        own[f] = new
+        mate[f : f + 1, :], next_[f : f + 1, :] = facing(new * (own_c * diffus[f]))
+    for half in range(2 if z.pair else 1):
+        for ref in (mate, next_):
+            ref[half * SUBL + z.fields : (half + 1) * SUBL, :] = jnp.zeros((SUBL - z.fields, z.cols), F32)
+    for f in range(z.fields):
+        s = own[f] * (own_c * diffus[f])
+        new = own[f] - 6.0 * s + sideways(s) + upright(s, 0.0, 0.0)
+        new = new + coupled(z, couple, lambda e: own[e], f)
+        if z.pair:
+            new = new + far[f] * (far_c * diffus[f])
+        out[f] = new
+
+
+def ends_kernel(z, recv, cond, diffus, mate_row, next_row, mate_in, next_in, mate, next_, spread_a, spread_b):
+    panel, rad, tile = lax.axis_index("panel"), lax.axis_index("rad"), lax.axis_index("ang")
+    outer = jnp.where(rad == z.rads - 1, 1.0, 0.0)
+    inner = jnp.where((tile == 0) | (tile == z.tiles - 1), 0.0, 1.0)
+    top, bottom = deposit_ends(z, recv, panel, spread_a, spread_b)
+    even = even_tile()
+    to_mate = jnp.where(even, bottom, top) * outer
+    to_next = jnp.where(even, top, bottom) * outer
+    cond_mate, cond_next = facing(cond[0, 0])
+    for f in range(z.fields):
+        from_mate, from_next = mate_row[f : f + 1, :], next_row[f : f + 1, :] * inner
+        if f == 3:
+            from_mate, from_next = from_mate + to_mate, from_next + to_next
+        mate[f : f + 1, :] = mate_in[f : f + 1, :] + from_mate * (cond_mate * diffus[f])
+        next_[f : f + 1, :] = next_in[f : f + 1, :] + from_next * (cond_next * diffus[f])
+
+
+def ghost_kernel(z, early, recv, cond, *refs):
+    if z.pair:
+        cond2, mate_in, next_in, diffus, couple, grow, gcol, gwt, out, added, spread_a, spread_b = refs
+    else:
+        mate_in, next_in, diffus, couple, grow, gcol, gwt, out, added, spread_a, spread_b = refs
     panel, rad, tile = lax.axis_index("panel"), lax.axis_index("rad"), lax.axis_index("ang")
     other = 1 - panel
     outer = jnp.where(rad == z.rads - 1, 1.0, 0.0)
+    above, below = around(z, mate_in[...], next_in[...])
 
     sets = [(other, rad), (panel, rad)]
     if z.pair:
@@ -307,9 +388,9 @@
     rows = [coupled(z, couple, lambda e: rim[e : e + 1], c) for c in range(z.fields)]
     mixed = jnp.concatenate(rows + [jnp.zeros((SUBL - z.fields, z.edge), F32)], axis=0)
 
-    g_row = [line_of(grow, None, q) for q in range(z.stencil)]
-    g_col = [line_of(gcol, None, q) for q in range(z.stencil)]
-    g_wt = [line_of(gwt, None, q) for q in range(z.stencil)]
+    g_row = [line_of(grow, q) for q in range(z.stencil)]
+    g_col = [line_of(gcol, q) for q in range(z.stencil)]
+    g_wt = [line_of(gwt, q) for q in range(z.stencil)]
     rim_ghost = None
     for q in range(z.stencil):
         target = jnp.where(
@@ -320,13 +401,13 @@
         term = split_dot(values, hits, 3, NT_DIMS)
         rim_ghost = term if rim_ghost is None else rim_ghost + term
     sources = z.rads * z.tiles
-    force = []
+    pulse = []
     for k in range(z.edge_rows):
         at = other * sources * z.block + z.feat_rows + k
-        force.append(jnp.sum(recv[pl.ds(at, sources, stride=z.block), :], axis=0, keepdims=True))
-    force = jnp.concatenate(force, axis=1) * outer
+        pulse.append(jnp.sum(recv[pl.ds(at, sources, stride=z.block), :], axis=0, keepdims=True))
+    pulse = jnp.concatenate(pulse, axis=1) * outer
     rim_first = rim + lap + mixed + rim_ghost[:SUBL]
-    rim_first = rim_first + jnp.where(iota((SUBL, z.edge), 0) == 3, force, 0.0)
+    rim_first = rim_first + jnp.where(iota((SUBL, z.edge), 0) == 3, pulse, 0.0)
     rim_second = rim_first * rim[z.fields : z.fields + 1] * dif
 
     row0 = tile * z.rows
@@ -336,7 +417,11 @@
     for load in loads:
         for f in range(z.fields):
             stacked.append(jnp.concatenate([load[f : f + 1] * aimed[q] for q in range(z.stencil)], axis=1))
-    height = len(stacked) * z.rows
+    for row in (row0 - 1, row0 + z.rows):
+        stacked.append(
+            jnp.concatenate([rim_s * jnp.where(g_row[q] == row, g_wt[q], 0.0) for q in range(z.stencil)], axis=1)
+        )
+    height = len(loads) * z.fields * z.rows + 2 * SUBL
     if height % 16:
         stacked.append(jnp.zeros((16 - height % 16, z.stencil * z.edge), F32))
     stacked = jnp.concatenate(stacked, axis=0)
@@ -348,59 +433,48 @@
         at = (step * z.fields + f) * z.rows
         return ghost[at : at + z.rows]
 
-    force0, force1 = deposit(z, recv, panel, spread_a, spread_b)
-
+    force = deposit(z, recv, panel, spread_a, spread_b)
+    at = len(loads) * z.fields * z.rows
+    ghost_above, ghost_below = ghost[at : at + SUBL], ghost[at + SUBL : at + 2 * SUBL]
     own_c = cond[0, 0]
-    far_c = cond2[0, 0] if z.pair else None
-    for f in range(z.fields):
-        s = adj[0, f, 0] * (own_c * diffus[f])
-        new = adj[0, f, 0] - 6.0 * s + sideways(s) + upright(s, above[f : f + 1], below[f : f + 1])
-        new = new + coupled(z, couple, lambda e: adj[0, e, 0], f) + ghost_of(0, f)
-        second = ghost_of(1, f)
+    for f in range(z.fields):
+        new = ghost_of(0, f) + brim(above[f : f + 1], below[f : f + 1], z.rows)
+        added[f] = new + force[1] * outer if f == 3 else new
+    for f in range(z.fields):
+        s = added[f] * (own_c * diffus[f])
+        high = ghost_above[f : f + 1] * (above[z.fields :] * diffus[f])
+        low = ghost_below[f : f + 1] * (below[z.fields :] * diffus[f])
+        new = early[f] + added[f] - 6.0 * s + sideways(s) + upright(s, high, low)
+        new = new + coupled(z, couple, lambda e: added[e], f) + ghost_of(1, f)
         if z.pair:
-            far = adj2[0, f, 0] * (far_c * diffus[f])
-            new = new + far
-            part = adj2[0, f, 0] - 6.0 * far + sideways(far) + upright(far, 0.0, 0.0) + s
-            part = part + coupled(z, couple, lambda e: adj2[0, e, 0], f) + ghost_of(2, f)
+            part = ghost_of(2, f)
             if f == 3:
-                part = part + force1 * (1.0 - outer)
-            second = second + part * (far_c * diffus[f])
-            at = SUBL + f
-            mate[at : at + 1, :], next_[at : at + 1, :] = facing(far)
-        else:
-            new = new + beside[f]
+                part = part + force[1] * (1.0 - outer)
+            new = new + part * (cond2[0, 0] * diffus[f])
         if f == 3:
-            new = new + force1 * outer
-            second = second + force0 * outer
-        first[f] = new
-        base[f] = second
-        s = new * (own_c * diffus[f])
-        mate[f : f + 1, :], next_[f : f + 1, :] = facing(s)
-    for half in range(2 if z.pair else 1):
-        for ref in (mate, next_):
-            ref[half * SUBL + z.fields : (half + 1) * SUBL, :] = jnp.zeros((SUBL - z.fields, z.cols), F32)
-
-
-def second_kernel(z, first, base, cond, *refs):
+            new = new + force[0] * outer
+        out[f] = new
+
+
+def brim(high, low, rows):
+    sub = iota((rows, high.shape[1]), 0)
+    return jnp.where(sub == 0, high, 0.0) + jnp.where(sub == rows - 1, low, 0.0)
+
+
+def last_kernel(z, late, *refs):
     if z.pair:
-        cond2, *refs = refs
+        cond2, mate_in, next_in, diffus, out = refs
     else:
-        beside, *refs = refs
-    mate_in, next_in, diffus, couple, out = refs
+        beside, mate_in, next_in, diffus, out = refs
     above, below = around(z, mate_in[...], next_in[...])
-    own_c = cond[0, 0]
-    for f in range(z.fields):
-        s = first[f] * (own_c * diffus[f])
-        new = first[f] - 6.0 * s + sideways(s) + base[f]
+    for f in range(z.fields):
         high, low = above[f : f + 1], below[f : f + 1]
         if z.pair:
             far_c = cond2[0, 0]
             high = high + above[SUBL + f : SUBL + f + 1] * (far_c[:1] * diffus[f])
             low = low + below[SUBL + f : SUBL + f + 1] * (far_c[z.rows - 1 :] * diffus[f])
-        else:
-            new = new + beside[f]
-        new = new + upright(s, high, low)
-        out[0, f, 0] = new + coupled(z, couple, lambda e: first[e], f)
+        new = late[f] + brim(high, low, z.rows)
+        out[0, f, 0] = new if z.pair else new + beside[f]
 
 
 def shifted(x, axis, step):
@@ -428,17 +502,18 @@
     return lax.ppermute(mate, axes, pairs), lax.ppermute(next_, axes, links)
 
 
-def call(kernel, shapes, scratch, args, scalars=(), spaces=None, room=48):
+def call(kernel, shapes, scratch, args, scalars=(), spaces=None, room=48, aliases=None):
     specs = [
         pl.BlockSpec(memory_space=spaces or (pltpu.SMEM if n in scalars else pltpu.VMEM))
         for n in range(len(args))
     ]
     return pl.pallas_call(
         kernel,
-        out_shape=[jax.ShapeDtypeStruct(shape, F32) for shape in shapes],
+        out_shape=[x if isinstance(x, jax.ShapeDtypeStruct) else jax.ShapeDtypeStruct(x, F32) for x in shapes],
         in_specs=specs,
         out_specs=[pl.BlockSpec(memory_space=pltpu.VMEM)] * len(shapes),
         scratch_shapes=scratch,
+        input_output_aliases=aliases or {},
         compiler_params=pltpu.CompilerParams(vmem_limit_bytes=room << 20),
     )(*args)
 
@@ -446,45 +521,61 @@
 def body(adj, cond, diffus, couple, ghost_row, ghost_col, ghost_wt, obs_dest, obs_cell, obs_wt, misfit):
     z = Sizes(adj, obs_cell, ghost_row)
     state = (z.fields, z.rows, z.cols)
+    line, lines = (SUBL, z.cols), (SUBL * (2 if z.pair else 1), z.cols)
     if z.pair:
         swap = [(0, 1), (1, 0)]
-        adj2 = lax.ppermute(adj, "rad", swap)
-        cond2 = lax.ppermute(cond, "rad", swap)
+        beside = [lax.ppermute(adj, "rad", swap), lax.ppermute(cond, "rad", swap)]
     else:
-        scaled = diffus[:, None, None] * cond[0, 0][None] * adj[0, :, 0]
-        beside = both_sides(scaled, "rad")
+        coeff = diffus[:, None, None] * cond[0, 0][None]
+        beside = [both_sides(coeff * adj[0, :, 0], "rad")]
+    far = beside[1:]
+
     given = [adj, cond, diffus, obs_dest.reshape(1, z.count), obs_cell, obs_wt, misfit]
     held = [pltpu.SMEM(x.shape, x.dtype) if x is diffus else pltpu.VMEM(x.shape, x.dtype) for x in given]
-    pay, mate, next_ = call(
+    pay, *rows = call(
         functools.partial(pack_kernel, z),
-        [(z.devices, z.block, LANES), (SUBL, z.cols), (SUBL, z.cols)],
+        [(z.devices, z.block, LANES), line, line],
         held + [pltpu.SemaphoreType.DMA((len(given),))],
         given,
         spaces=pltpu.HBM,
         room=64,
     )
     recv = lax.all_to_all(pay, ("panel", "rad", "ang"), split_axis=0, concat_axis=0, tiled=True)
-    mate, next_ = beside_rows(z, mate, next_)
+    recv = recv.reshape(z.devices * z.block, LANES)
+    rows = list(beside_rows(z, *rows))
+
+    args = [adj, cond] + beside + [diffus, couple]
+    early, mate, next_, *first = call(
+        functools.partial(early_kernel, z),
+        [state, lines, lines] + ([] if z.pair else [state]),
+        [pltpu.VMEM(state, F32)] * (2 if z.pair else 0),
+        args,
+        (len(args) - 2, len(args) - 1),
+    )
     points = z.rads * z.tiles * z.npr * LANES
-    lines = (SUBL * (2 if z.pair else 1), z.cols)
-    args = [adj, cond] + ([adj2, cond2] if z.pair else [beside])
-    args += [mate, next_, recv.reshape(z.devices * z.block, LANES), diffus, couple]
-    scalars = (len(args) - 2, len(args) - 1)
-    first, base, mate, next_ = call(
-        functools.partial(first_kernel, z),
-        [state, state, lines, lines],
-        [pltpu.VMEM((2 * TIMES * z.hi, points), BF16), pltpu.VMEM((LOW, points), BF16)],
-        args + [ghost_row, ghost_col, ghost_wt],
-        scalars,
+    ends = 2 * z.cols // LANES
+    mate, next_ = call(
+        functools.partial(ends_kernel, z),
+        [lines, lines],
+        [pltpu.VMEM((2 * ends, points), BF16), pltpu.VMEM((LANES, points), BF16)],
+        [recv, cond, diffus] + rows + [mate, next_],
+        (2,),
+        aliases={5: 0, 6: 1},
     )
     mate, next_ = beside_rows(z, mate, next_)
-    if z.pair:
-        args = [first, base, cond, cond2]
-    else:
-        scaled = diffus[:, None, None] * cond[0, 0][None] * first
-        args = [first, base, cond, both_sides(scaled, "rad")]
-    args += [mate, next_, diffus, couple]
-    (out,) = call(functools.partial(second_kernel, z), [adj.shape], [], args, (6, 7))
+    args = [early, recv, cond] + far + rows + [diffus, couple]
+    late, *added = call(
+        functools.partial(ghost_kernel, z),
+        [state] if z.pair else [state, state],
+        ([pltpu.VMEM(state, F32)] if z.pair else [])
+        + [pltpu.VMEM((2 * TIMES * z.hi, points), BF16), pltpu.VMEM((LOW, points), BF16)],
+        args + [ghost_row, ghost_col, ghost_wt],
+        (len(args) - 2, len(args) - 1),
+    )
+    if not z.pair:
+        far = [both_sides(coeff * (first[0] + added[0]), "rad")]
+    args = [late] + far + [mate, next_, diffus]
+    (out,) = call(functools.partial(last_kernel, z), [adj.shape], [], args, (len(args) - 1,))
     return out
 
 

time: 31.4 us -> 26.5 us (0.84)
  waiting for transfers between devices: 10 us -> 2.8 us
  Pallas kernels: 8.89 us -> 10.9 us
  starting transfers between devices: 11 us -> 11.4 us
    ppermute x4, waiting for transfers between devices: 5.83 us -> 0.01 us  [beside_rows(): return (lax.ppermute(mate, axes, pairs), lax.ppermute(next_, axes, links))]
    pallas_call x3 -> x5, Pallas kernels: 8.89 us -> 10.9 us  [call(): pl.pallas_call(kernel, out_shape=[x if isinstance(x, jax.ShapeDtypeStruct...]
    all_to_all x1, waiting for transfers between devices: 2.02 us -> 0.58 us  [body(): lax.all_to_all(pay, ('panel', 'rad', 'ang'), split_axis=0, concat_axis=0,...]
    ppermute x4, starting transfers between devices: 1.27 us -> 1.73 us  [beside_rows(): return (lax.ppermute(mate, axes, pairs), lax.ppermute(next_, axes, links))]
  transfers between devices with their start and end apart: 7 -> 7, of which waited for: 5 -> 2; matrix products, arithmetic and copies ran while one was open for 0% -> 0% of each run, Pallas kernels for 8% -> 31%
where the time goes in v3:
time: 26.5 us; the launch traced here: 26.3 us
  starting transfers between devices  11.4 us (43%)
  Pallas kernels  10.9 us (41%)
  waiting for transfers between devices  2.8 us (11%)
  local copies, waits for them, and re-layouts  1.01 us (4%)
    pallas_call x5, Pallas kernels, call(): pl.pallas_call(kernel, out_shape=[x if isinstance(x, jax.ShapeDtypeStruct...  10.9 us
    all_to_all x1, starting transfers between devices, body(): lax.all_to_all(pay, ('panel', 'rad', 'ang'), split_axis=0, concat_axis=0,...  4.9 us
    ppermute x2, starting transfers between devices, body(): beside = [lax.ppermute(adj, 'rad', swap), lax.ppermute(cond, 'rad', swap)]  4.8 us
    ppermute x2, waiting for transfers between devices, body(): beside = [lax.ppermute(adj, 'rad', swap), lax.ppermute(cond, 'rad', swap)]  2.21 us
    ppermute x4, starting transfers between devices, beside_rows(): return (lax.ppermute(mate, axes, pairs), lax.ppermute(next_, axes, links))  1.73 us
    unnamed x18, local copies, waits for them, and re-layouts  1.01 us
    all_to_all x1, waiting for transfers between devices, body(): lax.all_to_all(pay, ('panel', 'rad', 'ang'), split_axis=0, concat_axis=0,...  0.58 us
  transfers between devices with their start and end apart: 7, of which 2 were waited for; matrix products, arithmetic and copies ran while one was open for 0% of the time, Pallas kernels for 31%

profile of v3, /device:TPU:0, one launch (start us, length us, event | category | flops | bytes accessed | tf_op | source)
XLA Modules:
  0.0 26.3 jit_solution(4264691653831337917)
XLA Ops:
  0.0 3.0 %collective-permute-start = (f32[1,7,1,8,1536]{4,3,2,1,0:T(8,128)}, f32[1,7,1,8,1536]{4,3,2,1,0:T(8,128)}, u32[]{:S(2)}, u32[]{:S(2)}) collective-permute-start(f32[1,7,1,8,1536]{4,3,2,1,0:T(8,128)} %refs_0_.1), channel_id=1, source_target_pairs={{0,8},{8,0},{1,9},{9,1},{2,10},{10,2},{3,11},{11,3},{4,12},{12,4},... | collective-permute-start | bytes 1032200 | tf_op jit(solution)/shard_map/ppermute | solution.py:527
  3.0 2.2 %shard_map.110 = (f32[32,8,128]{2,1,0:T(8,128)}, f32[8,1536]{1,0:T(8,128)}, f32[8,1536]{1,0:T(8,128)}) custom-call(f32[1,7,1,8,1536]{4,3,2,1,0:T(8,128)} %refs_0_.1, f32[1,1,8,1536]{3,2,1,0:T(8,128)} %cond.5, f32[7]{0:T(128)} %refs_3_.5, s32[1,256]{1,0:T(1,128)} %bitcast.4, s32[1,1,4,256]{3,2,1,0:T(4,128)} %refs_4_.2, f32[1,1,4,256]{3,2,1,0:T(4,128)} %refs_5_.2, ...), custom_call_target="tpu_custom_call" | custom-call | tf_op jit(solution)/shard_map/pallas_call | solution.py:510
  5.2 0.0 copy-start.1
  5.2 0.0 copy-start.8
  5.2 0.0 copy-start.7
  5.2 0.0 copy-start.2
  5.2 4.9 %all-to-all-start = ((f32[32,8,128]{2,1,0:T(8,128)}), f32[32,8,128]{2,1,0:T(8,128)S(1)}, u32[]{:S(2)}, u32[]{:S(2)}) async-start(f32[32,8,128]{2,1,0:T(8,128)} %get-tuple-element.14), calls=%async_computation | async-start | bytes 262144 | tf_op jit(solution)/shard_map/all_to_all | solution.py:543
  10.1 0.0 copy-done.1
  10.1 1.8 %collective-permute-start.1 = (f32[1,1,8,1536]{3,2,1,0:T(8,128)S(1)}, f32[1,1,8,1536]{3,2,1,0:T(8,128)S(1)}, u32[]{:S(2)}, u32[]{:S(2)}) collective-permute-start(f32[1,1,8,1536]{3,2,1,0:T(8,128)S(1)} %copy-done.1), channel_id=1, source_target_pairs={{0,8},{8,0},{1,9},{9,1},{2,10},{10,2},{3,11},{11,3},{4,12},{12,4},... | collective-permute-start | bytes 147464 | tf_op jit(solution)/shard_map/ppermute | solution.py:527
  12.0 0.0 copy-done.8
  12.0 0.0 copy-start.3
  12.0 0.0 collective-permute-start.2
  12.0 0.0 copy-done.7
  12.0 0.3 %collective-permute-start.3 = (f32[8,1536]{1,0:T(8,128)S(1)}, f32[8,1536]{1,0:T(8,128)S(1)}, u32[]{:S(2)}, u32[]{:S(2)}) collective-permute-start(f32[8,1536]{1,0:T(8,128)S(1)} %copy-done.7), channel_id=1, source_target_pairs={{0,8},{1,2},{2,1},{3,4},{4,3},{5,6},{6,5},{7,15},{8,0},{9,10},{10,... | collective-permute-start | bytes 147464 | tf_op jit(solution)/shard_map/ppermute | solution.py:502
  12.3 2.2 %collective-permute-done.1.refs_1_.refs_0_ = f32[1,1,8,1536]{3,2,1,0:T(8,128)S(1)} collective-permute-done((f32[1,1,8,1536]{3,2,1,0:T(8,128)S(1)}, f32[1,1,8,1536]{3,2,1,0:T(8,128)S(1)}, u32[]{:S(2)}, u32[]{:S(2)}) %collective-permute-start.1) | collective-permute-done | bytes 49184 | tf_op jit(solution)/shard_map/ppermute | solution.py:527
  14.5 0.0 collective-permute-done.refs_0_
  14.5 0.0 copy-done.2
  14.5 0.0 copy-done.3
  14.5 0.0 copy-start
  14.5 1.0 %copy-done = f32[1,7,1,8,1536]{4,3,2,1,0:T(8,128)S(1)} copy-done((f32[1,7,1,8,1536]{4,3,2,1,0:T(8,128)S(1)}, f32[1,7,1,8,1536]{4,3,2,1,0:T(8,128)}, u32[]{:S(2)}) %copy-start) | copy-done | bytes 344088
  15.5 2.2 %shard_map.109 = (f32[7,8,1536]{2,1,0:T(8,128)S(1)}, f32[16,1536]{1,0:T(8,128)S(1)}, f32[16,1536]{1,0:T(8,128)S(1)}) custom-call(f32[1,7,1,8,1536]{4,3,2,1,0:T(8,128)S(1)} %copy-done, f32[1,1,8,1536]{3,2,1,0:T(8,128)S(1)} %copy-done.1, f32[1,7,1,8,1536]{4,3,2,1,0:T(8,128)} %collective-permute-done.refs_0_, ...), custom_call_target="tpu_custom_call" | custom-call | tf_op jit(solution)/shard_map/pallas_call | solution.py:510
  17.7 0.0 collective-permute-done.2.refs_1_.mate_row
  17.7 0.0 collective-permute-done.3.refs_2_.next_row
  17.7 0.6 %all-to-all-done = f32[32,8,128]{2,1,0:T(8,128)S(1)} async-done(((f32[32,8,128]{2,1,0:T(8,128)}), f32[32,8,128]{2,1,0:T(8,128)S(1)}, u32[]{:S(2)}, u32[]{:S(2)}) %all-to-all-start) | async-done | bytes 131104 | tf_op jit(solution)/shard_map/all_to_all | solution.py:543
  18.3 0.0 copy-start.5
  18.3 0.0 copy-start.6
  18.3 1.4 %shard_map.112 = (f32[16,1536]{1,0:T(8,128)S(1)}, f32[16,1536]{1,0:T(8,128)S(1)}) custom-call(f32[256,128]{1,0:T(8,128)S(1)} %bitcast.2, f32[1,1,8,1536]{3,2,1,0:T(8,128)S(1)} %copy-done.1, f32[7]{0:T(128)S(1)} %copy-done.3, f32[8,1536]{1,0:T(8,128)S(1)} %collective-permute-done.2.refs_1_.mate_row, ...), custom_call_target="tpu_custom_call", output_to_operand_aliasing={{0}: (5, {}), {1}: (6, {})} | custom-call | tf_op jit(solution)/shard_map/pallas_call | solution.py:510
  19.7 0.0 copy-start.4
  19.7 0.4 %collective-permute-start.4 = (f32[16,1536]{1,0:T(8,128)S(1)}, f32[16,1536]{1,0:T(8,128)S(1)}, u32[]{:S(2)}, u32[]{:S(2)}) collective-permute-start(f32[16,1536]{1,0:T(8,128)S(1)} %get-tuple-element.19), channel_id=1, source_target_pairs={{0,1},{1,0},{2,3},{3,2},{4,5},{5,4},{6,7},{7,6},{8,9},{9,8},{10,11... | collective-permute-start | bytes 294920 | tf_op jit(solution)/shard_map/ppermute | solution.py:502
  20.1 1.0 %collective-permute-start.5 = (f32[16,1536]{1,0:T(8,128)S(1)}, f32[16,1536]{1,0:T(8,128)S(1)}, u32[]{:S(2)}, u32[]{:S(2)}) collective-permute-start(f32[16,1536]{1,0:T(8,128)S(1)} %get-tuple-element.20), channel_id=1, source_target_pairs={{0,8},{1,2},{2,1},{3,4},{4,3},{5,6},{6,5},{7,15},{8,0},{9,10},{10,... | collective-permute-start | bytes 294920 | tf_op jit(solution)/shard_map/ppermute | solution.py:502
  21.1 0.0 copy-done.5
  21.1 0.0 copy-done.6
  21.1 0.0 copy-done.4
  21.1 3.7 %shard_map.111.late = f32[7,8,1536]{2,1,0:T(8,128)S(1)} custom-call(f32[7,8,1536]{2,1,0:T(8,128)S(1)} %get-tuple-element.13.early, f32[256,128]{1,0:T(8,128)S(1)} %bitcast.3, f32[1,1,8,1536]{3,2,1,0:T(8,128)S(1)} %copy-done.1, f32[1,1,8,1536]{3,2,1,0:T(8,128)S(1)} %collective-permute-done.1.refs_1_.refs_0_, ...), custom_call_target="tpu_custom_call" | custom-call | tf_op jit(solution)/shard_map/pallas_call | solution.py:510
  24.8 0.0 collective-permute-done.4.refs_1_
  24.8 0.0 collective-permute-done.5.refs_2_
  24.8 1.4 %shard_map.113 = f32[1,7,1,8,1536]{4,3,2,1,0:T(8,128)} custom-call(f32[7,8,1536]{2,1,0:T(8,128)S(1)} %shard_map.111.late, f32[1,1,8,1536]{3,2,1,0:T(8,128)S(1)} %collective-permute-done.1.refs_1_.refs_0_, f32[16,1536]{1,0:T(8,128)S(1)} %collective-permute-done.4.refs_1_, f32[16,1536]{1,0:T(8,128)S(1)} %collective-permute-done.5.refs_2_, f32[7]{0:T(128)S(1)} %copy-done.3), custom_call_target="tpu_custom_call" | custom-call | tf_op jit(solution)/shard_map/pallas_call | solution.py:510
Async XLA Ops:
  0.0 14.5 %collective-permute-start = (f32[1,7,1,8,1536]{4,3,2,1,0:T(8,128)}, f32[1,7,1,8,1536]{4,3,2,1,0:T(8,128)}, u32[]{:S(2)}, u32[]{:S(2)}) collective-permute-start(f32[1,7,1,8,1536]{4,3,2,1,0:T(8,128)} %refs_0_.1), channel_id=1, source_target_pairs={{0,8},{8,0},{1,9},{9,1},{2,10},{10,2},{3,11},{11,3},{4,12},{12,4},... | collective-permute-start | bytes 1032200 | tf_op jit(solution)/shard_map/ppermute | solution.py:527
  5.2 5.0 %copy-start.1 = (f32[1,1,8,1536]{3,2,1,0:T(8,128)S(1)}, f32[1,1,8,1536]{3,2,1,0:T(8,128)}, u32[]{:S(2)}) copy-start(f32[1,1,8,1536]{3,2,1,0:T(8,128)} %cond.5) | copy-start | bytes 147460
  5.2 6.8 %copy-start.8 = (f32[8,1536]{1,0:T(8,128)S(1)}, f32[8,1536]{1,0:T(8,128)}, u32[]{:S(2)}) copy-start(f32[8,1536]{1,0:T(8,128)} %get-tuple-element.15) | copy-start | bytes 147460
  5.2 6.8 %copy-start.7 = (f32[8,1536]{1,0:T(8,128)S(1)}, f32[8,1536]{1,0:T(8,128)}, u32[]{:S(2)}) copy-start(f32[8,1536]{1,0:T(8,128)} %get-tuple-element.16) | copy-start | bytes 147460
  5.2 9.3 %copy-start.2 = (f32[7,7]{1,0:T(8,128)S(1)}, f32[7,7]{1,0:T(8,128)}, u32[]{:S(2)}) copy-start(f32[7,7]{1,0:T(8,128)} %refs_4_.3) | copy-start | bytes 592
  5.2 13.1 %all-to-all-start = ((f32[32,8,128]{2,1,0:T(8,128)}), f32[32,8,128]{2,1,0:T(8,128)S(1)}, u32[]{:S(2)}, u32[]{:S(2)}) async-start(f32[32,8,128]{2,1,0:T(8,128)} %get-tuple-element.14), calls=%async_computation | async-start | bytes 262144 | tf_op jit(solution)/shard_map/all_to_all | solution.py:543
  10.1 4.4 %collective-permute-start.1 = (f32[1,1,8,1536]{3,2,1,0:T(8,128)S(1)}, f32[1,1,8,1536]{3,2,1,0:T(8,128)S(1)}, u32[]{:S(2)}, u32[]{:S(2)}) collective-permute-start(f32[1,1,8,1536]{3,2,1,0:T(8,128)S(1)} %copy-done.1), channel_id=1, source_target_pairs={{0,8},{8,0},{1,9},{9,1},{2,10},{10,2},{3,11},{11,3},{4,12},{12,4},... | collective-permute-start | bytes 147464 | tf_op jit(solution)/shard_map/ppermute | solution.py:527
  12.0 2.5 %copy-start.3 = (f32[7]{0:T(128)S(1)}, f32[7]{0:T(128)}, u32[]{:S(2)}) copy-start(f32[7]{0:T(128)} %refs_3_.5) | copy-start | bytes 88
  12.0 5.7 %collective-permute-start.2 = (f32[8,1536]{1,0:T(8,128)S(1)}, f32[8,1536]{1,0:T(8,128)S(1)}, u32[]{:S(2)}, u32[]{:S(2)}) collective-permute-start(f32[8,1536]{1,0:T(8,128)S(1)} %copy-done.8), channel_id=1, source_target_pairs={{0,1},{1,0},{2,3},{3,2},{4,5},{5,4},{6,7},{7,6},{8,9},{9,8},{10,11... | collective-permute-start | bytes 147464 | tf_op jit(solution)/shard_map/ppermute | solution.py:502
  12.0 5.7 %collective-permute-start.3 = (f32[8,1536]{1,0:T(8,128)S(1)}, f32[8,1536]{1,0:T(8,128)S(1)}, u32[]{:S(2)}, u32[]{:S(2)}) collective-permute-start(f32[8,1536]{1,0:T(8,128)S(1)} %copy-done.7), channel_id=1, source_target_pairs={{0,8},{1,2},{2,1},{3,4},{4,3},{5,6},{6,5},{7,15},{8,0},{9,10},{10,... | collective-permute-start | bytes 147464 | tf_op jit(solution)/shard_map/ppermute | solution.py:502
  14.5 1.0 %copy-start = (f32[1,7,1,8,1536]{4,3,2,1,0:T(8,128)S(1)}, f32[1,7,1,8,1536]{4,3,2,1,0:T(8,128)}, u32[]{:S(2)}) copy-start(f32[1,7,1,8,1536]{4,3,2,1,0:T(8,128)} %refs_0_.1) | copy-start | bytes 1032196
  18.3 2.8 %copy-start.5 = (s32[2,4,64]{2,1,0:T(4,128)S(1)}, s32[2,4,64]{2,1,0:T(4,128)}, u32[]{:S(2)}) copy-start(s32[2,4,64]{2,1,0:T(4,128)} %refs_6_.3) | copy-start | bytes 6148
  18.3 2.8 %copy-start.6 = (f32[2,4,64]{2,1,0:T(4,128)S(1)}, f32[2,4,64]{2,1,0:T(4,128)}, u32[]{:S(2)}) copy-start(f32[2,4,64]{2,1,0:T(4,128)} %refs_7_.1) | copy-start | bytes 6148
  19.7 1.4 %copy-start.4 = (s32[2,4,64]{2,1,0:T(4,128)S(1)}, s32[2,4,64]{2,1,0:T(4,128)}, u32[]{:S(2)}) copy-start(s32[2,4,64]{2,1,0:T(4,128)} %refs_5_.3) | copy-start | bytes 6148
  19.7 5.1 %collective-permute-start.4 = (f32[16,1536]{1,0:T(8,128)S(1)}, f32[16,1536]{1,0:T(8,128)S(1)}, u32[]{:S(2)}, u32[]{:S(2)}) collective-permute-start(f32[16,1536]{1,0:T(8,128)S(1)} %get-tuple-element.19), channel_id=1, source_target_pairs={{0,1},{1,0},{2,3},{3,2},{4,5},{5,4},{6,7},{7,6},{8,9},{9,8},{10,11... | collective-permute-start | bytes 294920 | tf_op jit(solution)/shard_map/ppermute | solution.py:502
  20.1 4.7 %collective-permute-start.5 = (f32[16,1536]{1,0:T(8,128)S(1)}, f32[16,1536]{1,0:T(8,128)S(1)}, u32[]{:S(2)}, u32[]{:S(2)}) collective-permute-start(f32[16,1536]{1,0:T(8,128)S(1)} %get-tuple-element.20), channel_id=1, source_target_pairs={{0,8},{1,2},{2,1},{3,4},{4,3},{5,6},{6,5},{7,15},{8,0},{9,10},{10,... | collective-permute-start | bytes 294920 | tf_op jit(solution)/shard_map/ppermute | solution.py:502

commit v4 on v3

--- a/solution.py
+++ b/solution.py
@@ -24,14 +24,6 @@
         parts.append(part)
         x = x - part.astype(F32)
     return parts
-
-
-def split_dot(x, onehot, count, dims):
-    total = None
-    for part in parts_of(x, count):
-        term = lax.dot_general(part, onehot, dims, preferred_element_type=F32)
-        total = term if total is None else total + term
-    return total
 
 
 def joint_dot(x, onehot, count, dims):
@@ -170,12 +162,14 @@
     return jnp.where(even, next_, mate), jnp.where(even, mate, next_)
 
 
-def by_field(z, scalar, width):
-    sub = iota((SUBL, width), 0)
-    out = jnp.zeros((SUBL, width), F32)
-    for f in range(z.fields):
-        out = jnp.where(sub == f, scalar(f), out)
-    return out
+def wide(value, rows, cols):
+    return jnp.concatenate([jnp.broadcast_to(value, (rows, LANES))] * (cols // LANES), axis=1)
+
+
+def weights_of(z, steps, couple, rows, cols):
+    dif = [wide(steps[:, f : f + 1], rows, cols) for f in range(z.fields)]
+    mix = [[wide(couple[e : e + 1, c : c + 1], rows, cols) for c in range(z.fields)] for e in range(z.fields)]
+    return dif, mix
 
 
 def unpack_strips(z, recv, sets):
@@ -191,7 +185,7 @@
     slot = lane // z.edge
     inner, plane = slot // SUBL, slot % SUBL
     picks = (iota((LANES, width), 0) == (plane * 2 + inner) * z.rows + lane % z.rows).astype(F32)
-    moved = split_dot(stacked, picks.astype(BF16), 3, (((1,), (0,)), ((), ())))
+    moved = joint_dot(stacked, picks.astype(BF16), 3, (((1,), (0,)), ((), ())))
     lane = iota((height, z.edge), 1)
     keep = lane // z.rows == iota((height, z.edge), 0)
     out = []
@@ -212,10 +206,10 @@
     return values * values[z.fields : z.fields + 1] * dif
 
 
-def coupled(z, couple, state, c):
+def coupled(z, mix, state, c):
     total = None
     for e in range(z.fields):
-        term = state(e) * couple[e, c]
+        term = state(e) * mix[e][c]
         total = term if total is None else total + term
     return total
 
@@ -305,62 +299,84 @@
     return north + south
 
 
-def early_kernel(z, adj, cond, *refs):
+def own_kernel(z, adj, cond, steps, couple, out, scaled):
+    dif, mix = weights_of(z, steps, couple, z.rows, z.cols)
+    for f in range(z.fields):
+        s = adj[0, f, 0] * (cond[0, 0] * dif[f])
+        scaled[f] = s
+        new = adj[0, f, 0] - 6.0 * s + sideways(s) + upright(s, 0.0, 0.0)
+        out[f] = new + coupled(z, mix, lambda e: adj[0, e, 0], f)
+
+
+def far_kernel(z, adj2, steps, couple, state, out):
+    dif, mix = weights_of(z, steps, couple, z.rows, z.cols)
+    for f in range(z.fields):
+        state[f] = adj2[0, f, 0] * dif[f]
+        out[f] = adj2[0, f, 0] + coupled(z, mix, lambda e: adj2[0, e, 0], f)
+
+
+def early_kernel(z, cond, first, scaled, *refs):
     if z.pair:
-        adj2, cond2, diffus, couple, out, mate, next_, own, far = refs
+        weighed, mixed, cond2, steps, couple, out, mate, next_, own, far = refs
     else:
-        beside, diffus, couple, out, mate, next_, own = refs
+        beside, steps, couple, out, mate, next_, own = refs
+    dif, mix = weights_of(z, steps, couple, z.rows, z.cols)
     own_c = cond[0, 0]
     far_c = cond2[0, 0] if z.pair else None
     for f in range(z.fields):
-        s = adj[0, f, 0] * (own_c * diffus[f])
-        new = adj[0, f, 0] - 6.0 * s + sideways(s) + upright(s, 0.0, 0.0)
-        new = new + coupled(z, couple, lambda e: adj[0, e, 0], f)
         if z.pair:
-            other = adj2[0, f, 0] * (far_c * diffus[f])
-            new = new + other
-            part = adj2[0, f, 0] - 6.0 * other + sideways(other) + upright(other, 0.0, 0.0) + s
-            far[f] = part + coupled(z, couple, lambda e: adj2[0, e, 0], f)
+            other = weighed[f] * far_c
+            new = first[f] + other
+            far[f] = mixed[f] - 6.0 * other + sideways(other) + upright(other, 0.0, 0.0) + scaled[f]
             at = SUBL + f
             mate[at : at + 1, :], next_[at : at + 1, :] = facing(other)
         else:
-            new = new + beside[f]
+            new = first[f] + beside[f]
         own[f] = new
-        mate[f : f + 1, :], next_[f : f + 1, :] = facing(new * (own_c * diffus[f]))
+        mate[f : f + 1, :], next_[f : f + 1, :] = facing(new * (own_c * dif[f]))
     for half in range(2 if z.pair else 1):
         for ref in (mate, next_):
             ref[half * SUBL + z.fields : (half + 1) * SUBL, :] = jnp.zeros((SUBL - z.fields, z.cols), F32)
     for f in range(z.fields):
-        s = own[f] * (own_c * diffus[f])
+        s = own[f] * (own_c * dif[f])
         new = own[f] - 6.0 * s + sideways(s) + upright(s, 0.0, 0.0)
-        new = new + coupled(z, couple, lambda e: own[e], f)
+        new = new + coupled(z, mix, lambda e: own[e], f)
         if z.pair:
-            new = new + far[f] * (far_c * diffus[f])
+            new = new + far[f] * (far_c * dif[f])
         out[f] = new
 
 
-def ends_kernel(z, recv, cond, diffus, mate_row, next_row, mate_in, next_in, mate, next_, spread_a, spread_b):
-    panel, rad, tile = lax.axis_index("panel"), lax.axis_index("rad"), lax.axis_index("ang")
-    outer = jnp.where(rad == z.rads - 1, 1.0, 0.0)
+def link_kernel(z, cond, steps, mate_row, next_row, mate_in, next_in, mate, next_):
+    tile = lax.axis_index("ang")
     inner = jnp.where((tile == 0) | (tile == z.tiles - 1), 0.0, 1.0)
-    top, bottom = deposit_ends(z, recv, panel, spread_a, spread_b)
-    even = even_tile()
-    to_mate = jnp.where(even, bottom, top) * outer
-    to_next = jnp.where(even, top, bottom) * outer
     cond_mate, cond_next = facing(cond[0, 0])
     for f in range(z.fields):
-        from_mate, from_next = mate_row[f : f + 1, :], next_row[f : f + 1, :] * inner
-        if f == 3:
-            from_mate, from_next = from_mate + to_mate, from_next + to_next
-        mate[f : f + 1, :] = mate_in[f : f + 1, :] + from_mate * (cond_mate * diffus[f])
-        next_[f : f + 1, :] = next_in[f : f + 1, :] + from_next * (cond_next * diffus[f])
+        dif = wide(steps[:, f : f + 1], 1, z.cols)
+        mate[f : f + 1, :] = mate_in[f : f + 1, :] + mate_row[f : f + 1, :] * (cond_mate * dif)
+        next_[f : f + 1, :] = next_in[f : f + 1, :] + next_row[f : f + 1, :] * (cond_next * dif * inner)
+
+
+def ends_kernel(z, recv, cond, steps, mate, next_, spread_a, spread_b):
+    panel, rad = lax.axis_index("panel"), lax.axis_index("rad")
+    mate[...] = jnp.zeros_like(mate)
+    next_[...] = jnp.zeros_like(next_)
+
+    @pl.when(rad == z.rads - 1)
+    def _():
+        top, bottom = deposit_ends(z, recv, panel, spread_a, spread_b)
+        weight = cond[0, 0] * wide(steps[:, 3:4], z.rows, z.cols)
+        top = top * weight[:1]
+        bottom = bottom * weight[z.rows - 1 :]
+        even = even_tile()
+        mate[...] = jnp.where(even, bottom, top)
+        next_[...] = jnp.where(even, top, bottom)
 
 
 def ghost_kernel(z, early, recv, cond, *refs):
     if z.pair:
-        cond2, mate_in, next_in, diffus, couple, grow, gcol, gwt, out, added, spread_a, spread_b = refs
+        cond2, mate_in, next_in, steps, couple, grow, gcol, gwt, out, added, spread_a, spread_b = refs
     else:
-        mate_in, next_in, diffus, couple, grow, gcol, gwt, out, added, spread_a, spread_b = refs
+        mate_in, next_in, steps, couple, grow, gcol, gwt, out, added, spread_a, spread_b = refs
     panel, rad, tile = lax.axis_index("panel"), lax.axis_index("rad"), lax.axis_index("ang")
     other = 1 - panel
     outer = jnp.where(rad == z.rads - 1, 1.0, 0.0)
@@ -374,41 +390,44 @@
         sets += [(other, jnp.maximum(rad - 1, 0)), (other, jnp.minimum(rad + 1, z.rads - 1))]
         near = [jnp.where(rad > 0, 1.0, 0.0), jnp.where(rad < z.rads - 1, 1.0, 0.0)]
     strips = unpack_strips(z, recv, sets)
-    dif = by_field(z, lambda f: diffus[f], z.edge)
+    dif, mix = weights_of(z, steps, couple, z.rows, z.cols)
+    plane = iota((SUBL, z.edge), 0)
+    by_plane = jnp.zeros((SUBL, z.edge), F32)
+    for f in range(z.fields):
+        by_plane = jnp.where(plane == f, wide(steps[:, f : f + 1], SUBL, z.edge), by_plane)
     rim, inside = strips[0]
-    rim_s = edge_scaled(z, rim, dif)
-    home_s = edge_scaled(z, strips[1][0], dif)
-    layers_s = [edge_scaled(z, strips[2 + k][0], dif) for k in range(len(near))]
-    lap = edge_scaled(z, inside, dif) - 6.0 * rim_s
+    rim_s = edge_scaled(z, rim, by_plane)
+    home_s = edge_scaled(z, strips[1][0], by_plane)
+    layers_s = [edge_scaled(z, strips[2 + k][0], by_plane) for k in range(len(near))]
+    lap = edge_scaled(z, inside, by_plane) - 6.0 * rim_s
     for k, one in enumerate(near):
         lap = lap + layers_s[k] * one
     spot = iota((SUBL, z.edge), 1) % z.total_rows
     lap = lap + jnp.where(spot == 0, 0.0, pltpu.roll(rim_s, 1, 1))
     lap = lap + jnp.where(spot == z.total_rows - 1, 0.0, pltpu.roll(rim_s, z.edge - 1, 1))
-    rows = [coupled(z, couple, lambda e: rim[e : e + 1], c) for c in range(z.fields)]
+    thin = [[mix[e][f][:1, : z.edge] for f in range(z.fields)] for e in range(z.fields)]
+    rows = [coupled(z, thin, lambda e: rim[e : e + 1], c) for c in range(z.fields)]
     mixed = jnp.concatenate(rows + [jnp.zeros((SUBL - z.fields, z.edge), F32)], axis=0)
 
     g_row = [line_of(grow, q) for q in range(z.stencil)]
     g_col = [line_of(gcol, q) for q in range(z.stencil)]
     g_wt = [line_of(gwt, q) for q in range(z.stencil)]
-    rim_ghost = None
+    targets = []
     for q in range(z.stencil):
-        target = jnp.where(
-            g_col[q] == 0, g_row[q], jnp.where(g_col[q] == z.cols - 1, z.total_rows + g_row[q], -1)
-        )
-        hits = (iota((z.edge, z.edge), 0) == target).astype(F32).astype(BF16)
-        values = jnp.concatenate([home_s * g_wt[q], jnp.zeros((SUBL, z.edge), F32)], axis=0)
-        term = split_dot(values, hits, 3, NT_DIMS)
-        rim_ghost = term if rim_ghost is None else rim_ghost + term
+        last_one = jnp.where(g_col[q] == z.cols - 1, z.total_rows + g_row[q], -1)
+        targets.append(jnp.where(g_col[q] == 0, g_row[q], last_one))
+    hits = (iota((z.edge, z.stencil * z.edge), 0) == jnp.concatenate(targets, axis=1)).astype(F32)
+    values = jnp.concatenate([home_s * g_wt[q] for q in range(z.stencil)], axis=1)
+    rim_ghost = joint_dot(values, hits.astype(BF16), 3, NT_DIMS)
     sources = z.rads * z.tiles
     pulse = []
     for k in range(z.edge_rows):
         at = other * sources * z.block + z.feat_rows + k
         pulse.append(jnp.sum(recv[pl.ds(at, sources, stride=z.block), :], axis=0, keepdims=True))
     pulse = jnp.concatenate(pulse, axis=1) * outer
-    rim_first = rim + lap + mixed + rim_ghost[:SUBL]
+    rim_first = rim + lap + mixed + rim_ghost
     rim_first = rim_first + jnp.where(iota((SUBL, z.edge), 0) == 3, pulse, 0.0)
-    rim_second = rim_first * rim[z.fields : z.fields + 1] * dif
+    rim_second = rim_first * rim[z.fields : z.fields + 1] * by_plane
 
     row0 = tile * z.rows
     aimed = [jnp.where(iota((z.rows, z.edge), 0) == g_row[q] - row0, g_wt[q], 0.0) for q in range(z.stencil)]
@@ -421,13 +440,10 @@
         stacked.append(
             jnp.concatenate([rim_s * jnp.where(g_row[q] == row, g_wt[q], 0.0) for q in range(z.stencil)], axis=1)
         )
-    height = len(loads) * z.fields * z.rows + 2 * SUBL
-    if height % 16:
-        stacked.append(jnp.zeros((16 - height % 16, z.stencil * z.edge), F32))
     stacked = jnp.concatenate(stacked, axis=0)
     spots = jnp.concatenate(g_col, axis=1)
     columns = (iota((z.cols, z.stencil * z.edge), 0) == spots).astype(F32).astype(BF16)
-    ghost = split_dot(stacked, columns, 2, NT_DIMS)
+    ghost = joint_dot(stacked, columns, 2, NT_DIMS)
 
     def ghost_of(step, f):
         at = (step * z.fields + f) * z.rows
@@ -441,16 +457,16 @@
         new = ghost_of(0, f) + brim(above[f : f + 1], below[f : f + 1], z.rows)
         added[f] = new + force[1] * outer if f == 3 else new
     for f in range(z.fields):
-        s = added[f] * (own_c * diffus[f])
-        high = ghost_above[f : f + 1] * (above[z.fields :] * diffus[f])
-        low = ghost_below[f : f + 1] * (below[z.fields :] * diffus[f])
+        s = added[f] * (own_c * dif[f])
+        high = ghost_above[f : f + 1] * (above[z.fields :] * dif[f][:1])
+        low = ghost_below[f : f + 1] * (below[z.fields :] * dif[f][:1])
         new = early[f] + added[f] - 6.0 * s + sideways(s) + upright(s, high, low)
-        new = new + coupled(z, couple, lambda e: added[e], f) + ghost_of(1, f)
+        new = new + coupled(z, mix, lambda e: added[e], f) + ghost_of(1, f)
         if z.pair:
             part = ghost_of(2, f)
             if f == 3:
                 part = part + force[1] * (1.0 - outer)
-            new = new + part * (cond2[0, 0] * diffus[f])
+            new = new + part * (cond2[0, 0] * dif[f])
         if f == 3:
             new = new + force[0] * outer
         out[f] = new
@@ -463,16 +479,19 @@
 
 def last_kernel(z, late, *refs):
     if z.pair:
-        cond2, mate_in, next_in, diffus, out = refs
+        cond2, mate_in, next_in, mate_end, next_end, steps, out = refs
     else:
-        beside, mate_in, next_in, diffus, out = refs
+        beside, mate_in, next_in, mate_end, next_end, steps, out = refs
     above, below = around(z, mate_in[...], next_in[...])
+    above_end, below_end = around(z, mate_end[...], next_end[...])
     for f in range(z.fields):
         high, low = above[f : f + 1], below[f : f + 1]
+        if f == 3:
+            high, low = high + above_end, low + below_end
         if z.pair:
-            far_c = cond2[0, 0]
-            high = high + above[SUBL + f : SUBL + f + 1] * (far_c[:1] * diffus[f])
-            low = low + below[SUBL + f : SUBL + f + 1] * (far_c[z.rows - 1 :] * diffus[f])
+            far_c = cond2[0, 0] * wide(steps[:, f : f + 1], z.rows, z.cols)
+            high = high + above[SUBL + f : SUBL + f + 1] * far_c[:1]
+            low = low + below[SUBL + f : SUBL + f + 1] * far_c[z.rows - 1 :]
         new = late[f] + brim(high, low, z.rows)
         out[0, f, 0] = new if z.pair else new + beside[f]
 
@@ -502,15 +521,28 @@
     return lax.ppermute(mate, axes, pairs), lax.ppermute(next_, axes, links)
 
 
-def call(kernel, shapes, scratch, args, scalars=(), spaces=None, room=48, aliases=None):
-    specs = [
-        pl.BlockSpec(memory_space=spaces or (pltpu.SMEM if n in scalars else pltpu.VMEM))
-        for n in range(len(args))
-    ]
+def outer_rows(z, mate, next_):
+    pairs, links = [], []
+    for panel in range(z.panels):
+        for rad in range(z.rads):
+            at = (panel * z.rads + rad) * z.tiles
+            for i in range(z.tiles):
+                pairs.append((at + i, at + (i ^ 1)))
+                if rad < z.rads - 1:
+                    links.append((at + i, at + (i ^ 1)))
+                elif 0 < i < z.tiles - 1:
+                    links.append((at + i, at + (i + 1 if i % 2 else i - 1)))
+                else:
+                    links.append((at + i, ((panel ^ 1) * z.rads + rad) * z.tiles + i))
+    axes = ("panel", "rad", "ang")
+    return lax.ppermute(mate, axes, pairs), lax.ppermute(next_, axes, links)
+
+
+def call(kernel, shapes, scratch, args, spaces=pltpu.VMEM, room=48, aliases=None):
     return pl.pallas_call(
         kernel,
-        out_shape=[x if isinstance(x, jax.ShapeDtypeStruct) else jax.ShapeDtypeStruct(x, F32) for x in shapes],
-        in_specs=specs,
+        out_shape=[jax.ShapeDtypeStruct(shape, F32) for shape in shapes],
+        in_specs=[pl.BlockSpec(memory_space=spaces)] * len(args),
         out_specs=[pl.BlockSpec(memory_space=pltpu.VMEM)] * len(shapes),
         scratch_shapes=scratch,
         input_output_aliases=aliases or {},
@@ -544,38 +576,46 @@
     recv = recv.reshape(z.devices * z.block, LANES)
     rows = list(beside_rows(z, *rows))
 
-    args = [adj, cond] + beside + [diffus, couple]
+    steps = diffus.reshape(1, z.fields)
+    own = call(functools.partial(own_kernel, z), [state, state], [], [adj, cond, steps, couple])
+    if z.pair:
+        beside[:1] = call(functools.partial(far_kernel, z), [state, state], [], [beside[0], steps, couple])
+    args = [cond] + list(own) + beside + [steps, couple]
     early, mate, next_, *first = call(
         functools.partial(early_kernel, z),
         [state, lines, lines] + ([] if z.pair else [state]),
         [pltpu.VMEM(state, F32)] * (2 if z.pair else 0),
         args,
-        (len(args) - 2, len(args) - 1),
-    )
+    )
+    links = call(
+        functools.partial(link_kernel, z),
+        [lines, lines],
+        [],
+        [cond, steps] + rows + [mate, next_],
+        aliases={4: 0, 5: 1},
+    )
+    beyond = list(beside_rows(z, *links))
     points = z.rads * z.tiles * z.npr * LANES
     ends = 2 * z.cols // LANES
-    mate, next_ = call(
+    ends = call(
         functools.partial(ends_kernel, z),
-        [lines, lines],
+        [(1, z.cols), (1, z.cols)],
         [pltpu.VMEM((2 * ends, points), BF16), pltpu.VMEM((LANES, points), BF16)],
-        [recv, cond, diffus] + rows + [mate, next_],
-        (2,),
-        aliases={5: 0, 6: 1},
-    )
-    mate, next_ = beside_rows(z, mate, next_)
-    args = [early, recv, cond] + far + rows + [diffus, couple]
+        [recv, cond, steps],
+    )
+    beyond += outer_rows(z, *ends)
+    args = [early, recv, cond] + far + rows + [steps, couple]
     late, *added = call(
         functools.partial(ghost_kernel, z),
         [state] if z.pair else [state, state],
         ([pltpu.VMEM(state, F32)] if z.pair else [])
         + [pltpu.VMEM((2 * TIMES * z.hi, points), BF16), pltpu.VMEM((LOW, points), BF16)],
         args + [ghost_row, ghost_col, ghost_wt],
-        (len(args) - 2, len(args) - 1),
     )
     if not z.pair:
         far = [both_sides(coeff * (first[0] + added[0]), "rad")]
-    args = [late] + far + [mate, next_, diffus]
-    (out,) = call(functools.partial(last_kernel, z), [adj.shape], [], args, (len(args) - 1,))
+    args = [late] + far + beyond + [steps]
+    (out,) = call(functools.partial(last_kernel, z), [adj.shape], [], args)
     return out
 
 

time: 26.5 us -> 23.3 us (0.88)
  Pallas kernels: 10.9 us -> 8.3 us
  waiting for transfers between devices: 2.8 us -> 0.72 us
  starting transfers between devices: 11.4 us -> 12.4 us
  local copies, waits for them, and re-layouts: 1.01 us -> 1.34 us
    pallas_call x5 -> x8, Pallas kernels: 10.9 us -> 8.3 us  [call(): pl.pallas_call(kernel, out_shape=[jax.ShapeDtypeStruct(shape, F32) for sh...]
    ppermute x2, waiting for transfers between devices: 2.21 us -> 0.01 us  [body(): beside = [lax.ppermute(adj, 'rad', swap), lax.ppermute(cond, 'rad', swap)]]
    ppermute x0 -> x2, starting transfers between devices: none -> 0.88 us  [outer_rows(): return (lax.ppermute(mate, axes, pairs), lax.ppermute(next_, axes, links))]
    ppermute x4, waiting for transfers between devices: 0.01 us -> 0.4 us  [beside_rows(): return (lax.ppermute(mate, axes, pairs), lax.ppermute(next_, axes, links))]
    unnamed x18, local copies, waits for them, and re-layouts: 1.01 us -> 1.34 us
  transfers between devices with their start and end apart: 7 -> 9, of which waited for: 2 -> 3; matrix products, arithmetic and copies ran while one was open for 0% -> 0% of each run, Pallas kernels for 31% -> 32%
where the time goes in v4:
time: 23.3 us; the launch traced here: 23 us
  starting transfers between devices  12.4 us (53%)
  Pallas kernels  8.3 us (36%)
  local copies, waits for them, and re-layouts  1.34 us (6%)
  waiting for transfers between devices  0.72 us (3%)
    pallas_call x8, Pallas kernels, call(): pl.pallas_call(kernel, out_shape=[jax.ShapeDtypeStruct(shape, F32) for sh...  8.3 us
    all_to_all x1, starting transfers between devices, body(): lax.all_to_all(pay, ('panel', 'rad', 'ang'), split_axis=0, concat_axis=0,...  4.9 us
    ppermute x2, starting transfers between devices, body(): beside = [lax.ppermute(adj, 'rad', swap), lax.ppermute(cond, 'rad', swap)]  4.8 us
    ppermute x4, starting transfers between devices, beside_rows(): return (lax.ppermute(mate, axes, pairs), lax.ppermute(next_, axes, links))  1.86 us
    unnamed x18, local copies, waits for them, and re-layouts  1.34 us
    ppermute x2, starting transfers between devices, outer_rows(): return (lax.ppermute(mate, axes, pairs), lax.ppermute(next_, axes, links))  0.88 us
  transfers between devices with their start and end apart: 9, of which 3 were waited for; matrix products, arithmetic and copies ran while one was open for 0% of the time, Pallas kernels for 32%

profile of v4, /device:TPU:0, one launch (start us, length us, event | category | flops | bytes accessed | tf_op | source)
XLA Modules:
  0.0 23.0 jit_solution(15041292430285589987)
XLA Ops:
  0.0 3.0 %collective-permute-start = (f32[1,7,1,8,1536]{4,3,2,1,0:T(8,128)}, f32[1,7,1,8,1536]{4,3,2,1,0:T(8,128)}, u32[]{:S(2)}, u32[]{:S(2)}) collective-permute-start(f32[1,7,1,8,1536]{4,3,2,1,0:T(8,128)} %refs_0_.1), channel_id=1, source_target_pairs={{0,8},{8,0},{1,9},{9,1},{2,10},{10,2},{3,11},{11,3},{4,12},{12,4},... | collective-permute-start | bytes 1032200 | tf_op jit(solution)/shard_map/ppermute | solution.py:559
  3.0 2.2 %shard_map.112 = (f32[32,8,128]{2,1,0:T(8,128)}, f32[8,1536]{1,0:T(8,128)}, f32[8,1536]{1,0:T(8,128)}) custom-call(f32[1,7,1,8,1536]{4,3,2,1,0:T(8,128)} %refs_0_.1, f32[1,1,8,1536]{3,2,1,0:T(8,128)} %cond.9, f32[7]{0:T(128)} %refs_2_.1, s32[1,256]{1,0:T(1,128)} %bitcast.12, s32[1,1,4,256]{3,2,1,0:T(4,128)} %refs_4_.4, f32[1,1,4,256]{3,2,1,0:T(4,128)} %refs_5_.2, ...), custom_call_target="tpu_custom_call" | custom-call | tf_op jit(solution)/shard_map/pallas_call | solution.py:542
  5.2 0.0 copy-start
  5.2 0.0 copy-start.8
  5.2 0.0 copy-start.7
  5.2 4.9 %all-to-all-start = ((f32[32,8,128]{2,1,0:T(8,128)}), f32[32,8,128]{2,1,0:T(8,128)S(1)}, u32[]{:S(2)}, u32[]{:S(2)}) async-start(f32[32,8,128]{2,1,0:T(8,128)} %get-tuple-element.24), calls=%async_computation | async-start | bytes 262144 | tf_op jit(solution)/shard_map/all_to_all | solution.py:575
  10.1 0.0 copy-done
  10.1 0.0 copy-start.2
  10.1 1.8 %collective-permute-start.1 = (f32[1,1,8,1536]{3,2,1,0:T(8,128)S(1)}, f32[1,1,8,1536]{3,2,1,0:T(8,128)S(1)}, u32[]{:S(2)}, u32[]{:S(2)}) collective-permute-start(f32[1,1,8,1536]{3,2,1,0:T(8,128)S(1)} %copy-done), channel_id=1, source_target_pairs={{0,8},{8,0},{1,9},{9,1},{2,10},{10,2},{3,11},{11,3},{4,12},{12,4},... | collective-permute-start | bytes 147464 | tf_op jit(solution)/shard_map/ppermute | solution.py:559
  11.9 0.0 copy-done.8
  12.0 0.0 collective-permute-start.2
  12.0 0.0 copy-done.7
  12.0 0.0 copy-start.3
  12.0 0.3 %collective-permute-start.3 = (f32[8,1536]{1,0:T(8,128)S(1)}, f32[8,1536]{1,0:T(8,128)S(1)}, u32[]{:S(2)}, u32[]{:S(2)}) collective-permute-start(f32[8,1536]{1,0:T(8,128)S(1)} %copy-done.7), channel_id=1, source_target_pairs={{0,8},{1,2},{2,1},{3,4},{4,3},{5,6},{6,5},{7,15},{8,0},{9,10},{10,... | collective-permute-start | bytes 147464 | tf_op jit(solution)/shard_map/ppermute | solution.py:521
  12.3 0.0 copy-done.2
  12.3 0.3 %copy-done.3 = f32[7]{0:T(128)S(1)} copy-done((f32[7]{0:T(128)S(1)}, f32[7]{0:T(128)}, u32[]{:S(2)}) %copy-start.3) | copy-done | bytes 52
  12.6 0.0 copy-start.1
  12.6 1.0 %copy-done.1 = f32[1,7,1,8,1536]{4,3,2,1,0:T(8,128)S(1)} copy-done((f32[1,7,1,8,1536]{4,3,2,1,0:T(8,128)S(1)}, f32[1,7,1,8,1536]{4,3,2,1,0:T(8,128)}, u32[]{:S(2)}) %copy-start.1) | copy-done | bytes 344088
  13.6 0.4 %shard_map.109 = (f32[7,8,1536]{2,1,0:T(8,128)S(1)}, f32[7,8,1536]{2,1,0:T(8,128)S(1)}) custom-call(f32[1,7,1,8,1536]{4,3,2,1,0:T(8,128)S(1)} %copy-done.1, f32[1,1,8,1536]{3,2,1,0:T(8,128)S(1)} %copy-done, f32[1,7]{1,0:T(1,128)S(1)} %bitcast.5, f32[7,7]{1,0:T(8,128)S(1)} %copy-done.2), custom_call_target="tpu_custom_call" | custom-call | tf_op jit(solution)/shard_map/pallas_call | solution.py:542
  14.0 0.0 collective-permute-done.adj2
  14.0 1.3 %shard_map.110 = (f32[7,8,1536]{2,1,0:T(8,128)S(1)}, f32[7,8,1536]{2,1,0:T(8,128)S(1)}) custom-call(f32[1,7,1,8,1536]{4,3,2,1,0:T(8,128)} %collective-permute-done.adj2, f32[1,7]{1,0:T(1,128)S(1)} %bitcast.6, f32[7,7]{1,0:T(8,128)S(1)} %copy-done.2), custom_call_target="tpu_custom_call" | custom-call | tf_op jit(solution)/shard_map/pallas_call | solution.py:542
  15.4 0.0 collective-permute-done.1.refs_2_.refs_0_
  15.4 0.8 %shard_map.111 = (f32[7,8,1536]{2,1,0:T(8,128)S(1)}, f32[16,1536]{1,0:T(8,128)S(1)}, f32[16,1536]{1,0:T(8,128)S(1)}) custom-call(f32[1,1,8,1536]{3,2,1,0:T(8,128)S(1)} %copy-done, f32[7,8,1536]{2,1,0:T(8,128)S(1)} %get-tuple-element.19.first, f32[7,8,1536]{2,1,0:T(8,128)S(1)} %get-tuple-element.20.scaled, f32[7,8,1536]{2,1,0:T(8,128)S(1)} %get-tuple-element.21.refs_0_, ...), custom_call_target="tpu_custom_call" | custom-call | tf_op jit(solution)/shard_map/pallas_call | solution.py:542
  16.1 0.0 collective-permute-done.2.refs_1_.mate_row
  16.1 0.1 collective-permute-done.3.refs_2_.next_row
  16.3 0.2 shard_map.114
  16.4 1.0 %collective-permute-start.4 = (f32[16,1536]{1,0:T(8,128)S(1)}, f32[16,1536]{1,0:T(8,128)S(1)}, u32[]{:S(2)}, u32[]{:S(2)}) collective-permute-start(f32[16,1536]{1,0:T(8,128)S(1)} %get-tuple-element.29), channel_id=1, source_target_pairs={{0,1},{1,0},{2,3},{3,2},{4,5},{5,4},{6,7},{7,6},{8,9},{9,8},{10,11... | collective-permute-start | bytes 294920 | tf_op jit(solution)/shard_map/ppermute | solution.py:521
  17.4 0.6 %collective-permute-start.5 = (f32[16,1536]{1,0:T(8,128)S(1)}, f32[16,1536]{1,0:T(8,128)S(1)}, u32[]{:S(2)}, u32[]{:S(2)}) collective-permute-start(f32[16,1536]{1,0:T(8,128)S(1)} %get-tuple-element.30), channel_id=1, source_target_pairs={{0,8},{1,2},{2,1},{3,4},{4,3},{5,6},{6,5},{7,15},{8,0},{9,10},{10,... | collective-permute-start | bytes 294920 | tf_op jit(solution)/shard_map/ppermute | solution.py:521
  18.0 0.3 %all-to-all-done = f32[32,8,128]{2,1,0:T(8,128)S(1)} async-done(((f32[32,8,128]{2,1,0:T(8,128)}), f32[32,8,128]{2,1,0:T(8,128)S(1)}, u32[]{:S(2)}, u32[]{:S(2)}) %all-to-all-start) | async-done | bytes 131104 | tf_op jit(solution)/shard_map/all_to_all | solution.py:575
  18.3 0.0 copy-start.5
  18.3 0.0 copy-start.6
  18.3 0.0 copy-start.4
  18.3 0.8 %collective-permute-start.6 = (f32[1,1536]{1,0:T(1,128)S(1)}, f32[1,1536]{1,0:T(1,128)S(1)}, u32[]{:S(2)}, u32[]{:S(2)}) collective-permute-start(f32[1,1536]{1,0:T(1,128)S(1)} %get-tuple-element.31), channel_id=1, source_target_pairs={{0,1},{1,0},{2,3},{3,2},{4,5},{5,4},{6,7},{7,6},{8,9},{9,8},{10,11... | collective-permute-start | bytes 18440 | tf_op jit(solution)/shard_map/ppermute | solution.py:538
  19.1 0.1 collective-permute-start.7
  19.2 0.0 copy-done.5
  19.2 0.0 copy-done.6
  19.2 0.0 copy-done.4
  19.2 2.5 %shard_map.113.late = f32[7,8,1536]{2,1,0:T(8,128)S(1)} custom-call(f32[7,8,1536]{2,1,0:T(8,128)S(1)} %get-tuple-element.23.early, f32[256,128]{1,0:T(8,128)S(1)} %bitcast.4, f32[1,1,8,1536]{3,2,1,0:T(8,128)S(1)} %copy-done, f32[1,1,8,1536]{3,2,1,0:T(8,128)S(1)} %collective-permute-done.1.refs_2_.refs_0_, ...), custom_call_target="tpu_custom_call" | custom-call | tf_op jit(solution)/shard_map/pallas_call | solution.py:542
  21.7 0.0 collective-permute-done.6.refs_3_
  21.7 0.0 collective-permute-done.7.refs_4_
  21.7 0.0 collective-permute-done.4.refs_1_
  21.7 0.3 %collective-permute-done.5.refs_2_ = f32[16,1536]{1,0:T(8,128)S(1)} collective-permute-done((f32[16,1536]{1,0:T(8,128)S(1)}, f32[16,1536]{1,0:T(8,128)S(1)}, u32[]{:S(2)}, u32[]{:S(2)}) %collective-permute-start.5) | collective-permute-done | bytes 98336 | tf_op jit(solution)/shard_map/ppermute | solution.py:521
  22.0 0.9 %shard_map.116 = f32[1,7,1,8,1536]{4,3,2,1,0:T(8,128)} custom-call(f32[7,8,1536]{2,1,0:T(8,128)S(1)} %shard_map.113.late, f32[1,1,8,1536]{3,2,1,0:T(8,128)S(1)} %collective-permute-done.1.refs_2_.refs_0_, f32[16,1536]{1,0:T(8,128)S(1)} %collective-permute-done.4.refs_1_, f32[16,1536]{1,0:T(8,128)S(1)} %collective-permute-done.5.refs_2_, ...), custom_call_target="tpu_custom_call" | custom-call | tf_op jit(solution)/shard_map/pallas_call | solution.py:542
  (1 shorter events, 0.0 us)
Async XLA Ops:
  0.0 14.0 %collective-permute-start = (f32[1,7,1,8,1536]{4,3,2,1,0:T(8,128)}, f32[1,7,1,8,1536]{4,3,2,1,0:T(8,128)}, u32[]{:S(2)}, u32[]{:S(2)}) collective-permute-start(f32[1,7,1,8,1536]{4,3,2,1,0:T(8,128)} %refs_0_.1), channel_id=1, source_target_pairs={{0,8},{8,0},{1,9},{9,1},{2,10},{10,2},{3,11},{11,3},{4,12},{12,4},... | collective-permute-start | bytes 1032200 | tf_op jit(solution)/shard_map/ppermute | solution.py:559
  5.2 4.9 %copy-start = (f32[1,1,8,1536]{3,2,1,0:T(8,128)S(1)}, f32[1,1,8,1536]{3,2,1,0:T(8,128)}, u32[]{:S(2)}) copy-start(f32[1,1,8,1536]{3,2,1,0:T(8,128)} %cond.9) | copy-start | bytes 147460
  5.2 6.8 %copy-start.8 = (f32[8,1536]{1,0:T(8,128)S(1)}, f32[8,1536]{1,0:T(8,128)}, u32[]{:S(2)}) copy-start(f32[8,1536]{1,0:T(8,128)} %get-tuple-element.25) | copy-start | bytes 147460
  5.2 6.8 %copy-start.7 = (f32[8,1536]{1,0:T(8,128)S(1)}, f32[8,1536]{1,0:T(8,128)}, u32[]{:S(2)}) copy-start(f32[8,1536]{1,0:T(8,128)} %get-tuple-element.26) | copy-start | bytes 147460
  5.2 13.1 %all-to-all-start = ((f32[32,8,128]{2,1,0:T(8,128)}), f32[32,8,128]{2,1,0:T(8,128)S(1)}, u32[]{:S(2)}, u32[]{:S(2)}) async-start(f32[32,8,128]{2,1,0:T(8,128)} %get-tuple-element.24), calls=%async_computation | async-start | bytes 262144 | tf_op jit(solution)/shard_map/all_to_all | solution.py:575
  10.1 2.2 %copy-start.2 = (f32[7,7]{1,0:T(8,128)S(1)}, f32[7,7]{1,0:T(8,128)}, u32[]{:S(2)}) copy-start(f32[7,7]{1,0:T(8,128)} %refs_4_.5) | copy-start | bytes 592
  10.1 5.2 %collective-permute-start.1 = (f32[1,1,8,1536]{3,2,1,0:T(8,128)S(1)}, f32[1,1,8,1536]{3,2,1,0:T(8,128)S(1)}, u32[]{:S(2)}, u32[]{:S(2)}) collective-permute-start(f32[1,1,8,1536]{3,2,1,0:T(8,128)S(1)} %copy-done), channel_id=1, source_target_pairs={{0,8},{8,0},{1,9},{9,1},{2,10},{10,2},{3,11},{11,3},{4,12},{12,4},... | collective-permute-start | bytes 147464 | tf_op jit(solution)/shard_map/ppermute | solution.py:559
  12.0 4.2 %collective-permute-start.2 = (f32[8,1536]{1,0:T(8,128)S(1)}, f32[8,1536]{1,0:T(8,128)S(1)}, u32[]{:S(2)}, u32[]{:S(2)}) collective-permute-start(f32[8,1536]{1,0:T(8,128)S(1)} %copy-done.8), channel_id=1, source_target_pairs={{0,1},{1,0},{2,3},{3,2},{4,5},{5,4},{6,7},{7,6},{8,9},{9,8},{10,11... | collective-permute-start | bytes 147464 | tf_op jit(solution)/shard_map/ppermute | solution.py:521
  12.0 0.7 %copy-start.3 = (f32[7]{0:T(128)S(1)}, f32[7]{0:T(128)}, u32[]{:S(2)}) copy-start(f32[7]{0:T(128)} %refs_2_.1) | copy-start | bytes 88
  12.0 4.3 %collective-permute-start.3 = (f32[8,1536]{1,0:T(8,128)S(1)}, f32[8,1536]{1,0:T(8,128)S(1)}, u32[]{:S(2)}, u32[]{:S(2)}) collective-permute-start(f32[8,1536]{1,0:T(8,128)S(1)} %copy-done.7), channel_id=1, source_target_pairs={{0,8},{1,2},{2,1},{3,4},{4,3},{5,6},{6,5},{7,15},{8,0},{9,10},{10,... | collective-permute-start | bytes 147464 | tf_op jit(solution)/shard_map/ppermute | solution.py:521
  12.6 1.0 %copy-start.1 = (f32[1,7,1,8,1536]{4,3,2,1,0:T(8,128)S(1)}, f32[1,7,1,8,1536]{4,3,2,1,0:T(8,128)}, u32[]{:S(2)}) copy-start(f32[1,7,1,8,1536]{4,3,2,1,0:T(8,128)} %refs_0_.1) | copy-start | bytes 1032196
  16.4 5.3 %collective-permute-start.4 = (f32[16,1536]{1,0:T(8,128)S(1)}, f32[16,1536]{1,0:T(8,128)S(1)}, u32[]{:S(2)}, u32[]{:S(2)}) collective-permute-start(f32[16,1536]{1,0:T(8,128)S(1)} %get-tuple-element.29), channel_id=1, source_target_pairs={{0,1},{1,0},{2,3},{3,2},{4,5},{5,4},{6,7},{7,6},{8,9},{9,8},{10,11... | collective-permute-start | bytes 294920 | tf_op jit(solution)/shard_map/ppermute | solution.py:521
  17.4 4.6 %collective-permute-start.5 = (f32[16,1536]{1,0:T(8,128)S(1)}, f32[16,1536]{1,0:T(8,128)S(1)}, u32[]{:S(2)}, u32[]{:S(2)}) collective-permute-start(f32[16,1536]{1,0:T(8,128)S(1)} %get-tuple-element.30), channel_id=1, source_target_pairs={{0,8},{1,2},{2,1},{3,4},{4,3},{5,6},{6,5},{7,15},{8,0},{9,10},{10,... | collective-permute-start | bytes 294920 | tf_op jit(solution)/shard_map/ppermute | solution.py:521
  18.3 0.9 %copy-start.5 = (s32[2,4,64]{2,1,0:T(4,128)S(1)}, s32[2,4,64]{2,1,0:T(4,128)}, u32[]{:S(2)}) copy-start(s32[2,4,64]{2,1,0:T(4,128)} %refs_6_.3) | copy-start | bytes 6148
  18.3 0.9 %copy-start.6 = (f32[2,4,64]{2,1,0:T(4,128)S(1)}, f32[2,4,64]{2,1,0:T(4,128)}, u32[]{:S(2)}) copy-start(f32[2,4,64]{2,1,0:T(4,128)} %refs_7_.1) | copy-start | bytes 6148
  18.3 0.9 %copy-start.4 = (s32[2,4,64]{2,1,0:T(4,128)S(1)}, s32[2,4,64]{2,1,0:T(4,128)}, u32[]{:S(2)}) copy-start(s32[2,4,64]{2,1,0:T(4,128)} %refs_5_.3) | copy-start | bytes 6148
  18.3 3.4 %collective-permute-start.6 = (f32[1,1536]{1,0:T(1,128)S(1)}, f32[1,1536]{1,0:T(1,128)S(1)}, u32[]{:S(2)}, u32[]{:S(2)}) collective-permute-start(f32[1,1536]{1,0:T(1,128)S(1)} %get-tuple-element.31), channel_id=1, source_target_pairs={{0,1},{1,0},{2,3},{3,2},{4,5},{5,4},{6,7},{7,6},{8,9},{9,8},{10,11... | collective-permute-start | bytes 18440 | tf_op jit(solution)/shard_map/ppermute | solution.py:538
  19.1 2.6 %collective-permute-start.7 = (f32[1,1536]{1,0:T(1,128)S(1)}, f32[1,1536]{1,0:T(1,128)S(1)}, u32[]{:S(2)}, u32[]{:S(2)}) collective-permute-start(f32[1,1536]{1,0:T(1,128)S(1)} %get-tuple-element.32), channel_id=1, source_target_pairs={{0,1},{1,0},{2,3},{3,2},{4,5},{5,4},{6,7},{7,6},{8,24},{9,10},{10,... | collective-permute-start | bytes 18440 | tf_op jit(solution)/shard_map/ppermute | solution.py:538

commit v5 on v4

--- a/solution.py
+++ b/solution.py
@@ -237,6 +237,7 @@
 def dealt(z, values, highs, lows, height, spread_a, spread_b):
     width = spread_b.shape[0]
     sources = highs[0].shape[0]
+    used = 2 * len(values[0]) * height
     sub_high = iota((height, LANES), 0)
     sub_low = iota((width, LANES), 0)
     for h in range(z.npr):
@@ -249,16 +250,16 @@
             for k, part in enumerate(parts):
                 spread_a[k * height : (k + 1) * height, at : at + LANES] = jnp.where(hit, part[n : n + 1], 0.0).astype(BF16)
             spread_b[:, at : at + LANES] = (sub_low == lows[h][n : n + 1]).astype(F32).astype(BF16)
-    grid = lax.dot_general(spread_a[...], spread_b[...], NT_DIMS, preferred_element_type=F32)
+    grid = lax.dot_general(spread_a[:used, :], spread_b[...], NT_DIMS, preferred_element_type=F32)
     return [
         grid[2 * k * height : (2 * k + 1) * height] + grid[(2 * k + 1) * height : (2 * k + 2) * height]
         for k in range(len(values[0]))
     ]
 
 
-def deposit(z, recv, panel, spread_a, spread_b):
+def deposit(z, recv, panel, times, spread_a, spread_b):
     weights, codes, misfits = observed(z, recv, panel)
-    values = [[mis * weight for mis in misfits] for weight in weights]
+    values = [[misfits[t] * weight for t in times] for weight in weights]
     highs = [code // LOW for code in codes]
     lows = [code % LOW for code in codes]
     out = []
@@ -299,39 +300,31 @@
     return north + south
 
 
-def own_kernel(z, adj, cond, steps, couple, out, scaled):
-    dif, mix = weights_of(z, steps, couple, z.rows, z.cols)
-    for f in range(z.fields):
-        s = adj[0, f, 0] * (cond[0, 0] * dif[f])
-        scaled[f] = s
-        new = adj[0, f, 0] - 6.0 * s + sideways(s) + upright(s, 0.0, 0.0)
-        out[f] = new + coupled(z, mix, lambda e: adj[0, e, 0], f)
-
-
-def far_kernel(z, adj2, steps, couple, state, out):
-    dif, mix = weights_of(z, steps, couple, z.rows, z.cols)
-    for f in range(z.fields):
-        state[f] = adj2[0, f, 0] * dif[f]
-        out[f] = adj2[0, f, 0] + coupled(z, mix, lambda e: adj2[0, e, 0], f)
-
-
-def early_kernel(z, cond, first, scaled, *refs):
+def far_kernel(z, adj2, out):
+    out[...] = adj2[0, :, 0]
+
+
+def early_kernel(z, adj, cond, *refs):
     if z.pair:
-        weighed, mixed, cond2, steps, couple, out, mate, next_, own, far = refs
+        adj2, cond2, steps, couple, out, mate, next_, own, far = refs
     else:
         beside, steps, couple, out, mate, next_, own = refs
     dif, mix = weights_of(z, steps, couple, z.rows, z.cols)
     own_c = cond[0, 0]
     far_c = cond2[0, 0] if z.pair else None
     for f in range(z.fields):
+        s = adj[0, f, 0] * (own_c * dif[f])
+        new = adj[0, f, 0] - 6.0 * s + sideways(s) + upright(s, 0.0, 0.0)
+        new = new + coupled(z, mix, lambda e: adj[0, e, 0], f)
         if z.pair:
-            other = weighed[f] * far_c
-            new = first[f] + other
-            far[f] = mixed[f] - 6.0 * other + sideways(other) + upright(other, 0.0, 0.0) + scaled[f]
+            other = adj2[f] * (far_c * dif[f])
+            new = new + other
+            part = adj2[f] - 6.0 * other + sideways(other) + upright(other, 0.0, 0.0) + s
+            far[f] = part + coupled(z, mix, lambda e: adj2[e], f)
             at = SUBL + f
             mate[at : at + 1, :], next_[at : at + 1, :] = facing(other)
         else:
-            new = first[f] + beside[f]
+            new = new + beside[f]
         own[f] = new
         mate[f : f + 1, :], next_[f : f + 1, :] = facing(new * (own_c * dif[f]))
     for half in range(2 if z.pair else 1):
@@ -356,20 +349,27 @@
         next_[f : f + 1, :] = next_in[f : f + 1, :] + next_row[f : f + 1, :] * (cond_next * dif * inner)
 
 
-def ends_kernel(z, recv, cond, steps, mate, next_, spread_a, spread_b):
-    panel, rad = lax.axis_index("panel"), lax.axis_index("rad")
-    mate[...] = jnp.zeros_like(mate)
-    next_[...] = jnp.zeros_like(next_)
-
-    @pl.when(rad == z.rads - 1)
+def is_outer(z):
+    return lax.axis_index("rad") == z.rads - 1
+
+
+def ends_kernel(z, recv, cond, steps, mate_in, next_in, mate, next_, spread_a, spread_b):
+    panel = lax.axis_index("panel")
+    next_[mate.shape[0] :, :] = jnp.zeros((next_.shape[0] - mate.shape[0], z.cols), F32)
+    for f in range(mate.shape[0]):
+        at = f % z.fields + f // z.fields * SUBL
+        mate[f : f + 1, :] = mate_in[at : at + 1, :]
+        next_[f : f + 1, :] = next_in[at : at + 1, :]
+
+    @pl.when(is_outer(z))
     def _():
         top, bottom = deposit_ends(z, recv, panel, spread_a, spread_b)
         weight = cond[0, 0] * wide(steps[:, 3:4], z.rows, z.cols)
         top = top * weight[:1]
         bottom = bottom * weight[z.rows - 1 :]
         even = even_tile()
-        mate[...] = jnp.where(even, bottom, top)
-        next_[...] = jnp.where(even, top, bottom)
+        mate[3:4, :] = mate_in[3:4, :] + jnp.where(even, bottom, top)
+        next_[3:4, :] = next_in[3:4, :] + jnp.where(even, top, bottom)
 
 
 def ghost_kernel(z, early, recv, cond, *refs):
@@ -449,7 +449,7 @@
         at = (step * z.fields + f) * z.rows
         return ghost[at : at + z.rows]
 
-    force = deposit(z, recv, panel, spread_a, spread_b)
+    force = deposit(z, recv, panel, (0, 1), spread_a, spread_b)
     at = len(loads) * z.fields * z.rows
     ghost_above, ghost_below = ghost[at : at + SUBL], ghost[at + SUBL : at + 2 * SUBL]
     own_c = cond[0, 0]
@@ -479,19 +479,24 @@
 
 def last_kernel(z, late, *refs):
     if z.pair:
-        cond2, mate_in, next_in, mate_end, next_end, steps, out = refs
+        cond2, mate_inner, next_inner, mate_outer, next_outer, steps, out = refs
     else:
-        beside, mate_in, next_in, mate_end, next_end, steps, out = refs
-    above, below = around(z, mate_in[...], next_in[...])
-    above_end, below_end = around(z, mate_end[...], next_end[...])
-    for f in range(z.fields):
-        high, low = above[f : f + 1], below[f : f + 1]
-        if f == 3:
-            high, low = high + above_end, low + below_end
+        beside, mate_inner, next_inner, mate_outer, next_outer, steps, out = refs
+    outer = is_outer(z)
+
+    def beyond(half, f):
+        inner_at, outer_at = half * SUBL + f, half * z.fields + f
+        mate_in = jnp.where(outer, mate_outer[outer_at : outer_at + 1, :], mate_inner[inner_at : inner_at + 1, :])
+        next_in = jnp.where(outer, next_outer[outer_at : outer_at + 1, :], next_inner[inner_at : inner_at + 1, :])
+        return around(z, mate_in, next_in)
+
+    for f in range(z.fields):
+        high, low = beyond(0, f)
         if z.pair:
+            far_high, far_low = beyond(1, f)
             far_c = cond2[0, 0] * wide(steps[:, f : f + 1], z.rows, z.cols)
-            high = high + above[SUBL + f : SUBL + f + 1] * far_c[:1]
-            low = low + below[SUBL + f : SUBL + f + 1] * far_c[z.rows - 1 :]
+            high = high + far_high * far_c[:1]
+            low = low + far_low * far_c[z.rows - 1 :]
         new = late[f] + brim(high, low, z.rows)
         out[0, f, 0] = new if z.pair else new + beside[f]
 
@@ -521,14 +526,14 @@
     return lax.ppermute(mate, axes, pairs), lax.ppermute(next_, axes, links)
 
 
-def outer_rows(z, mate, next_):
+def some_rows(z, mate, next_, outer):
     pairs, links = [], []
     for panel in range(z.panels):
         for rad in range(z.rads):
             at = (panel * z.rads + rad) * z.tiles
             for i in range(z.tiles):
                 pairs.append((at + i, at + (i ^ 1)))
-                if rad < z.rads - 1:
+                if (rad == z.rads - 1) != outer:
                     links.append((at + i, at + (i ^ 1)))
                 elif 0 < i < z.tiles - 1:
                     links.append((at + i, at + (i + 1 if i % 2 else i - 1)))
@@ -538,7 +543,7 @@
     return lax.ppermute(mate, axes, pairs), lax.ppermute(next_, axes, links)
 
 
-def call(kernel, shapes, scratch, args, spaces=pltpu.VMEM, room=48, aliases=None):
+def call(kernel, shapes, scratch, args, spaces=pltpu.VMEM, room=48, aliases=None, cost=0):
     return pl.pallas_call(
         kernel,
         out_shape=[jax.ShapeDtypeStruct(shape, F32) for shape in shapes],
@@ -546,6 +551,7 @@
         out_specs=[pl.BlockSpec(memory_space=pltpu.VMEM)] * len(shapes),
         scratch_shapes=scratch,
         input_output_aliases=aliases or {},
+        cost_estimate=pl.CostEstimate(flops=0, bytes_accessed=cost, transcendentals=0) if cost else None,
         compiler_params=pltpu.CompilerParams(vmem_limit_bytes=room << 20),
     )(*args)
 
@@ -577,10 +583,9 @@
     rows = list(beside_rows(z, *rows))
 
     steps = diffus.reshape(1, z.fields)
-    own = call(functools.partial(own_kernel, z), [state, state], [], [adj, cond, steps, couple])
     if z.pair:
-        beside[:1] = call(functools.partial(far_kernel, z), [state, state], [], [beside[0], steps, couple])
-    args = [cond] + list(own) + beside + [steps, couple]
+        beside[:1] = call(functools.partial(far_kernel, z), [state], [], [beside[0]], cost=16 << 20)
+    args = [adj, cond] + beside + [steps, couple]
     early, mate, next_, *first = call(
         functools.partial(early_kernel, z),
         [state, lines, lines] + ([] if z.pair else [state]),
@@ -594,16 +599,16 @@
         [cond, steps] + rows + [mate, next_],
         aliases={4: 0, 5: 1},
     )
-    beyond = list(beside_rows(z, *links))
+    beyond = list(some_rows(z, *links, outer=False))
     points = z.rads * z.tiles * z.npr * LANES
     ends = 2 * z.cols // LANES
     ends = call(
         functools.partial(ends_kernel, z),
-        [(1, z.cols), (1, z.cols)],
+        [(z.fields * (2 if z.pair else 1) + spare, z.cols) for spare in range(2)],
         [pltpu.VMEM((2 * ends, points), BF16), pltpu.VMEM((LANES, points), BF16)],
-        [recv, cond, steps],
-    )
-    beyond += outer_rows(z, *ends)
+        [recv, cond, steps, *links],
+    )
+    beyond += some_rows(z, *ends, outer=True)
     args = [early, recv, cond] + far + rows + [steps, couple]
     late, *added = call(
         functools.partial(ghost_kernel, z),

time: 23.3 us -> 22.9 us (0.983)
  local copies, waits for them, and re-layouts: 1.34 us -> 0.14 us
  waiting for transfers between devices: 0.72 us -> 1.64 us
    ppermute x2 -> x4, starting transfers between devices: 0.88 us -> 2.57 us  [some_rows(): return (lax.ppermute(mate, axes, pairs), lax.ppermute(next_, axes, links))]
    ppermute x4 -> x2, starting transfers between devices: 1.86 us -> 0.32 us  [beside_rows(): return (lax.ppermute(mate, axes, pairs), lax.ppermute(next_, axes, links))]
    unnamed x18, local copies, waits for them, and re-layouts: 1.34 us -> 0.14 us
    ppermute x2, waiting for transfers between devices: 0.01 us -> 1.16 us  [body(): beside = [lax.ppermute(adj, 'rad', swap), lax.ppermute(cond, 'rad', swap)]]
    all_to_all x1, waiting for transfers between devices: 0.32 us -> 0.01 us  [body(): lax.all_to_all(pay, ('panel', 'rad', 'ang'), split_axis=0, concat_axis=0,...]
    pallas_call x8 -> x7, Pallas kernels: 8.3 us -> 8.12 us  [call(): pl.pallas_call(kernel, out_shape=[jax.ShapeDtypeStruct(shape, F32) for sh...]
    ppermute x4 -> x2, waiting for transfers between devices: 0.4 us -> 0.47 us  [beside_rows(): return (lax.ppermute(mate, axes, pairs), lax.ppermute(next_, axes, links))]
  transfers between devices with their start and end apart: 9 -> 9, of which waited for: 3 -> 2; matrix products, arithmetic and copies ran while one was open for 0% -> 0% of each run, Pallas kernels for 32% -> 32%
where the time goes in v5:
time: 22.9 us; the launch traced here: 22.7 us
  starting transfers between devices  12.6 us (55%)
  Pallas kernels  8.12 us (35%)
  waiting for transfers between devices  1.64 us (7%)
    pallas_call x7, Pallas kernels, call(): pl.pallas_call(kernel, out_shape=[jax.ShapeDtypeStruct(shape, F32) for sh...  8.12 us
    all_to_all x1, starting transfers between devices, body(): lax.all_to_all(pay, ('panel', 'rad', 'ang'), split_axis=0, concat_axis=0,...  4.9 us
    ppermute x2, starting transfers between devices, body(): beside = [lax.ppermute(adj, 'rad', swap), lax.ppermute(cond, 'rad', swap)]  4.8 us
    ppermute x4, starting transfers between devices, some_rows(): return (lax.ppermute(mate, axes, pairs), lax.ppermute(next_, axes, links))  2.57 us
    ppermute x2, waiting for transfers between devices, body(): beside = [lax.ppermute(adj, 'rad', swap), lax.ppermute(cond, 'rad', swap)]  1.16 us
    ppermute x2, waiting for transfers between devices, beside_rows(): return (lax.ppermute(mate, axes, pairs), lax.ppermute(next_, axes, links))  0.47 us
  transfers between devices with their start and end apart: 9, of which 2 were waited for; matrix products, arithmetic and copies ran while one was open for 0% of the time, Pallas kernels for 32%

profile of v5, /device:TPU:0, one launch (start us, length us, event | category | flops | bytes accessed | tf_op | source)
XLA Modules:
  0.0 22.7 jit_solution(3001275058828567979)
XLA Ops:
  0.0 3.0 %collective-permute-start = (f32[1,7,1,8,1536]{4,3,2,1,0:T(8,128)}, f32[1,7,1,8,1536]{4,3,2,1,0:T(8,128)}, u32[]{:S(2)}, u32[]{:S(2)}) collective-permute-start(f32[1,7,1,8,1536]{4,3,2,1,0:T(8,128)} %refs_0_.1), channel_id=1, source_target_pairs={{0,8},{8,0},{1,9},{9,1},{2,10},{10,2},{3,11},{11,3},{4,12},{12,4},... | collective-permute-start | bytes 1032200 | tf_op jit(solution)/shard_map/ppermute | solution.py:565
  3.0 2.2 %shard_map.111 = (f32[32,8,128]{2,1,0:T(8,128)}, f32[8,1536]{1,0:T(8,128)}, f32[8,1536]{1,0:T(8,128)}) custom-call(f32[1,7,1,8,1536]{4,3,2,1,0:T(8,128)} %refs_0_.1, f32[1,1,8,1536]{3,2,1,0:T(8,128)} %cond.7, f32[7]{0:T(128)} %refs_2_.1, s32[1,256]{1,0:T(1,128)} %bitcast.10, s32[1,1,4,256]{3,2,1,0:T(4,128)} %refs_4_.2, f32[1,1,4,256]{3,2,1,0:T(4,128)} %refs_5_.2, ...), custom_call_target="tpu_custom_call" | custom-call | tf_op jit(solution)/shard_map/pallas_call | solution.py:547
  5.1 0.0 copy-start.1
  5.2 0.0 copy-start.8
  5.2 0.0 copy-start.7
  5.2 4.9 %all-to-all-start = ((f32[32,8,128]{2,1,0:T(8,128)}), f32[32,8,128]{2,1,0:T(8,128)S(1)}, u32[]{:S(2)}, u32[]{:S(2)}) async-start(f32[32,8,128]{2,1,0:T(8,128)} %get-tuple-element.16), calls=%async_computation | async-start | bytes 262144 | tf_op jit(solution)/shard_map/all_to_all | solution.py:581
  10.1 0.0 copy-done.1
  10.1 1.8 %collective-permute-start.1 = (f32[1,1,8,1536]{3,2,1,0:T(8,128)S(1)}, f32[1,1,8,1536]{3,2,1,0:T(8,128)S(1)}, u32[]{:S(2)}, u32[]{:S(2)}) collective-permute-start(f32[1,1,8,1536]{3,2,1,0:T(8,128)S(1)} %copy-done.1), channel_id=1, source_target_pairs={{0,8},{8,0},{1,9},{9,1},{2,10},{10,2},{3,11},{11,3},{4,12},{12,4},... | collective-permute-start | bytes 147464 | tf_op jit(solution)/shard_map/ppermute | solution.py:565
  11.9 0.0 copy-done.8
  11.9 0.0 collective-permute-start.2
  11.9 0.0 copy-done.7
  11.9 0.0 copy-start
  12.0 0.3 %collective-permute-start.3 = (f32[8,1536]{1,0:T(8,128)S(1)}, f32[8,1536]{1,0:T(8,128)S(1)}, u32[]{:S(2)}, u32[]{:S(2)}) collective-permute-start(f32[8,1536]{1,0:T(8,128)S(1)} %copy-done.7), channel_id=1, source_target_pairs={{0,8},{1,2},{2,1},{3,4},{4,3},{5,6},{6,5},{7,15},{8,0},{9,10},{10,... | collective-permute-start | bytes 147464 | tf_op jit(solution)/shard_map/ppermute | solution.py:526
  12.3 0.0 collective-permute-done.adj2
  12.3 0.0 copy-start.3
  12.3 1.0 %shard_map.109.refs_0_ = f32[7,8,1536]{2,1,0:T(8,128)S(1)} custom-call(f32[1,7,1,8,1536]{4,3,2,1,0:T(8,128)} %collective-permute-done.adj2), custom_call_target="tpu_custom_call" | custom-call | bytes 16777216 | tf_op jit(solution)/shard_map/pallas_call | solution.py:547
  13.3 0.0 copy-start.2
  13.3 1.2 %collective-permute-done.1.refs_1_.refs_0_ = f32[1,1,8,1536]{3,2,1,0:T(8,128)S(1)} collective-permute-done((f32[1,1,8,1536]{3,2,1,0:T(8,128)S(1)}, f32[1,1,8,1536]{3,2,1,0:T(8,128)S(1)}, u32[]{:S(2)}, u32[]{:S(2)}) %collective-permute-start.1) | collective-permute-done | bytes 49184 | tf_op jit(solution)/shard_map/ppermute | solution.py:565
  14.5 0.0 copy-done
  14.5 0.0 copy-done.3
  14.5 0.0 copy-done.2
  14.5 1.3 %shard_map.110 = (f32[7,8,1536]{2,1,0:T(8,128)S(1)}, f32[16,1536]{1,0:T(8,128)S(1)}, f32[16,1536]{1,0:T(8,128)S(1)}) custom-call(f32[1,7,1,8,1536]{4,3,2,1,0:T(8,128)S(1)} %copy-done, f32[1,1,8,1536]{3,2,1,0:T(8,128)S(1)} %copy-done.1, f32[7,8,1536]{2,1,0:T(8,128)S(1)} %shard_map.109.refs_0_, f32[1,1,8,1536]{3,2,1,0:T(8,128)S(1)} %collective-permute-done.1.refs_1_.refs_0_, ...), custom_call_target="tpu_custom_call" | custom-call | tf_op jit(solution)/shard_map/pallas_call | solution.py:547
  15.8 0.0 collective-permute-done.2.refs_1_.mate_row
  15.8 0.5 %collective-permute-done.3.refs_2_.next_row = f32[8,1536]{1,0:T(8,128)S(1)} collective-permute-done((f32[8,1536]{1,0:T(8,128)S(1)}, f32[8,1536]{1,0:T(8,128)S(1)}, u32[]{:S(2)}, u32[]{:S(2)}) %collective-permute-start.3) | collective-permute-done | bytes 49184 | tf_op jit(solution)/shard_map/ppermute | solution.py:526
  16.2 0.2 shard_map.113
  16.4 0.5 %collective-permute-start.4 = (f32[16,1536]{1,0:T(8,128)S(1)}, f32[16,1536]{1,0:T(8,128)S(1)}, u32[]{:S(2)}, u32[]{:S(2)}) collective-permute-start(f32[16,1536]{1,0:T(8,128)S(1)} %get-tuple-element.21.mate_in), channel_id=1, source_target_pairs={{0,1},{1,0},{2,3},{3,2},{4,5},{5,4},{6,7},{7,6},{8,9},{9,8},{10,11... | collective-permute-start | bytes 294920 | tf_op jit(solution)/shard_map/ppermute | solution.py:543
  16.9 1.5 %collective-permute-start.5 = (f32[16,1536]{1,0:T(8,128)S(1)}, f32[16,1536]{1,0:T(8,128)S(1)}, u32[]{:S(2)}, u32[]{:S(2)}) collective-permute-start(f32[16,1536]{1,0:T(8,128)S(1)} %get-tuple-element.22.next_in), channel_id=1, source_target_pairs={{0,16},{1,2},{2,1},{3,4},{4,3},{5,6},{6,5},{7,23},{8,9},{9,8},{10,... | collective-permute-start | bytes 294920 | tf_op jit(solution)/shard_map/ppermute | solution.py:543
  18.4 0.0 all-to-all-done
  18.4 0.0 copy-start.5
  18.4 0.0 copy-start.6
  18.5 0.0 copy-start.4
  18.5 0.3 %collective-permute-start.7 = (f32[15,1536]{1,0:T(8,128)S(1)}, f32[15,1536]{1,0:T(8,128)S(1)}, u32[]{:S(2)}, u32[]{:S(2)}) collective-permute-start(f32[15,1536]{1,0:T(8,128)S(1)} %get-tuple-element.24), channel_id=1, source_target_pairs={{0,1},{1,0},{2,3},{3,2},{4,5},{5,4},{6,7},{7,6},{8,24},{9,10},{10,... | collective-permute-start | bytes 276488 | tf_op jit(solution)/shard_map/ppermute | solution.py:543
  18.7 0.3 %collective-permute-start.6 = (f32[14,1536]{1,0:T(8,128)S(1)}, f32[14,1536]{1,0:T(8,128)S(1)}, u32[]{:S(2)}, u32[]{:S(2)}) collective-permute-start(f32[14,1536]{1,0:T(8,128)S(1)} %get-tuple-element.23), channel_id=1, source_target_pairs={{0,1},{1,0},{2,3},{3,2},{4,5},{5,4},{6,7},{7,6},{8,9},{9,8},{10,11... | collective-permute-start | bytes 258056 | tf_op jit(solution)/shard_map/ppermute | solution.py:543
  19.1 0.0 copy-done.5
  19.1 0.0 copy-done.6
  19.1 0.0 copy-done.4
  19.2 2.5 %shard_map.112.late = f32[7,8,1536]{2,1,0:T(8,128)S(1)} custom-call(f32[7,8,1536]{2,1,0:T(8,128)S(1)} %get-tuple-element.15.early, f32[256,128]{1,0:T(8,128)S(1)} %bitcast.4, f32[1,1,8,1536]{3,2,1,0:T(8,128)S(1)} %copy-done.1, f32[1,1,8,1536]{3,2,1,0:T(8,128)S(1)} %collective-permute-done.1.refs_1_.refs_0_, ...), custom_call_target="tpu_custom_call" | custom-call | tf_op jit(solution)/shard_map/pallas_call | solution.py:547
  21.7 0.0 collective-permute-done.6.refs_3_
  21.7 0.0 collective-permute-done.7.refs_4_
  21.7 0.0 collective-permute-done.4.refs_1_
  21.7 0.0 collective-permute-done.5.refs_2_
  21.7 0.9 %shard_map.115 = f32[1,7,1,8,1536]{4,3,2,1,0:T(8,128)} custom-call(f32[7,8,1536]{2,1,0:T(8,128)S(1)} %shard_map.112.late, f32[1,1,8,1536]{3,2,1,0:T(8,128)S(1)} %collective-permute-done.1.refs_1_.refs_0_, f32[16,1536]{1,0:T(8,128)S(1)} %collective-permute-done.4.refs_1_, f32[16,1536]{1,0:T(8,128)S(1)} %collective-permute-done.5.refs_2_, ...), custom_call_target="tpu_custom_call" | custom-call | tf_op jit(solution)/shard_map/pallas_call | solution.py:547
  (1 shorter events, 0.0 us)
Async XLA Ops:
  0.0 12.3 %collective-permute-start = (f32[1,7,1,8,1536]{4,3,2,1,0:T(8,128)}, f32[1,7,1,8,1536]{4,3,2,1,0:T(8,128)}, u32[]{:S(2)}, u32[]{:S(2)}) collective-permute-start(f32[1,7,1,8,1536]{4,3,2,1,0:T(8,128)} %refs_0_.1), channel_id=1, source_target_pairs={{0,8},{8,0},{1,9},{9,1},{2,10},{10,2},{3,11},{11,3},{4,12},{12,4},... | collective-permute-start | bytes 1032200 | tf_op jit(solution)/shard_map/ppermute | solution.py:565
  5.1 4.9 %copy-start.1 = (f32[1,1,8,1536]{3,2,1,0:T(8,128)S(1)}, f32[1,1,8,1536]{3,2,1,0:T(8,128)}, u32[]{:S(2)}) copy-start(f32[1,1,8,1536]{3,2,1,0:T(8,128)} %cond.7) | copy-start | bytes 147460
  5.2 6.8 %copy-start.8 = (f32[8,1536]{1,0:T(8,128)S(1)}, f32[8,1536]{1,0:T(8,128)}, u32[]{:S(2)}) copy-start(f32[8,1536]{1,0:T(8,128)} %get-tuple-element.17) | copy-start | bytes 147460
  5.2 6.8 %copy-start.7 = (f32[8,1536]{1,0:T(8,128)S(1)}, f32[8,1536]{1,0:T(8,128)}, u32[]{:S(2)}) copy-start(f32[8,1536]{1,0:T(8,128)} %get-tuple-element.18) | copy-start | bytes 147460
  5.2 13.2 %all-to-all-start = ((f32[32,8,128]{2,1,0:T(8,128)}), f32[32,8,128]{2,1,0:T(8,128)S(1)}, u32[]{:S(2)}, u32[]{:S(2)}) async-start(f32[32,8,128]{2,1,0:T(8,128)} %get-tuple-element.16), calls=%async_computation | async-start | bytes 262144 | tf_op jit(solution)/shard_map/all_to_all | solution.py:581
  10.1 4.4 %collective-permute-start.1 = (f32[1,1,8,1536]{3,2,1,0:T(8,128)S(1)}, f32[1,1,8,1536]{3,2,1,0:T(8,128)S(1)}, u32[]{:S(2)}, u32[]{:S(2)}) collective-permute-start(f32[1,1,8,1536]{3,2,1,0:T(8,128)S(1)} %copy-done.1), channel_id=1, source_target_pairs={{0,8},{8,0},{1,9},{9,1},{2,10},{10,2},{3,11},{11,3},{4,12},{12,4},... | collective-permute-start | bytes 147464 | tf_op jit(solution)/shard_map/ppermute | solution.py:565
  11.9 3.8 %collective-permute-start.2 = (f32[8,1536]{1,0:T(8,128)S(1)}, f32[8,1536]{1,0:T(8,128)S(1)}, u32[]{:S(2)}, u32[]{:S(2)}) collective-permute-start(f32[8,1536]{1,0:T(8,128)S(1)} %copy-done.8), channel_id=1, source_target_pairs={{0,1},{1,0},{2,3},{3,2},{4,5},{5,4},{6,7},{7,6},{8,9},{9,8},{10,11... | collective-permute-start | bytes 147464 | tf_op jit(solution)/shard_map/ppermute | solution.py:526
  11.9 2.5 %copy-start = (f32[1,7,1,8,1536]{4,3,2,1,0:T(8,128)S(1)}, f32[1,7,1,8,1536]{4,3,2,1,0:T(8,128)}, u32[]{:S(2)}) copy-start(f32[1,7,1,8,1536]{4,3,2,1,0:T(8,128)} %refs_0_.1) | copy-start | bytes 1032196
  12.0 4.3 %collective-permute-start.3 = (f32[8,1536]{1,0:T(8,128)S(1)}, f32[8,1536]{1,0:T(8,128)S(1)}, u32[]{:S(2)}, u32[]{:S(2)}) collective-permute-start(f32[8,1536]{1,0:T(8,128)S(1)} %copy-done.7), channel_id=1, source_target_pairs={{0,8},{1,2},{2,1},{3,4},{4,3},{5,6},{6,5},{7,15},{8,0},{9,10},{10,... | collective-permute-start | bytes 147464 | tf_op jit(solution)/shard_map/ppermute | solution.py:526
  12.3 2.2 %copy-start.3 = (f32[7,7]{1,0:T(8,128)S(1)}, f32[7,7]{1,0:T(8,128)}, u32[]{:S(2)}) copy-start(f32[7,7]{1,0:T(8,128)} %refs_4_.3) | copy-start | bytes 592
  13.3 1.2 %copy-start.2 = (f32[7]{0:T(128)S(1)}, f32[7]{0:T(128)}, u32[]{:S(2)}) copy-start(f32[7]{0:T(128)} %refs_2_.1) | copy-start | bytes 88
  16.4 5.3 %collective-permute-start.4 = (f32[16,1536]{1,0:T(8,128)S(1)}, f32[16,1536]{1,0:T(8,128)S(1)}, u32[]{:S(2)}, u32[]{:S(2)}) collective-permute-start(f32[16,1536]{1,0:T(8,128)S(1)} %get-tuple-element.21.mate_in), channel_id=1, source_target_pairs={{0,1},{1,0},{2,3},{3,2},{4,5},{5,4},{6,7},{7,6},{8,9},{9,8},{10,11... | collective-permute-start | bytes 294920 | tf_op jit(solution)/shard_map/ppermute | solution.py:543
  16.9 4.8 %collective-permute-start.5 = (f32[16,1536]{1,0:T(8,128)S(1)}, f32[16,1536]{1,0:T(8,128)S(1)}, u32[]{:S(2)}, u32[]{:S(2)}) collective-permute-start(f32[16,1536]{1,0:T(8,128)S(1)} %get-tuple-element.22.next_in), channel_id=1, source_target_pairs={{0,16},{1,2},{2,1},{3,4},{4,3},{5,6},{6,5},{7,23},{8,9},{9,8},{10,... | collective-permute-start | bytes 294920 | tf_op jit(solution)/shard_map/ppermute | solution.py:543
  18.4 0.7 %copy-start.5 = (s32[2,4,64]{2,1,0:T(4,128)S(1)}, s32[2,4,64]{2,1,0:T(4,128)}, u32[]{:S(2)}) copy-start(s32[2,4,64]{2,1,0:T(4,128)} %refs_6_.3) | copy-start | bytes 6148
  18.4 0.7 %copy-start.6 = (f32[2,4,64]{2,1,0:T(4,128)S(1)}, f32[2,4,64]{2,1,0:T(4,128)}, u32[]{:S(2)}) copy-start(f32[2,4,64]{2,1,0:T(4,128)} %refs_7_.1) | copy-start | bytes 6148
  18.5 0.7 %copy-start.4 = (s32[2,4,64]{2,1,0:T(4,128)S(1)}, s32[2,4,64]{2,1,0:T(4,128)}, u32[]{:S(2)}) copy-start(s32[2,4,64]{2,1,0:T(4,128)} %refs_5_.3) | copy-start | bytes 6148
  18.5 3.2 %collective-permute-start.7 = (f32[15,1536]{1,0:T(8,128)S(1)}, f32[15,1536]{1,0:T(8,128)S(1)}, u32[]{:S(2)}, u32[]{:S(2)}) collective-permute-start(f32[15,1536]{1,0:T(8,128)S(1)} %get-tuple-element.24), channel_id=1, source_target_pairs={{0,1},{1,0},{2,3},{3,2},{4,5},{5,4},{6,7},{7,6},{8,24},{9,10},{10,... | collective-permute-start | bytes 276488 | tf_op jit(solution)/shard_map/ppermute | solution.py:543
  18.7 2.9 %collective-permute-start.6 = (f32[14,1536]{1,0:T(8,128)S(1)}, f32[14,1536]{1,0:T(8,128)S(1)}, u32[]{:S(2)}, u32[]{:S(2)}) collective-permute-start(f32[14,1536]{1,0:T(8,128)S(1)} %get-tuple-element.23), channel_id=1, source_target_pairs={{0,1},{1,0},{2,3},{3,2},{4,5},{5,4},{6,7},{7,6},{8,9},{9,8},{10,11... | collective-permute-start | bytes 258056 | tf_op jit(solution)/shard_map/ppermute | solution.py:543

commit v6 on v5

--- a/solution.py
+++ b/solution.py
@@ -39,6 +39,22 @@
 
 def iota(shape, dim):
     return lax.broadcasted_iota(jnp.int32, shape, dim)
+
+
+def tall(row, height):
+    tile = jnp.broadcast_to(row, (16, row.shape[1])).astype(BF16)
+    return jnp.concatenate([tile] * (height // 16), axis=0)
+
+
+def matches(row, height):
+    return iota((height, row.shape[1]), 0).astype(F32).astype(BF16) == tall(row.astype(F32), height)
+
+
+def onehot(index, height):
+    within = matches(jnp.maximum(index, 0) % LANES, LANES)
+    nothing = jnp.zeros(within.shape, BF16)
+    blocks = [jnp.where(within, tall((index // LANES == k).astype(F32), LANES), nothing) for k in range(height // LANES)]
+    return jnp.concatenate(blocks, axis=0)
 
 
 class Sizes:
@@ -93,15 +109,13 @@
     col = where - row * z.cols
     full_row = owner * z.rows + row
     edge_at = jnp.where(col == 0, full_row, jnp.where(col == z.cols - 1, z.total_rows + full_row, -1))
-    hits = jnp.concatenate(
-        [(iota((z.edge, z.count), 0) == edge_at[s : s + 1]).astype(F32) for s in range(POINTS)], axis=1
-    )
+    hits = onehot(jnp.concatenate([edge_at[s : s + 1] for s in range(POINTS)], axis=1), z.edge)
     value = jnp.concatenate([mis[1:2] * weight[s : s + 1] for s in range(POINTS)], axis=1)
-    edge_force = joint_dot(value, hits.astype(BF16), 3, NT_DIMS)
+    edge_force = joint_dot(value, hits, 3, NT_DIMS)
 
     rank = jnp.sum(ranks * mine, axis=0, keepdims=True)
     place = owner * LANES + rank.astype(jnp.int32)
-    spread = (iota((z.tiles * LANES, z.count), 0) == place).astype(F32).astype(BF16)
+    spread = onehot(place, z.tiles * LANES)
     code = ((col // LOW) * z.rows + row) * LOW + col % LOW
     code = code.astype(F32)
     feats = []
@@ -237,20 +251,19 @@
 def dealt(z, values, highs, lows, height, spread_a, spread_b):
     width = spread_b.shape[0]
     sources = highs[0].shape[0]
-    used = 2 * len(values[0]) * height
-    sub_high = iota((height, LANES), 0)
-    sub_low = iota((width, LANES), 0)
+    zero, one = jnp.zeros((height, LANES), BF16), jnp.ones((width, LANES), BF16)
     for h in range(z.npr):
         parts = []
         for value in values[h]:
             parts += [part.astype(F32) for part in parts_of(value, 2)]
         for n in range(sources):
             at = (n * z.npr + h) * LANES
-            hit = sub_high == highs[h][n : n + 1]
+            hit = matches(highs[h][n : n + 1], height)
             for k, part in enumerate(parts):
-                spread_a[k * height : (k + 1) * height, at : at + LANES] = jnp.where(hit, part[n : n + 1], 0.0).astype(BF16)
-            spread_b[:, at : at + LANES] = (sub_low == lows[h][n : n + 1]).astype(F32).astype(BF16)
-    grid = lax.dot_general(spread_a[:used, :], spread_b[...], NT_DIMS, preferred_element_type=F32)
+                spread_a[k * height : (k + 1) * height, at : at + LANES] = jnp.where(hit, tall(part[n : n + 1], height), zero)
+            hit = matches(lows[h][n : n + 1], width)
+            spread_b[:, at : at + LANES] = jnp.where(hit, one, jnp.zeros_like(one))
+    grid = lax.dot_general(spread_a[...], spread_b[...], NT_DIMS, preferred_element_type=F32)
     return [
         grid[2 * k * height : (2 * k + 1) * height] + grid[(2 * k + 1) * height : (2 * k + 2) * height]
         for k in range(len(values[0]))
@@ -271,7 +284,7 @@
 def deposit_ends(z, recv, panel, spread_a, spread_b):
     weights, codes, misfits = observed(z, recv, panel)
     values = [[misfits[1] * weight] for weight in weights]
-    chunks = z.cols // LANES
+    chunks = -(-z.cols // LANES // 16) * 16
     highs, lows = [], []
     for code in codes:
         row = (code // LOW) % z.rows
@@ -280,7 +293,7 @@
         highs.append(jnp.where(row == 0, chunk, end))
         lows.append(code % LANES)
     (both,) = dealt(z, values, highs, lows, 2 * chunks, spread_a, spread_b)
-    ends = [[both[e * chunks + k : e * chunks + k + 1] for k in range(chunks)] for e in range(2)]
+    ends = [[both[e * chunks + k : e * chunks + k + 1] for k in range(z.cols // LANES)] for e in range(2)]
     return [jnp.concatenate(end, axis=1) for end in ends]
 
 
@@ -416,9 +429,9 @@
     for q in range(z.stencil):
         last_one = jnp.where(g_col[q] == z.cols - 1, z.total_rows + g_row[q], -1)
         targets.append(jnp.where(g_col[q] == 0, g_row[q], last_one))
-    hits = (iota((z.edge, z.stencil * z.edge), 0) == jnp.concatenate(targets, axis=1)).astype(F32)
+    hits = onehot(jnp.concatenate(targets, axis=1), z.edge)
     values = jnp.concatenate([home_s * g_wt[q] for q in range(z.stencil)], axis=1)
-    rim_ghost = joint_dot(values, hits.astype(BF16), 3, NT_DIMS)
+    rim_ghost = joint_dot(values, hits, 3, NT_DIMS)
     sources = z.rads * z.tiles
     pulse = []
     for k in range(z.edge_rows):
@@ -442,7 +455,7 @@
         )
     stacked = jnp.concatenate(stacked, axis=0)
     spots = jnp.concatenate(g_col, axis=1)
-    columns = (iota((z.cols, z.stencil * z.edge), 0) == spots).astype(F32).astype(BF16)
+    columns = onehot(spots, z.cols)
     ghost = joint_dot(stacked, columns, 2, NT_DIMS)
 
     def ghost_of(step, f):
@@ -527,20 +540,28 @@
 
 
 def some_rows(z, mate, next_, outer):
-    pairs, links = [], []
+    def at(panel, rad, tile):
+        return (panel * z.rads + rad) * z.tiles + tile
+
+    last, below = z.rads - 1, z.rads - 2
+    pairs, links = [], {}
     for panel in range(z.panels):
         for rad in range(z.rads):
-            at = (panel * z.rads + rad) * z.tiles
             for i in range(z.tiles):
-                pairs.append((at + i, at + (i ^ 1)))
-                if (rad == z.rads - 1) != outer:
-                    links.append((at + i, at + (i ^ 1)))
+                pairs.append((at(panel, rad, i), at(panel, rad, i ^ 1)))
+                if (rad == last) != outer:
+                    links[at(panel, rad, i)] = at(panel, rad, i ^ 1)
                 elif 0 < i < z.tiles - 1:
-                    links.append((at + i, at + (i + 1 if i % 2 else i - 1)))
+                    links[at(panel, rad, i)] = at(panel, rad, i + 1 if i % 2 else i - 1)
                 else:
-                    links.append((at + i, ((panel ^ 1) * z.rads + rad) * z.tiles + i))
+                    links[at(panel, rad, i)] = at(panel ^ 1, rad, i)
+    for end in (0, z.tiles - 1):
+        for panel in range(0 if outer else z.panels):
+            ring = [at(panel, below, end), at(panel, last, end ^ 1), at(panel, last, end)]
+            for n, source in enumerate(ring):
+                links[source] = ring[(n + 1) % len(ring)]
     axes = ("panel", "rad", "ang")
-    return lax.ppermute(mate, axes, pairs), lax.ppermute(next_, axes, links)
+    return lax.ppermute(mate, axes, pairs), lax.ppermute(next_, axes, list(links.items()))
 
 
 def call(kernel, shapes, scratch, args, spaces=pltpu.VMEM, room=48, aliases=None, cost=0):
@@ -601,7 +622,7 @@
     )
     beyond = list(some_rows(z, *links, outer=False))
     points = z.rads * z.tiles * z.npr * LANES
-    ends = 2 * z.cols // LANES
+    ends = 2 * (-(-z.cols // LANES // 16) * 16)
     ends = call(
         functools.partial(ends_kernel, z),
         [(z.fields * (2 if z.pair else 1) + spare, z.cols) for spare in range(2)],

time: 22.9 us -> 22.8 us (level)
  waiting for transfers between devices: 1.64 us -> 2.24 us
  starting transfers between devices: 12.6 us -> 12.1 us
  Pallas kernels: 8.12 us -> 7.84 us
    ppermute x4, starting transfers between devices: 2.57 us -> 2.11 us  [the longest x2 1.4 us: some_rows(): lax.ppermute(next_, axes, list(links.items()))]
    all_to_all x1, waiting for transfers between devices: 0.01 us -> 0.33 us  [body(): lax.all_to_all(pay, ('panel', 'rad', 'ang'), split_axis=0, concat_axis=0,...]
    pallas_call x7, Pallas kernels: 8.12 us -> 7.84 us  [call(): pl.pallas_call(kernel, out_shape=[jax.ShapeDtypeStruct(shape, F32) for sh...]
    ppermute x4, waiting for transfers between devices: 0.01 us -> 0.28 us  [the longest x2 0.28 us: some_rows(): lax.ppermute(next_, axes, list(links.items()))]
  transfers between devices with their start and end apart: 9 -> 9, of which waited for: 2 -> 4; matrix products, arithmetic and copies ran while one was open for 0% -> 0% of each run, Pallas kernels for 32% -> 31%
where the time goes in v6:
time: 22.8 us; the launch traced here: 22.5 us
  starting transfers between devices  12.1 us (53%)
  Pallas kernels  7.84 us (34%)
  waiting for transfers between devices  2.24 us (10%)
    pallas_call x7, Pallas kernels, call(): pl.pallas_call(kernel, out_shape=[jax.ShapeDtypeStruct(shape, F32) for sh...  7.84 us
    all_to_all x1, starting transfers between devices, body(): lax.all_to_all(pay, ('panel', 'rad', 'ang'), split_axis=0, concat_axis=0,...  4.9 us
    ppermute x2, starting transfers between devices, body(): beside = [lax.ppermute(adj, 'rad', swap), lax.ppermute(cond, 'rad', swap)]  4.8 us
    ppermute x2, starting transfers between devices, some_rows(): lax.ppermute(next_, axes, list(links.items()))  1.4 us
    ppermute x2, waiting for transfers between devices, body(): beside = [lax.ppermute(adj, 'rad', swap), lax.ppermute(cond, 'rad', swap)]  1.16 us
    ppermute x2, starting transfers between devices, some_rows(): lax.ppermute(mate, axes, pairs)  0.71 us
    ppermute x2, waiting for transfers between devices, beside_rows(): return (lax.ppermute(mate, axes, pairs), lax.ppermute(next_, axes, links))  0.47 us
  transfers between devices with their start and end apart: 9, of which 4 were waited for; matrix products, arithmetic and copies ran while one was open for 0% of the time, Pallas kernels for 31%

profile of v6, /device:TPU:0, one launch (start us, length us, event | category | flops | bytes accessed | tf_op | source)
XLA Modules:
  0.0 22.5 jit_solution(8650105995122440689)
XLA Ops:
  0.0 3.0 %collective-permute-start = (f32[1,7,1,8,1536]{4,3,2,1,0:T(8,128)}, f32[1,7,1,8,1536]{4,3,2,1,0:T(8,128)}, u32[]{:S(2)}, u32[]{:S(2)}) collective-permute-start(f32[1,7,1,8,1536]{4,3,2,1,0:T(8,128)} %refs_0_.1), channel_id=1, source_target_pairs={{0,8},{8,0},{1,9},{9,1},{2,10},{10,2},{3,11},{11,3},{4,12},{12,4},... | collective-permute-start | bytes 1032200 | tf_op jit(solution)/shard_map/ppermute | solution.py:586
  3.0 2.2 %shard_map.111 = (f32[32,8,128]{2,1,0:T(8,128)}, f32[8,1536]{1,0:T(8,128)}, f32[8,1536]{1,0:T(8,128)}) custom-call(f32[1,7,1,8,1536]{4,3,2,1,0:T(8,128)} %refs_0_.1, f32[1,1,8,1536]{3,2,1,0:T(8,128)} %cond.7, f32[7]{0:T(128)} %refs_2_.1, s32[1,256]{1,0:T(1,128)} %bitcast.10, s32[1,1,4,256]{3,2,1,0:T(4,128)} %refs_4_.2, f32[1,1,4,256]{3,2,1,0:T(4,128)} %refs_5_.2, ...), custom_call_target="tpu_custom_call" | custom-call | tf_op jit(solution)/shard_map/pallas_call | solution.py:568
  5.2 0.0 copy-start.1
  5.2 0.0 copy-start.8
  5.2 0.0 copy-start.7
  5.2 4.9 %all-to-all-start = ((f32[32,8,128]{2,1,0:T(8,128)}), f32[32,8,128]{2,1,0:T(8,128)S(1)}, u32[]{:S(2)}, u32[]{:S(2)}) async-start(f32[32,8,128]{2,1,0:T(8,128)} %get-tuple-element.16), calls=%async_computation | async-start | bytes 262144 | tf_op jit(solution)/shard_map/all_to_all | solution.py:602
  10.1 0.0 copy-done.1
  10.1 1.8 %collective-permute-start.1 = (f32[1,1,8,1536]{3,2,1,0:T(8,128)S(1)}, f32[1,1,8,1536]{3,2,1,0:T(8,128)S(1)}, u32[]{:S(2)}, u32[]{:S(2)}) collective-permute-start(f32[1,1,8,1536]{3,2,1,0:T(8,128)S(1)} %copy-done.1), channel_id=1, source_target_pairs={{0,8},{8,0},{1,9},{9,1},{2,10},{10,2},{3,11},{11,3},{4,12},{12,4},... | collective-permute-start | bytes 147464 | tf_op jit(solution)/shard_map/ppermute | solution.py:586
  11.9 0.0 copy-done.8
  11.9 0.0 collective-permute-start.2
  11.9 0.0 copy-done.7
  12.0 0.0 copy-start
  12.0 0.3 %collective-permute-start.3 = (f32[8,1536]{1,0:T(8,128)S(1)}, f32[8,1536]{1,0:T(8,128)S(1)}, u32[]{:S(2)}, u32[]{:S(2)}) collective-permute-start(f32[8,1536]{1,0:T(8,128)S(1)} %copy-done.7), channel_id=1, source_target_pairs={{0,8},{1,2},{2,1},{3,4},{4,3},{5,6},{6,5},{7,15},{8,0},{9,10},{10,... | collective-permute-start | bytes 147464 | tf_op jit(solution)/shard_map/ppermute | solution.py:539
  12.3 0.0 collective-permute-done.adj2
  12.3 0.0 copy-start.3
  12.3 1.0 %shard_map.109.refs_0_ = f32[7,8,1536]{2,1,0:T(8,128)S(1)} custom-call(f32[1,7,1,8,1536]{4,3,2,1,0:T(8,128)} %collective-permute-done.adj2), custom_call_target="tpu_custom_call" | custom-call | bytes 16777216 | tf_op jit(solution)/shard_map/pallas_call | solution.py:568
  13.3 0.0 copy-start.2
  13.3 1.2 %collective-permute-done.1.refs_1_.refs_0_ = f32[1,1,8,1536]{3,2,1,0:T(8,128)S(1)} collective-permute-done((f32[1,1,8,1536]{3,2,1,0:T(8,128)S(1)}, f32[1,1,8,1536]{3,2,1,0:T(8,128)S(1)}, u32[]{:S(2)}, u32[]{:S(2)}) %collective-permute-start.1) | collective-permute-done | bytes 49184 | tf_op jit(solution)/shard_map/ppermute | solution.py:586
  14.5 0.0 copy-done
  14.5 0.0 copy-done.3
  14.5 0.0 copy-done.2
  14.5 1.3 %shard_map.110 = (f32[7,8,1536]{2,1,0:T(8,128)S(1)}, f32[16,1536]{1,0:T(8,128)S(1)}, f32[16,1536]{1,0:T(8,128)S(1)}) custom-call(f32[1,7,1,8,1536]{4,3,2,1,0:T(8,128)S(1)} %copy-done, f32[1,1,8,1536]{3,2,1,0:T(8,128)S(1)} %copy-done.1, f32[7,8,1536]{2,1,0:T(8,128)S(1)} %shard_map.109.refs_0_, f32[1,1,8,1536]{3,2,1,0:T(8,128)S(1)} %collective-permute-done.1.refs_1_.refs_0_, ...), custom_call_target="tpu_custom_call" | custom-call | tf_op jit(solution)/shard_map/pallas_call | solution.py:568
  15.8 0.0 collective-permute-done.2.refs_1_.mate_row
  15.8 0.5 %collective-permute-done.3.refs_2_.next_row = f32[8,1536]{1,0:T(8,128)S(1)} collective-permute-done((f32[8,1536]{1,0:T(8,128)S(1)}, f32[8,1536]{1,0:T(8,128)S(1)}, u32[]{:S(2)}, u32[]{:S(2)}) %collective-permute-start.3) | collective-permute-done | bytes 49184 | tf_op jit(solution)/shard_map/ppermute | solution.py:539
  16.3 0.2 shard_map.113
  16.4 0.5 %collective-permute-start.4 = (f32[16,1536]{1,0:T(8,128)S(1)}, f32[16,1536]{1,0:T(8,128)S(1)}, u32[]{:S(2)}, u32[]{:S(2)}) collective-permute-start(f32[16,1536]{1,0:T(8,128)S(1)} %get-tuple-element.21.mate_in), channel_id=1, source_target_pairs={{0,1},{1,0},{2,3},{3,2},{4,5},{5,4},{6,7},{7,6},{8,9},{9,8},{10,11... | collective-permute-start | bytes 294920 | tf_op jit(solution)/shard_map/ppermute | solution.py:564
  16.9 1.0 %collective-permute-start.5 = (f32[16,1536]{1,0:T(8,128)S(1)}, f32[16,1536]{1,0:T(8,128)S(1)}, u32[]{:S(2)}, u32[]{:S(2)}) collective-permute-start(f32[16,1536]{1,0:T(8,128)S(1)} %get-tuple-element.22.next_in), channel_id=1, source_target_pairs={{0,9},{1,2},{2,1},{3,4},{4,3},{5,6},{6,5},{7,14},{8,0},{9,8},{10,1... | collective-permute-start | bytes 294920 | tf_op jit(solution)/shard_map/ppermute | solution.py:564
  18.0 0.3 %all-to-all-done = f32[32,8,128]{2,1,0:T(8,128)S(1)} async-done(((f32[32,8,128]{2,1,0:T(8,128)}), f32[32,8,128]{2,1,0:T(8,128)S(1)}, u32[]{:S(2)}, u32[]{:S(2)}) %all-to-all-start) | async-done | bytes 131104 | tf_op jit(solution)/shard_map/all_to_all | solution.py:602
  18.3 0.0 copy-start.5
  18.3 0.0 copy-start.6
  18.3 0.0 copy-start.4
  18.4 0.4 %collective-permute-start.7 = (f32[15,1536]{1,0:T(8,128)S(1)}, f32[15,1536]{1,0:T(8,128)S(1)}, u32[]{:S(2)}, u32[]{:S(2)}) collective-permute-start(f32[15,1536]{1,0:T(8,128)S(1)} %get-tuple-element.24), channel_id=1, source_target_pairs={{0,1},{1,0},{2,3},{3,2},{4,5},{5,4},{6,7},{7,6},{8,24},{9,10},{10,... | collective-permute-start | bytes 276488 | tf_op jit(solution)/shard_map/ppermute | solution.py:564
  18.7 0.2 collective-permute-start.6
  18.9 0.0 copy-done.5
  19.0 0.0 copy-done.6
  19.0 0.0 copy-done.4
  19.0 2.2 %shard_map.112.late = f32[7,8,1536]{2,1,0:T(8,128)S(1)} custom-call(f32[7,8,1536]{2,1,0:T(8,128)S(1)} %get-tuple-element.15.early, f32[256,128]{1,0:T(8,128)S(1)} %bitcast.4, f32[1,1,8,1536]{3,2,1,0:T(8,128)S(1)} %copy-done.1, f32[1,1,8,1536]{3,2,1,0:T(8,128)S(1)} %collective-permute-done.1.refs_1_.refs_0_, ...), custom_call_target="tpu_custom_call" | custom-call | tf_op jit(solution)/shard_map/pallas_call | solution.py:568
  21.3 0.0 collective-permute-done.6.refs_3_
  21.3 0.0 collective-permute-done.7.refs_4_
  21.3 0.0 collective-permute-done.4.refs_1_
  21.3 0.3 %collective-permute-done.5.refs_2_ = f32[16,1536]{1,0:T(8,128)S(1)} collective-permute-done((f32[16,1536]{1,0:T(8,128)S(1)}, f32[16,1536]{1,0:T(8,128)S(1)}, u32[]{:S(2)}, u32[]{:S(2)}) %collective-permute-start.5) | collective-permute-done | bytes 98336 | tf_op jit(solution)/shard_map/ppermute | solution.py:564
  21.6 0.9 %shard_map.115 = f32[1,7,1,8,1536]{4,3,2,1,0:T(8,128)} custom-call(f32[7,8,1536]{2,1,0:T(8,128)S(1)} %shard_map.112.late, f32[1,1,8,1536]{3,2,1,0:T(8,128)S(1)} %collective-permute-done.1.refs_1_.refs_0_, f32[16,1536]{1,0:T(8,128)S(1)} %collective-permute-done.4.refs_1_, f32[16,1536]{1,0:T(8,128)S(1)} %collective-permute-done.5.refs_2_, ...), custom_call_target="tpu_custom_call" | custom-call | tf_op jit(solution)/shard_map/pallas_call | solution.py:568
  (1 shorter events, 0.0 us)
Async XLA Ops:
  0.0 12.3 %collective-permute-start = (f32[1,7,1,8,1536]{4,3,2,1,0:T(8,128)}, f32[1,7,1,8,1536]{4,3,2,1,0:T(8,128)}, u32[]{:S(2)}, u32[]{:S(2)}) collective-permute-start(f32[1,7,1,8,1536]{4,3,2,1,0:T(8,128)} %refs_0_.1), channel_id=1, source_target_pairs={{0,8},{8,0},{1,9},{9,1},{2,10},{10,2},{3,11},{11,3},{4,12},{12,4},... | collective-permute-start | bytes 1032200 | tf_op jit(solution)/shard_map/ppermute | solution.py:586
  5.2 4.9 %copy-start.1 = (f32[1,1,8,1536]{3,2,1,0:T(8,128)S(1)}, f32[1,1,8,1536]{3,2,1,0:T(8,128)}, u32[]{:S(2)}) copy-start(f32[1,1,8,1536]{3,2,1,0:T(8,128)} %cond.7) | copy-start | bytes 147460
  5.2 6.8 %copy-start.8 = (f32[8,1536]{1,0:T(8,128)S(1)}, f32[8,1536]{1,0:T(8,128)}, u32[]{:S(2)}) copy-start(f32[8,1536]{1,0:T(8,128)} %get-tuple-element.17) | copy-start | bytes 147460
  5.2 6.8 %copy-start.7 = (f32[8,1536]{1,0:T(8,128)S(1)}, f32[8,1536]{1,0:T(8,128)}, u32[]{:S(2)}) copy-start(f32[8,1536]{1,0:T(8,128)} %get-tuple-element.18) | copy-start | bytes 147460
  5.2 13.1 %all-to-all-start = ((f32[32,8,128]{2,1,0:T(8,128)}), f32[32,8,128]{2,1,0:T(8,128)S(1)}, u32[]{:S(2)}, u32[]{:S(2)}) async-start(f32[32,8,128]{2,1,0:T(8,128)} %get-tuple-element.16), calls=%async_computation | async-start | bytes 262144 | tf_op jit(solution)/shard_map/all_to_all | solution.py:602
  10.1 4.4 %collective-permute-start.1 = (f32[1,1,8,1536]{3,2,1,0:T(8,128)S(1)}, f32[1,1,8,1536]{3,2,1,0:T(8,128)S(1)}, u32[]{:S(2)}, u32[]{:S(2)}) collective-permute-start(f32[1,1,8,1536]{3,2,1,0:T(8,128)S(1)} %copy-done.1), channel_id=1, source_target_pairs={{0,8},{8,0},{1,9},{9,1},{2,10},{10,2},{3,11},{11,3},{4,12},{12,4},... | collective-permute-start | bytes 147464 | tf_op jit(solution)/shard_map/ppermute | solution.py:586
  11.9 3.8 %collective-permute-start.2 = (f32[8,1536]{1,0:T(8,128)S(1)}, f32[8,1536]{1,0:T(8,128)S(1)}, u32[]{:S(2)}, u32[]{:S(2)}) collective-permute-start(f32[8,1536]{1,0:T(8,128)S(1)} %copy-done.8), channel_id=1, source_target_pairs={{0,1},{1,0},{2,3},{3,2},{4,5},{5,4},{6,7},{7,6},{8,9},{9,8},{10,11... | collective-permute-start | bytes 147464 | tf_op jit(solution)/shard_map/ppermute | solution.py:539
  12.0 2.5 %copy-start = (f32[1,7,1,8,1536]{4,3,2,1,0:T(8,128)S(1)}, f32[1,7,1,8,1536]{4,3,2,1,0:T(8,128)}, u32[]{:S(2)}) copy-start(f32[1,7,1,8,1536]{4,3,2,1,0:T(8,128)} %refs_0_.1) | copy-start | bytes 1032196
  12.0 4.3 %collective-permute-start.3 = (f32[8,1536]{1,0:T(8,128)S(1)}, f32[8,1536]{1,0:T(8,128)S(1)}, u32[]{:S(2)}, u32[]{:S(2)}) collective-permute-start(f32[8,1536]{1,0:T(8,128)S(1)} %copy-done.7), channel_id=1, source_target_pairs={{0,8},{1,2},{2,1},{3,4},{4,3},{5,6},{6,5},{7,15},{8,0},{9,10},{10,... | collective-permute-start | bytes 147464 | tf_op jit(solution)/shard_map/ppermute | solution.py:539
  12.3 2.2 %copy-start.3 = (f32[7,7]{1,0:T(8,128)S(1)}, f32[7,7]{1,0:T(8,128)}, u32[]{:S(2)}) copy-start(f32[7,7]{1,0:T(8,128)} %refs_4_.3) | copy-start | bytes 592
  13.3 1.2 %copy-start.2 = (f32[7]{0:T(128)S(1)}, f32[7]{0:T(128)}, u32[]{:S(2)}) copy-start(f32[7]{0:T(128)} %refs_2_.1) | copy-start | bytes 88
  16.4 4.9 %collective-permute-start.4 = (f32[16,1536]{1,0:T(8,128)S(1)}, f32[16,1536]{1,0:T(8,128)S(1)}, u32[]{:S(2)}, u32[]{:S(2)}) collective-permute-start(f32[16,1536]{1,0:T(8,128)S(1)} %get-tuple-element.21.mate_in), channel_id=1, source_target_pairs={{0,1},{1,0},{2,3},{3,2},{4,5},{5,4},{6,7},{7,6},{8,9},{9,8},{10,11... | collective-permute-start | bytes 294920 | tf_op jit(solution)/shard_map/ppermute | solution.py:564
  16.9 4.6 %collective-permute-start.5 = (f32[16,1536]{1,0:T(8,128)S(1)}, f32[16,1536]{1,0:T(8,128)S(1)}, u32[]{:S(2)}, u32[]{:S(2)}) collective-permute-start(f32[16,1536]{1,0:T(8,128)S(1)} %get-tuple-element.22.next_in), channel_id=1, source_target_pairs={{0,9},{1,2},{2,1},{3,4},{4,3},{5,6},{6,5},{7,14},{8,0},{9,8},{10,1... | collective-permute-start | bytes 294920 | tf_op jit(solution)/shard_map/ppermute | solution.py:564
  18.3 0.7 %copy-start.5 = (s32[2,4,64]{2,1,0:T(4,128)S(1)}, s32[2,4,64]{2,1,0:T(4,128)}, u32[]{:S(2)}) copy-start(s32[2,4,64]{2,1,0:T(4,128)} %refs_6_.3) | copy-start | bytes 6148
  18.3 0.7 %copy-start.6 = (f32[2,4,64]{2,1,0:T(4,128)S(1)}, f32[2,4,64]{2,1,0:T(4,128)}, u32[]{:S(2)}) copy-start(f32[2,4,64]{2,1,0:T(4,128)} %refs_7_.1) | copy-start | bytes 6148
  18.3 0.7 %copy-start.4 = (s32[2,4,64]{2,1,0:T(4,128)S(1)}, s32[2,4,64]{2,1,0:T(4,128)}, u32[]{:S(2)}) copy-start(s32[2,4,64]{2,1,0:T(4,128)} %refs_5_.3) | copy-start | bytes 6148
  18.4 2.9 %collective-permute-start.7 = (f32[15,1536]{1,0:T(8,128)S(1)}, f32[15,1536]{1,0:T(8,128)S(1)}, u32[]{:S(2)}, u32[]{:S(2)}) collective-permute-start(f32[15,1536]{1,0:T(8,128)S(1)} %get-tuple-element.24), channel_id=1, source_target_pairs={{0,1},{1,0},{2,3},{3,2},{4,5},{5,4},{6,7},{7,6},{8,24},{9,10},{10,... | collective-permute-start | bytes 276488 | tf_op jit(solution)/shard_map/ppermute | solution.py:564
  18.7 2.5 %collective-permute-start.6 = (f32[14,1536]{1,0:T(8,128)S(1)}, f32[14,1536]{1,0:T(8,128)S(1)}, u32[]{:S(2)}, u32[]{:S(2)}) collective-permute-start(f32[14,1536]{1,0:T(8,128)S(1)} %get-tuple-element.23), channel_id=1, source_target_pairs={{0,1},{1,0},{2,3},{3,2},{4,5},{5,4},{6,7},{7,6},{8,9},{9,8},{10,11... | collective-permute-start | bytes 258056 | tf_op jit(solution)/shard_map/ppermute | solution.py:564

commit v7 on v6

--- a/solution.py
+++ b/solution.py
@@ -317,27 +317,37 @@
     out[...] = adj2[0, :, 0]
 
 
-def early_kernel(z, adj, cond, *refs):
+def lone_kernel(z, adj, cond, *refs):
     if z.pair:
-        adj2, cond2, steps, couple, out, mate, next_, own, far = refs
+        adj2, steps, couple, first, mixed = refs
+    else:
+        steps, couple, first = refs
+    dif, mix = weights_of(z, steps, couple, z.rows, z.cols)
+    for f in range(z.fields):
+        s = adj[0, f, 0] * (cond[0, 0] * dif[f])
+        new = adj[0, f, 0] - 6.0 * s + sideways(s) + upright(s, 0.0, 0.0)
+        first[f] = new + coupled(z, mix, lambda e: adj[0, e, 0], f)
+        if z.pair:
+            mixed[f] = adj2[f] + s + coupled(z, mix, lambda e: adj2[e], f)
+
+
+def early_kernel(z, cond, first, *refs):
+    if z.pair:
+        mixed, adj2, cond2, steps, couple, out, mate, next_, own, far = refs
     else:
         beside, steps, couple, out, mate, next_, own = refs
     dif, mix = weights_of(z, steps, couple, z.rows, z.cols)
     own_c = cond[0, 0]
     far_c = cond2[0, 0] if z.pair else None
     for f in range(z.fields):
-        s = adj[0, f, 0] * (own_c * dif[f])
-        new = adj[0, f, 0] - 6.0 * s + sideways(s) + upright(s, 0.0, 0.0)
-        new = new + coupled(z, mix, lambda e: adj[0, e, 0], f)
         if z.pair:
             other = adj2[f] * (far_c * dif[f])
-            new = new + other
-            part = adj2[f] - 6.0 * other + sideways(other) + upright(other, 0.0, 0.0) + s
-            far[f] = part + coupled(z, mix, lambda e: adj2[e], f)
+            new = first[f] + other
+            far[f] = mixed[f] - 6.0 * other + sideways(other) + upright(other, 0.0, 0.0)
             at = SUBL + f
             mate[at : at + 1, :], next_[at : at + 1, :] = facing(other)
         else:
-            new = new + beside[f]
+            new = first[f] + beside[f]
         own[f] = new
         mate[f : f + 1, :], next_[f : f + 1, :] = facing(new * (own_c * dif[f]))
     for half in range(2 if z.pair else 1):
@@ -360,19 +370,21 @@
         dif = wide(steps[:, f : f + 1], 1, z.cols)
         mate[f : f + 1, :] = mate_in[f : f + 1, :] + mate_row[f : f + 1, :] * (cond_mate * dif)
         next_[f : f + 1, :] = next_in[f : f + 1, :] + next_row[f : f + 1, :] * (cond_next * dif * inner)
+        if z.pair:
+            mate[z.fields + f : z.fields + f + 1, :] = mate_in[SUBL + f : SUBL + f + 1, :]
+            next_[z.fields + f : z.fields + f + 1, :] = next_in[SUBL + f : SUBL + f + 1, :]
+    spare = next_.shape[0] - 1
+    next_[spare:, :] = jnp.zeros((1, z.cols), F32)
 
 
 def is_outer(z):
     return lax.axis_index("rad") == z.rads - 1
 
 
-def ends_kernel(z, recv, cond, steps, mate_in, next_in, mate, next_, spread_a, spread_b):
+def ends_kernel(z, recv, cond, steps, mate, next_, spread_a, spread_b):
     panel = lax.axis_index("panel")
-    next_[mate.shape[0] :, :] = jnp.zeros((next_.shape[0] - mate.shape[0], z.cols), F32)
-    for f in range(mate.shape[0]):
-        at = f % z.fields + f // z.fields * SUBL
-        mate[f : f + 1, :] = mate_in[at : at + 1, :]
-        next_[f : f + 1, :] = next_in[at : at + 1, :]
+    mate[...] = jnp.zeros_like(mate)
+    next_[...] = jnp.zeros_like(next_)
 
     @pl.when(is_outer(z))
     def _():
@@ -381,8 +393,8 @@
         top = top * weight[:1]
         bottom = bottom * weight[z.rows - 1 :]
         even = even_tile()
-        mate[3:4, :] = mate_in[3:4, :] + jnp.where(even, bottom, top)
-        next_[3:4, :] = next_in[3:4, :] + jnp.where(even, top, bottom)
+        mate[...] = jnp.where(even, bottom, top)
+        next_[:1, :] = jnp.where(even, top, bottom)
 
 
 def ghost_kernel(z, early, recv, cond, *refs):
@@ -492,24 +504,19 @@
 
 def last_kernel(z, late, *refs):
     if z.pair:
-        cond2, mate_inner, next_inner, mate_outer, next_outer, steps, out = refs
+        cond2, mate_in, next_in, mate_end, next_end, steps, out = refs
     else:
-        beside, mate_inner, next_inner, mate_outer, next_outer, steps, out = refs
-    outer = is_outer(z)
-
-    def beyond(half, f):
-        inner_at, outer_at = half * SUBL + f, half * z.fields + f
-        mate_in = jnp.where(outer, mate_outer[outer_at : outer_at + 1, :], mate_inner[inner_at : inner_at + 1, :])
-        next_in = jnp.where(outer, next_outer[outer_at : outer_at + 1, :], next_inner[inner_at : inner_at + 1, :])
-        return around(z, mate_in, next_in)
-
-    for f in range(z.fields):
-        high, low = beyond(0, f)
+        beside, mate_in, next_in, mate_end, next_end, steps, out = refs
+    above, below = around(z, mate_in[...], next_in[: mate_in.shape[0], :])
+    above_end, below_end = around(z, mate_end[...], next_end[:1, :])
+    for f in range(z.fields):
+        high, low = above[f : f + 1], below[f : f + 1]
+        if f == 3:
+            high, low = high + above_end, low + below_end
         if z.pair:
-            far_high, far_low = beyond(1, f)
             far_c = cond2[0, 0] * wide(steps[:, f : f + 1], z.rows, z.cols)
-            high = high + far_high * far_c[:1]
-            low = low + far_low * far_c[z.rows - 1 :]
+            high = high + above[z.fields + f : z.fields + f + 1] * far_c[:1]
+            low = low + below[z.fields + f : z.fields + f + 1] * far_c[z.rows - 1 :]
         new = late[f] + brim(high, low, z.rows)
         out[0, f, 0] = new if z.pair else new + beside[f]
 
@@ -524,44 +531,38 @@
     return shifted(x, axis, 1) + shifted(x, axis, -1)
 
 
-def beside_rows(z, mate, next_):
+def beside_rows(z, mate, next_, across):
     pairs, links = [], []
-    for rad in range(z.rads):
-        at = rad * z.tiles
-        other = (rad ^ 1) * z.tiles
-        for i in range(z.tiles):
-            pairs.append((at + i, at + (i ^ 1)))
-            if 0 < i < z.tiles - 1:
-                links.append((at + i, at + (i + 1 if i % 2 else i - 1)))
-            else:
-                links.append((at + i, other + i))
-    axes = ("rad", "ang")
-    return lax.ppermute(mate, axes, pairs), lax.ppermute(next_, axes, links)
-
-
-def some_rows(z, mate, next_, outer):
-    def at(panel, rad, tile):
-        return (panel * z.rads + rad) * z.tiles + tile
-
-    last, below = z.rads - 1, z.rads - 2
-    pairs, links = [], {}
     for panel in range(z.panels):
         for rad in range(z.rads):
+            at = (panel * z.rads + rad) * z.tiles
+            there = (panel ^ 1, rad) if across == "panel" else (panel, rad ^ 1)
+            other = (there[0] * z.rads + there[1]) * z.tiles
             for i in range(z.tiles):
-                pairs.append((at(panel, rad, i), at(panel, rad, i ^ 1)))
-                if (rad == last) != outer:
-                    links[at(panel, rad, i)] = at(panel, rad, i ^ 1)
+                pairs.append((at + i, at + (i ^ 1)))
+                if 0 < i < z.tiles - 1:
+                    links.append((at + i, at + (i + 1 if i % 2 else i - 1)))
+                else:
+                    links.append((at + i, other + i))
+    axes = ("panel", "rad", "ang")
+    return lax.ppermute(mate, axes, pairs), lax.ppermute(next_, axes, links)
+
+
+def outer_rows(z, mate, next_):
+    pairs, links = [], []
+    for panel in range(z.panels):
+        for rad in range(z.rads):
+            at = (panel * z.rads + rad) * z.tiles
+            for i in range(z.tiles):
+                pairs.append((at + i, at + (i ^ 1)))
+                if rad < z.rads - 1:
+                    links.append((at + i, at + (i ^ 1)))
                 elif 0 < i < z.tiles - 1:
-                    links[at(panel, rad, i)] = at(panel, rad, i + 1 if i % 2 else i - 1)
+                    links.append((at + i, at + (i + 1 if i % 2 else i - 1)))
                 else:
-                    links[at(panel, rad, i)] = at(panel ^ 1, rad, i)
-    for end in (0, z.tiles - 1):
-        for panel in range(0 if outer else z.panels):
-            ring = [at(panel, below, end), at(panel, last, end ^ 1), at(panel, last, end)]
-            for n, source in enumerate(ring):
-                links[source] = ring[(n + 1) % len(ring)]
+                    links.append((at + i, ((panel ^ 1) * z.rads + rad) * z.tiles + i))
     axes = ("panel", "rad", "ang")
-    return lax.ppermute(mate, axes, pairs), lax.ppermute(next_, axes, list(links.items()))
+    return lax.ppermute(mate, axes, pairs), lax.ppermute(next_, axes, links)
 
 
 def call(kernel, shapes, scratch, args, spaces=pltpu.VMEM, room=48, aliases=None, cost=0):
@@ -601,35 +602,41 @@
     )
     recv = lax.all_to_all(pay, ("panel", "rad", "ang"), split_axis=0, concat_axis=0, tiled=True)
     recv = recv.reshape(z.devices * z.block, LANES)
-    rows = list(beside_rows(z, *rows))
+    rows = list(beside_rows(z, *rows, "rad"))
 
     steps = diffus.reshape(1, z.fields)
     if z.pair:
         beside[:1] = call(functools.partial(far_kernel, z), [state], [], [beside[0]], cost=16 << 20)
-    args = [adj, cond] + beside + [steps, couple]
+    lone = call(
+        functools.partial(lone_kernel, z),
+        [state] * (2 if z.pair else 1),
+        [],
+        [adj, cond] + (beside[:1] if z.pair else []) + [steps, couple],
+    )
+    args = [cond, *lone] + beside + [steps, couple]
     early, mate, next_, *first = call(
         functools.partial(early_kernel, z),
         [state, lines, lines] + ([] if z.pair else [state]),
         [pltpu.VMEM(state, F32)] * (2 if z.pair else 0),
         args,
     )
+    beyond_rows = z.fields * (2 if z.pair else 1)
     links = call(
         functools.partial(link_kernel, z),
-        [lines, lines],
+        [(beyond_rows, z.cols), (beyond_rows + 1, z.cols)],
         [],
         [cond, steps] + rows + [mate, next_],
-        aliases={4: 0, 5: 1},
-    )
-    beyond = list(some_rows(z, *links, outer=False))
+    )
+    beyond = list(beside_rows(z, *links, "rad"))
     points = z.rads * z.tiles * z.npr * LANES
     ends = 2 * (-(-z.cols // LANES // 16) * 16)
     ends = call(
         functools.partial(ends_kernel, z),
-        [(z.fields * (2 if z.pair else 1) + spare, z.cols) for spare in range(2)],
+        [(1, z.cols), (2, z.cols)],
         [pltpu.VMEM((2 * ends, points), BF16), pltpu.VMEM((LANES, points), BF16)],
-        [recv, cond, steps, *links],
-    )
-    beyond += some_rows(z, *ends, outer=True)
+        [recv, cond, steps],
+    )
+    beyond += outer_rows(z, *ends)
     args = [early, recv, cond] + far + rows + [steps, couple]
     late, *added = call(
         functools.partial(ghost_kernel, z),

time: 22.8 us -> 22.5 us (0.987)
  waiting for transfers between devices: 2.24 us -> 1.45 us
  local copies, waits for them, and re-layouts: 0.14 us -> 0.79 us
    ppermute x4 -> x2, starting transfers between devices: 2.11 us -> 0.58 us  [outer_rows(): return (lax.ppermute(mate, axes, pairs), lax.ppermute(next_, axes, links))]
    ppermute x2 -> x4, starting transfers between devices: 0.32 us -> 1.6 us  [beside_rows(): return (lax.ppermute(mate, axes, pairs), lax.ppermute(next_, axes, links))]
    ppermute x2, waiting for transfers between devices: 1.16 us -> 0.01 us  [body(): beside = [lax.ppermute(adj, 'rad', swap), lax.ppermute(cond, 'rad', swap)]]
    unnamed x18, local copies, waits for them, and re-layouts: 0.14 us -> 0.79 us
    ppermute x2 -> x4, waiting for transfers between devices: 0.47 us -> 0.85 us  [beside_rows(): return (lax.ppermute(mate, axes, pairs), lax.ppermute(next_, axes, links))]
    ppermute x4 -> x2, waiting for transfers between devices: 0.28 us -> 0.01 us  [outer_rows(): return (lax.ppermute(mate, axes, pairs), lax.ppermute(next_, axes, links))]
    all_to_all x1, waiting for transfers between devices: 0.33 us -> 0.59 us  [body(): lax.all_to_all(pay, ('panel', 'rad', 'ang'), split_axis=0, concat_axis=0,...]
    pallas_call x7 -> x8, Pallas kernels: 7.84 us -> 7.95 us  [call(): pl.pallas_call(kernel, out_shape=[jax.ShapeDtypeStruct(shape, F32) for sh...]
  transfers between devices with their start and end apart: 9 -> 9, of which waited for: 4 -> 2; matrix products, arithmetic and copies ran while one was open for 0% -> 0% of each run, Pallas kernels for 31% -> 31%
where the time goes in v7:
time: 22.5 us; the launch traced here: 22.2 us
  starting transfers between devices  11.9 us (53%)
  Pallas kernels  7.95 us (35%)
  waiting for transfers between devices  1.45 us (6%)
  local copies, waits for them, and re-layouts  0.79 us (4%)
    pallas_call x8, Pallas kernels, call(): pl.pallas_call(kernel, out_shape=[jax.ShapeDtypeStruct(shape, F32) for sh...  7.95 us
    all_to_all x1, starting transfers between devices, body(): lax.all_to_all(pay, ('panel', 'rad', 'ang'), split_axis=0, concat_axis=0,...  4.9 us
    ppermute x2, starting transfers between devices, body(): beside = [lax.ppermute(adj, 'rad', swap), lax.ppermute(cond, 'rad', swap)]  4.8 us
    ppermute x4, starting transfers between devices, beside_rows(): return (lax.ppermute(mate, axes, pairs), lax.ppermute(next_, axes, links))  1.6 us
    ppermute x4, waiting for transfers between devices, beside_rows(): return (lax.ppermute(mate, axes, pairs), lax.ppermute(next_, axes, links))  0.85 us
    unnamed x18, local copies, waits for them, and re-layouts  0.79 us
    all_to_all x1, waiting for transfers between devices, body(): lax.all_to_all(pay, ('panel', 'rad', 'ang'), split_axis=0, concat_axis=0,...  0.59 us
    ppermute x2, starting transfers between devices, outer_rows(): return (lax.ppermute(mate, axes, pairs), lax.ppermute(next_, axes, links))  0.58 us
  transfers between devices with their start and end apart: 9, of which 2 were waited for; matrix products, arithmetic and copies ran while one was open for 0% of the time, Pallas kernels for 31%

profile of v7, /device:TPU:0, one launch (start us, length us, event | category | flops | bytes accessed | tf_op | source)
XLA Modules:
  0.0 22.2 jit_solution(15599643433760942127)
XLA Ops:
  0.0 3.0 %collective-permute-start = (f32[1,7,1,8,1536]{4,3,2,1,0:T(8,128)}, f32[1,7,1,8,1536]{4,3,2,1,0:T(8,128)}, u32[]{:S(2)}, u32[]{:S(2)}) collective-permute-start(f32[1,7,1,8,1536]{4,3,2,1,0:T(8,128)} %refs_0_.1), channel_id=1, source_target_pairs={{0,8},{8,0},{1,9},{9,1},{2,10},{10,2},{3,11},{11,3},{4,12},{12,4},... | collective-permute-start | bytes 1032200 | tf_op jit(solution)/shard_map/ppermute | solution.py:587
  3.0 2.2 %shard_map.112 = (f32[32,8,128]{2,1,0:T(8,128)}, f32[8,1536]{1,0:T(8,128)}, f32[8,1536]{1,0:T(8,128)}) custom-call(f32[1,7,1,8,1536]{4,3,2,1,0:T(8,128)} %refs_0_.1, f32[1,1,8,1536]{3,2,1,0:T(8,128)} %cond.9, f32[7]{0:T(128)} %refs_2_.3, s32[1,256]{1,0:T(1,128)} %bitcast.11, s32[1,1,4,256]{3,2,1,0:T(4,128)} %refs_4_.4, f32[1,1,4,256]{3,2,1,0:T(4,128)} %refs_5_.2, ...), custom_call_target="tpu_custom_call" | custom-call | tf_op jit(solution)/shard_map/pallas_call | solution.py:569
  5.2 0.0 copy-start
  5.2 0.0 copy-start.8
  5.2 0.0 copy-start.7
  5.2 4.9 %all-to-all-start = ((f32[32,8,128]{2,1,0:T(8,128)}), f32[32,8,128]{2,1,0:T(8,128)S(1)}, u32[]{:S(2)}, u32[]{:S(2)}) async-start(f32[32,8,128]{2,1,0:T(8,128)} %get-tuple-element.20), calls=%async_computation | async-start | bytes 262144 | tf_op jit(solution)/shard_map/all_to_all | solution.py:603
  10.1 0.0 copy-done
  10.1 1.8 %collective-permute-start.1 = (f32[1,1,8,1536]{3,2,1,0:T(8,128)S(1)}, f32[1,1,8,1536]{3,2,1,0:T(8,128)S(1)}, u32[]{:S(2)}, u32[]{:S(2)}) collective-permute-start(f32[1,1,8,1536]{3,2,1,0:T(8,128)S(1)} %copy-done), channel_id=1, source_target_pairs={{0,8},{8,0},{1,9},{9,1},{2,10},{10,2},{3,11},{11,3},{4,12},{12,4},... | collective-permute-start | bytes 147464 | tf_op jit(solution)/shard_map/ppermute | solution.py:587
  11.9 0.0 copy-done.8
  12.0 0.0 collective-permute-start.2
  12.0 0.0 copy-done.7
  12.0 0.0 copy-start.1
  12.0 0.3 %collective-permute-start.3 = (f32[8,1536]{1,0:T(8,128)S(1)}, f32[8,1536]{1,0:T(8,128)S(1)}, u32[]{:S(2)}, u32[]{:S(2)}) collective-permute-start(f32[8,1536]{1,0:T(8,128)S(1)} %copy-done.7), channel_id=1, source_target_pairs={{0,8},{1,2},{2,1},{3,4},{4,3},{5,6},{6,5},{7,15},{8,0},{9,10},{10,... | collective-permute-start | bytes 147464 | tf_op jit(solution)/shard_map/ppermute | solution.py:548
  12.3 0.0 collective-permute-done.adj2
  12.3 0.0 copy-start.2
  12.3 1.0 %shard_map.109.refs_0_.refs_1_ = f32[7,8,1536]{2,1,0:T(8,128)S(1)} custom-call(f32[1,7,1,8,1536]{4,3,2,1,0:T(8,128)} %collective-permute-done.adj2), custom_call_target="tpu_custom_call" | custom-call | bytes 16777216 | tf_op jit(solution)/shard_map/pallas_call | solution.py:569
  13.3 0.0 copy-start.3
  13.3 0.0 copy-done.1
  13.3 0.0 copy-done.2
  13.4 0.6 %copy-done.3 = f32[7]{0:T(128)S(1)} copy-done((f32[7]{0:T(128)S(1)}, f32[7]{0:T(128)}, u32[]{:S(2)}) %copy-start.3) | copy-done | bytes 52
  14.0 0.6 %shard_map.110 = (f32[7,8,1536]{2,1,0:T(8,128)S(1)}, f32[7,8,1536]{2,1,0:T(8,128)S(1)}) custom-call(f32[1,7,1,8,1536]{4,3,2,1,0:T(8,128)S(1)} %copy-done.1, f32[1,1,8,1536]{3,2,1,0:T(8,128)S(1)} %copy-done, f32[7,8,1536]{2,1,0:T(8,128)S(1)} %shard_map.109.refs_0_.refs_1_, f32[1,7]{1,0:T(1,128)S(1)} %bitcast.5, f32[7,7]{1,0:T(8,128)S(1)} %copy-done.2), custom_call_target="tpu_custom_call" | custom-call | tf_op jit(solution)/shard_map/pallas_call | solution.py:569
  14.6 0.0 collective-permute-done.1.refs_2_.refs_0_
  14.6 0.8 %shard_map.111 = (f32[7,8,1536]{2,1,0:T(8,128)S(1)}, f32[16,1536]{1,0:T(8,128)S(1)}, f32[16,1536]{1,0:T(8,128)S(1)}) custom-call(f32[1,1,8,1536]{3,2,1,0:T(8,128)S(1)} %copy-done, f32[7,8,1536]{2,1,0:T(8,128)S(1)} %get-tuple-element.17.first, f32[7,8,1536]{2,1,0:T(8,128)S(1)} %get-tuple-element.18.refs_0_, f32[7,8,1536]{2,1,0:T(8,128)S(1)} %shard_map.109.refs_0_.refs_1_, ...), custom_call_target="tpu_custom_call" | custom-call | tf_op jit(solution)/shard_map/pallas_call | solution.py:569
  15.4 0.0 collective-permute-done.2.refs_1_.mate_row
  15.4 0.8 %collective-permute-done.3.refs_2_.next_row = f32[8,1536]{1,0:T(8,128)S(1)} collective-permute-done((f32[8,1536]{1,0:T(8,128)S(1)}, f32[8,1536]{1,0:T(8,128)S(1)}, u32[]{:S(2)}, u32[]{:S(2)}) %collective-permute-start.3) | collective-permute-done | bytes 49184 | tf_op jit(solution)/shard_map/ppermute | solution.py:548
  16.3 0.2 shard_map.114
  16.4 1.0 %collective-permute-start.5 = (f32[15,1536]{1,0:T(8,128)S(1)}, f32[15,1536]{1,0:T(8,128)S(1)}, u32[]{:S(2)}, u32[]{:S(2)}) collective-permute-start(f32[15,1536]{1,0:T(8,128)S(1)} %get-tuple-element.26), channel_id=1, source_target_pairs={{0,8},{1,2},{2,1},{3,4},{4,3},{5,6},{6,5},{7,15},{8,0},{9,10},{10,... | collective-permute-start | bytes 276488 | tf_op jit(solution)/shard_map/ppermute | solution.py:548
  17.4 0.3 %collective-permute-start.4 = (f32[14,1536]{1,0:T(8,128)S(1)}, f32[14,1536]{1,0:T(8,128)S(1)}, u32[]{:S(2)}, u32[]{:S(2)}) collective-permute-start(f32[14,1536]{1,0:T(8,128)S(1)} %get-tuple-element.25), channel_id=1, source_target_pairs={{0,1},{1,0},{2,3},{3,2},{4,5},{5,4},{6,7},{7,6},{8,9},{9,8},{10,11... | collective-permute-start | bytes 258056 | tf_op jit(solution)/shard_map/ppermute | solution.py:548
  17.7 0.6 %all-to-all-done = f32[32,8,128]{2,1,0:T(8,128)S(1)} async-done(((f32[32,8,128]{2,1,0:T(8,128)}), f32[32,8,128]{2,1,0:T(8,128)S(1)}, u32[]{:S(2)}, u32[]{:S(2)}) %all-to-all-start) | async-done | bytes 131104 | tf_op jit(solution)/shard_map/all_to_all | solution.py:603
  18.3 0.0 copy-start.5
  18.3 0.0 copy-start.6
  18.3 0.0 copy-start.4
  18.3 0.4 %collective-permute-start.7 = (f32[2,1536]{1,0:T(2,128)S(1)}, f32[2,1536]{1,0:T(2,128)S(1)}, u32[]{:S(2)}, u32[]{:S(2)}) collective-permute-start(f32[2,1536]{1,0:T(2,128)S(1)} %get-tuple-element.28), channel_id=1, source_target_pairs={{0,1},{1,0},{2,3},{3,2},{4,5},{5,4},{6,7},{7,6},{8,24},{9,10},{10,... | collective-permute-start | bytes 36872 | tf_op jit(solution)/shard_map/ppermute | solution.py:565
  18.7 0.2 collective-permute-start.6
  18.9 0.1 copy-done.5
  19.0 0.0 copy-done.6
  19.0 0.0 copy-done.4
  19.0 2.2 %shard_map.113.late = f32[7,8,1536]{2,1,0:T(8,128)S(1)} custom-call(f32[7,8,1536]{2,1,0:T(8,128)S(1)} %get-tuple-element.19.early, f32[256,128]{1,0:T(8,128)S(1)} %bitcast.4, f32[1,1,8,1536]{3,2,1,0:T(8,128)S(1)} %copy-done, f32[1,1,8,1536]{3,2,1,0:T(8,128)S(1)} %collective-permute-done.1.refs_2_.refs_0_, ...), custom_call_target="tpu_custom_call" | custom-call | tf_op jit(solution)/shard_map/pallas_call | solution.py:569
  21.2 0.0 collective-permute-done.6.refs_3_
  21.2 0.0 collective-permute-done.7.refs_4_
  21.2 0.0 collective-permute-done.4.refs_1_
  21.3 0.0 collective-permute-done.5.refs_2_
  21.3 1.0 %shard_map.116 = f32[1,7,1,8,1536]{4,3,2,1,0:T(8,128)} custom-call(f32[7,8,1536]{2,1,0:T(8,128)S(1)} %shard_map.113.late, f32[1,1,8,1536]{3,2,1,0:T(8,128)S(1)} %collective-permute-done.1.refs_2_.refs_0_, f32[14,1536]{1,0:T(8,128)S(1)} %collective-permute-done.4.refs_1_, f32[15,1536]{1,0:T(8,128)S(1)} %collective-permute-done.5.refs_2_, ...), custom_call_target="tpu_custom_call" | custom-call | tf_op jit(solution)/shard_map/pallas_call | solution.py:569
  (1 shorter events, 0.0 us)
Async XLA Ops:
  0.0 12.3 %collective-permute-start = (f32[1,7,1,8,1536]{4,3,2,1,0:T(8,128)}, f32[1,7,1,8,1536]{4,3,2,1,0:T(8,128)}, u32[]{:S(2)}, u32[]{:S(2)}) collective-permute-start(f32[1,7,1,8,1536]{4,3,2,1,0:T(8,128)} %refs_0_.1), channel_id=1, source_target_pairs={{0,8},{8,0},{1,9},{9,1},{2,10},{10,2},{3,11},{11,3},{4,12},{12,4},... | collective-permute-start | bytes 1032200 | tf_op jit(solution)/shard_map/ppermute | solution.py:587
  5.2 4.9 %copy-start = (f32[1,1,8,1536]{3,2,1,0:T(8,128)S(1)}, f32[1,1,8,1536]{3,2,1,0:T(8,128)}, u32[]{:S(2)}) copy-start(f32[1,1,8,1536]{3,2,1,0:T(8,128)} %cond.9) | copy-start | bytes 147460
  5.2 6.8 %copy-start.8 = (f32[8,1536]{1,0:T(8,128)S(1)}, f32[8,1536]{1,0:T(8,128)}, u32[]{:S(2)}) copy-start(f32[8,1536]{1,0:T(8,128)} %get-tuple-element.21) | copy-start | bytes 147460
  5.2 6.8 %copy-start.7 = (f32[8,1536]{1,0:T(8,128)S(1)}, f32[8,1536]{1,0:T(8,128)}, u32[]{:S(2)}) copy-start(f32[8,1536]{1,0:T(8,128)} %get-tuple-element.22) | copy-start | bytes 147460
  5.2 13.1 %all-to-all-start = ((f32[32,8,128]{2,1,0:T(8,128)}), f32[32,8,128]{2,1,0:T(8,128)S(1)}, u32[]{:S(2)}, u32[]{:S(2)}) async-start(f32[32,8,128]{2,1,0:T(8,128)} %get-tuple-element.20), calls=%async_computation | async-start | bytes 262144 | tf_op jit(solution)/shard_map/all_to_all | solution.py:603
  10.1 4.5 %collective-permute-start.1 = (f32[1,1,8,1536]{3,2,1,0:T(8,128)S(1)}, f32[1,1,8,1536]{3,2,1,0:T(8,128)S(1)}, u32[]{:S(2)}, u32[]{:S(2)}) collective-permute-start(f32[1,1,8,1536]{3,2,1,0:T(8,128)S(1)} %copy-done), channel_id=1, source_target_pairs={{0,8},{8,0},{1,9},{9,1},{2,10},{10,2},{3,11},{11,3},{4,12},{12,4},... | collective-permute-start | bytes 147464 | tf_op jit(solution)/shard_map/ppermute | solution.py:587
  12.0 3.5 %collective-permute-start.2 = (f32[8,1536]{1,0:T(8,128)S(1)}, f32[8,1536]{1,0:T(8,128)S(1)}, u32[]{:S(2)}, u32[]{:S(2)}) collective-permute-start(f32[8,1536]{1,0:T(8,128)S(1)} %copy-done.8), channel_id=1, source_target_pairs={{0,1},{1,0},{2,3},{3,2},{4,5},{5,4},{6,7},{7,6},{8,9},{9,8},{10,11... | collective-permute-start | bytes 147464 | tf_op jit(solution)/shard_map/ppermute | solution.py:548
  12.0 1.4 %copy-start.1 = (f32[1,7,1,8,1536]{4,3,2,1,0:T(8,128)S(1)}, f32[1,7,1,8,1536]{4,3,2,1,0:T(8,128)}, u32[]{:S(2)}) copy-start(f32[1,7,1,8,1536]{4,3,2,1,0:T(8,128)} %refs_0_.1) | copy-start | bytes 1032196
  12.0 4.3 %collective-permute-start.3 = (f32[8,1536]{1,0:T(8,128)S(1)}, f32[8,1536]{1,0:T(8,128)S(1)}, u32[]{:S(2)}, u32[]{:S(2)}) collective-permute-start(f32[8,1536]{1,0:T(8,128)S(1)} %copy-done.7), channel_id=1, source_target_pairs={{0,8},{1,2},{2,1},{3,4},{4,3},{5,6},{6,5},{7,15},{8,0},{9,10},{10,... | collective-permute-start | bytes 147464 | tf_op jit(solution)/shard_map/ppermute | solution.py:548
  12.3 1.0 %copy-start.2 = (f32[7,7]{1,0:T(8,128)S(1)}, f32[7,7]{1,0:T(8,128)}, u32[]{:S(2)}) copy-start(f32[7,7]{1,0:T(8,128)} %refs_4_.5) | copy-start | bytes 592
  13.3 0.7 %copy-start.3 = (f32[7]{0:T(128)S(1)}, f32[7]{0:T(128)}, u32[]{:S(2)}) copy-start(f32[7]{0:T(128)} %refs_2_.3) | copy-start | bytes 88
  16.4 4.8 %collective-permute-start.5 = (f32[15,1536]{1,0:T(8,128)S(1)}, f32[15,1536]{1,0:T(8,128)S(1)}, u32[]{:S(2)}, u32[]{:S(2)}) collective-permute-start(f32[15,1536]{1,0:T(8,128)S(1)} %get-tuple-element.26), channel_id=1, source_target_pairs={{0,8},{1,2},{2,1},{3,4},{4,3},{5,6},{6,5},{7,15},{8,0},{9,10},{10,... | collective-permute-start | bytes 276488 | tf_op jit(solution)/shard_map/ppermute | solution.py:548
  17.4 3.8 %collective-permute-start.4 = (f32[14,1536]{1,0:T(8,128)S(1)}, f32[14,1536]{1,0:T(8,128)S(1)}, u32[]{:S(2)}, u32[]{:S(2)}) collective-permute-start(f32[14,1536]{1,0:T(8,128)S(1)} %get-tuple-element.25), channel_id=1, source_target_pairs={{0,1},{1,0},{2,3},{3,2},{4,5},{5,4},{6,7},{7,6},{8,9},{9,8},{10,11... | collective-permute-start | bytes 258056 | tf_op jit(solution)/shard_map/ppermute | solution.py:548
  18.3 0.7 %copy-start.5 = (s32[2,4,64]{2,1,0:T(4,128)S(1)}, s32[2,4,64]{2,1,0:T(4,128)}, u32[]{:S(2)}) copy-start(s32[2,4,64]{2,1,0:T(4,128)} %refs_6_.3) | copy-start | bytes 6148
  18.3 0.7 %copy-start.6 = (f32[2,4,64]{2,1,0:T(4,128)S(1)}, f32[2,4,64]{2,1,0:T(4,128)}, u32[]{:S(2)}) copy-start(f32[2,4,64]{2,1,0:T(4,128)} %refs_7_.1) | copy-start | bytes 6148
  18.3 0.7 %copy-start.4 = (s32[2,4,64]{2,1,0:T(4,128)S(1)}, s32[2,4,64]{2,1,0:T(4,128)}, u32[]{:S(2)}) copy-start(s32[2,4,64]{2,1,0:T(4,128)} %refs_5_.3) | copy-start | bytes 6148
  18.3 2.9 %collective-permute-start.7 = (f32[2,1536]{1,0:T(2,128)S(1)}, f32[2,1536]{1,0:T(2,128)S(1)}, u32[]{:S(2)}, u32[]{:S(2)}) collective-permute-start(f32[2,1536]{1,0:T(2,128)S(1)} %get-tuple-element.28), channel_id=1, source_target_pairs={{0,1},{1,0},{2,3},{3,2},{4,5},{5,4},{6,7},{7,6},{8,24},{9,10},{10,... | collective-permute-start | bytes 36872 | tf_op jit(solution)/shard_map/ppermute | solution.py:565
  18.7 2.5 %collective-permute-start.6 = (f32[1,1536]{1,0:T(1,128)S(1)}, f32[1,1536]{1,0:T(1,128)S(1)}, u32[]{:S(2)}, u32[]{:S(2)}) collective-permute-start(f32[1,1536]{1,0:T(1,128)S(1)} %get-tuple-element.27), channel_id=1, source_target_pairs={{0,1},{1,0},{2,3},{3,2},{4,5},{5,4},{6,7},{7,6},{8,9},{9,8},{10,11... | collective-permute-start | bytes 18440 | tf_op jit(solution)/shard_map/ppermute | solution.py:565

commit v8 on v7

--- a/solution.py
+++ b/solution.py
@@ -72,8 +72,7 @@
         self.npr = POINTS // self.spr
         self.feat_rows = 2 * self.npr + 1
         self.edge_rows = self.edge // LANES
-        self.strip = self.feat_rows + self.edge_rows
-        self.block = -(-(self.strip + 2) // SUBL) * SUBL
+        self.block = max(self.feat_rows + 1, self.edge_rows + 2)
         self.stencil = ghost_row.shape[1]
         self.hi = self.rows * self.cols // LOW
         self.pair = self.rads == 2
@@ -144,15 +143,29 @@
                 acc = jnp.where(lane == (f * 2 + inner) * z.rows + sub, line, acc)
         strips.append(jnp.sum(acc, axis=0, keepdims=True))
 
-    common = [edge_force[:, k * LANES : (k + 1) * LANES] for k in range(z.edge_rows)] + strips
-    spare = z.block - z.strip - 2
-    if spare:
-        common.append(jnp.zeros((spare, LANES), F32))
-    common = jnp.concatenate(common, axis=0)
+    acc = jnp.zeros((z.rows, LANES), F32)
+    for f in range(z.fields):
+        for side in range(2):
+            at = side * (z.cols - 1)
+            line = adj[0, f, 0, :, at : at + 1] * cond[0, 0, :, at : at + 1] * diffus[f]
+            acc = jnp.where(lane == (f * 2 + side) * z.rows + sub, line, acc)
+    edges = jnp.sum(acc, axis=0, keepdims=True)
+
+    def filled(rows):
+        used = sum(row.shape[0] for row in rows)
+        return rows + ([jnp.zeros((z.block - used, LANES), F32)] if used < z.block else [])
+
+    to_own, to_other = [], []
     for t in range(z.tiles):
-        part = jnp.concatenate([slots[:, t * LANES : (t + 1) * LANES], common], axis=0)
-        for group in range(z.panels * z.rads):
-            pay[group * z.tiles + t] = part
+        to_own += filled([slots[:, t * LANES : (t + 1) * LANES], edges])
+        to_other += filled([edge_force[:, k * LANES : (k + 1) * LANES] for k in range(z.edge_rows)] + strips)
+    to_own, to_other = jnp.concatenate(to_own, axis=0), jnp.concatenate(to_other, axis=0)
+    height = z.tiles * z.block
+    for panel in range(z.panels):
+        part = jnp.where(lax.axis_index("panel") == panel, to_own, to_other)
+        for rad in range(z.rads):
+            at = (panel * z.rads + rad) * height
+            pay[at : at + height, :] = part
 
     for f in range(z.fields):
         mate[f : f + 1, :], next_[f : f + 1, :] = facing(adj[0, f, 0] * (cond[0, 0] * diffus[f]))
@@ -186,13 +199,16 @@
     return dif, mix
 
 
-def unpack_strips(z, recv, sets):
+def unpack_strips(z, recv, sets, own):
+    def base(panel, rad):
+        return (panel * z.rads + rad) * z.tiles * z.block
+
     height = 2 * z.tiles
     stacked = []
     for panel, rad in sets:
-        base = (panel * z.rads + rad) * z.tiles * z.block + z.strip
         for side in range(2):
-            stacked.append(recv[pl.ds(base + side, z.tiles, stride=z.block), :])
+            stacked.append(recv[pl.ds(base(panel, rad) + z.edge_rows + side, z.tiles, stride=z.block), :])
+    stacked.append(recv[pl.ds(base(*own) + z.feat_rows, z.tiles, stride=z.block), :])
     stacked = jnp.concatenate(stacked, axis=0)
     width = 2 * SUBL * z.edge
     lane = iota((LANES, width), 1)
@@ -213,7 +229,18 @@
                 rows.append(jnp.sum(jnp.where(keep, tile, 0.0), axis=0, keepdims=True))
             both.append(jnp.concatenate(rows, axis=0))
         out.append(both)
-    return out
+    lane = iota((z.tiles, z.edge), 1)
+    side = lane // z.total_rows
+    keep = (lane % z.total_rows) // z.rows == iota((z.tiles, z.edge), 0)
+    rows = []
+    for f in range(z.fields):
+        first, last = [
+            moved[len(sets) * height :, (k * SUBL + f) * z.edge : (k * SUBL + f + 1) * z.edge] for k in range(2)
+        ]
+        tile = jnp.where(side == 0, first, last)
+        rows.append(jnp.sum(jnp.where(keep, tile, 0.0), axis=0, keepdims=True))
+    rows.append(jnp.zeros((SUBL - z.fields, z.edge), F32))
+    return out, jnp.concatenate(rows, axis=0)
 
 
 def edge_scaled(z, values, dif):
@@ -407,14 +434,14 @@
     outer = jnp.where(rad == z.rads - 1, 1.0, 0.0)
     above, below = around(z, mate_in[...], next_in[...])
 
-    sets = [(other, rad), (panel, rad)]
+    sets = [(other, rad)]
     if z.pair:
         sets.append((other, 1 - rad))
         near = [1.0]
     else:
         sets += [(other, jnp.maximum(rad - 1, 0)), (other, jnp.minimum(rad + 1, z.rads - 1))]
         near = [jnp.where(rad > 0, 1.0, 0.0), jnp.where(rad < z.rads - 1, 1.0, 0.0)]
-    strips = unpack_strips(z, recv, sets)
+    strips, home_s = unpack_strips(z, recv, sets, (panel, rad))
     dif, mix = weights_of(z, steps, couple, z.rows, z.cols)
     plane = iota((SUBL, z.edge), 0)
     by_plane = jnp.zeros((SUBL, z.edge), F32)
@@ -422,8 +449,7 @@
         by_plane = jnp.where(plane == f, wide(steps[:, f : f + 1], SUBL, z.edge), by_plane)
     rim, inside = strips[0]
     rim_s = edge_scaled(z, rim, by_plane)
-    home_s = edge_scaled(z, strips[1][0], by_plane)
-    layers_s = [edge_scaled(z, strips[2 + k][0], by_plane) for k in range(len(near))]
+    layers_s = [edge_scaled(z, strips[1 + k][0], by_plane) for k in range(len(near))]
     lap = edge_scaled(z, inside, by_plane) - 6.0 * rim_s
     for k, one in enumerate(near):
         lap = lap + layers_s[k] * one
@@ -447,7 +473,7 @@
     sources = z.rads * z.tiles
     pulse = []
     for k in range(z.edge_rows):
-        at = other * sources * z.block + z.feat_rows + k
+        at = other * sources * z.block + k
         pulse.append(jnp.sum(recv[pl.ds(at, sources, stride=z.block), :], axis=0, keepdims=True))
     pulse = jnp.concatenate(pulse, axis=1) * outer
     rim_first = rim + lap + mixed + rim_ghost
@@ -594,12 +620,13 @@
     held = [pltpu.SMEM(x.shape, x.dtype) if x is diffus else pltpu.VMEM(x.shape, x.dtype) for x in given]
     pay, *rows = call(
         functools.partial(pack_kernel, z),
-        [(z.devices, z.block, LANES), line, line],
+        [(z.devices * z.block, LANES), line, line],
         held + [pltpu.SemaphoreType.DMA((len(given),))],
         given,
         spaces=pltpu.HBM,
         room=64,
     )
+    pay = pay.reshape(z.devices, 1, z.block * LANES)
     recv = lax.all_to_all(pay, ("panel", "rad", "ang"), split_axis=0, concat_axis=0, tiled=True)
     recv = recv.reshape(z.devices * z.block, LANES)
     rows = list(beside_rows(z, *rows, "rad"))

time: 22.5 us -> 22.4 us (level)
    all_to_all x1, waiting for transfers between devices: 0.59 us -> 0.32 us  [body(): lax.all_to_all(pay, ('panel', 'rad', 'ang'), split_axis=0, concat_axis=0,...]
    ppermute x4, waiting for transfers between devices: 0.85 us -> 1.1 us  [beside_rows(): return (lax.ppermute(mate, axes, pairs), lax.ppermute(next_, axes, links))]
  transfers between devices with their start and end apart: 9 -> 9, of which waited for: 2 -> 3; matrix products, arithmetic and copies ran while one was open for 0% -> 0% of each run, Pallas kernels for 31% -> 32%
where the time goes in v8:
time: 22.4 us; the launch traced here: 22.1 us
  starting transfers between devices  11.7 us (52%)
  Pallas kernels  8.01 us (36%)
  waiting for transfers between devices  1.43 us (6%)
  local copies, waits for them, and re-layouts  0.79 us (4%)
    pallas_call x8, Pallas kernels, call(): pl.pallas_call(kernel, out_shape=[jax.ShapeDtypeStruct(shape, F32) for sh...  8.01 us
    all_to_all x1, starting transfers between devices, body(): lax.all_to_all(pay, ('panel', 'rad', 'ang'), split_axis=0, concat_axis=0,...  4.9 us
    ppermute x2, starting transfers between devices, body(): beside = [lax.ppermute(adj, 'rad', swap), lax.ppermute(cond, 'rad', swap)]  4.8 us
    ppermute x4, starting transfers between devices, beside_rows(): return (lax.ppermute(mate, axes, pairs), lax.ppermute(next_, axes, links))  1.45 us
    ppermute x4, waiting for transfers between devices, beside_rows(): return (lax.ppermute(mate, axes, pairs), lax.ppermute(next_, axes, links))  1.1 us
    unnamed x18, local copies, waits for them, and re-layouts  0.79 us
    ppermute x2, starting transfers between devices, outer_rows(): return (lax.ppermute(mate, axes, pairs), lax.ppermute(next_, axes, links))  0.58 us
  transfers between devices with their start and end apart: 9, of which 3 were waited for; matrix products, arithmetic and copies ran while one was open for 0% of the time, Pallas kernels for 32%

profile of v8, /device:TPU:0, one launch (start us, length us, event | category | flops | bytes accessed | tf_op | source)
XLA Modules:
  0.0 22.1 jit_solution(2365018865248940474)
XLA Ops:
  0.0 3.0 %collective-permute-start = (f32[1,7,1,8,1536]{4,3,2,1,0:T(8,128)}, f32[1,7,1,8,1536]{4,3,2,1,0:T(8,128)}, u32[]{:S(2)}, u32[]{:S(2)}) collective-permute-start(f32[1,7,1,8,1536]{4,3,2,1,0:T(8,128)} %refs_0_.1), channel_id=1, source_target_pairs={{0,8},{8,0},{1,9},{9,1},{2,10},{10,2},{3,11},{11,3},{4,12},{12,4},... | collective-permute-start | bytes 1032200 | tf_op jit(solution)/shard_map/ppermute | solution.py:613
  3.0 2.2 %shard_map.112 = (f32[192,128]{1,0:T(8,128)}, f32[8,1536]{1,0:T(8,128)}, f32[8,1536]{1,0:T(8,128)}) custom-call(f32[1,7,1,8,1536]{4,3,2,1,0:T(8,128)} %refs_0_.1, f32[1,1,8,1536]{3,2,1,0:T(8,128)} %cond.9, f32[7]{0:T(128)} %refs_2_.3, s32[1,256]{1,0:T(1,128)} %bitcast.13, s32[1,1,4,256]{3,2,1,0:T(4,128)} %refs_4_.4, f32[1,1,4,256]{3,2,1,0:T(4,128)} %refs_5_.2, ...), custom_call_target="tpu_custom_call" | custom-call | tf_op jit(solution)/shard_map/pallas_call | solution.py:595
  5.2 0.0 copy-start
  5.2 0.0 copy-start.8
  5.2 0.0 copy-start.7
  5.2 4.9 %all-to-all-start = ((f32[32,1,768]{2,1,0:T(1,128)}), f32[32,1,768]{2,1,0:T(1,128)S(1)}, u32[]{:S(2)}, u32[]{:S(2)}) async-start(f32[32,1,768]{2,1,0:T(1,128)} %bitcast.12), calls=%async_computation | async-start | bytes 196608 | tf_op jit(solution)/shard_map/all_to_all | solution.py:630
  10.1 0.0 copy-done
  10.1 1.8 %collective-permute-start.1 = (f32[1,1,8,1536]{3,2,1,0:T(8,128)S(1)}, f32[1,1,8,1536]{3,2,1,0:T(8,128)S(1)}, u32[]{:S(2)}, u32[]{:S(2)}) collective-permute-start(f32[1,1,8,1536]{3,2,1,0:T(8,128)S(1)} %copy-done), channel_id=1, source_target_pairs={{0,8},{8,0},{1,9},{9,1},{2,10},{10,2},{3,11},{11,3},{4,12},{12,4},... | collective-permute-start | bytes 147464 | tf_op jit(solution)/shard_map/ppermute | solution.py:613
  12.0 0.0 copy-done.8
  12.0 0.0 collective-permute-start.2
  12.0 0.0 copy-done.7
  12.0 0.0 copy-start.1
  12.0 0.3 %collective-permute-start.3 = (f32[8,1536]{1,0:T(8,128)S(1)}, f32[8,1536]{1,0:T(8,128)S(1)}, u32[]{:S(2)}, u32[]{:S(2)}) collective-permute-start(f32[8,1536]{1,0:T(8,128)S(1)} %copy-done.7), channel_id=1, source_target_pairs={{0,8},{1,2},{2,1},{3,4},{4,3},{5,6},{6,5},{7,15},{8,0},{9,10},{10,... | collective-permute-start | bytes 147464 | tf_op jit(solution)/shard_map/ppermute | solution.py:574
  12.3 0.0 collective-permute-done.adj2
  12.3 0.0 copy-start.2
  12.3 1.0 %shard_map.109.refs_0_.refs_1_ = f32[7,8,1536]{2,1,0:T(8,128)S(1)} custom-call(f32[1,7,1,8,1536]{4,3,2,1,0:T(8,128)} %collective-permute-done.adj2), custom_call_target="tpu_custom_call" | custom-call | bytes 16777216 | tf_op jit(solution)/shard_map/pallas_call | solution.py:595
  13.3 0.0 copy-start.3
  13.3 0.0 copy-done.1
  13.4 0.0 copy-done.2
  13.4 0.6 %copy-done.3 = f32[7]{0:T(128)S(1)} copy-done((f32[7]{0:T(128)S(1)}, f32[7]{0:T(128)}, u32[]{:S(2)}) %copy-start.3) | copy-done | bytes 52
  14.0 0.6 %shard_map.110 = (f32[7,8,1536]{2,1,0:T(8,128)S(1)}, f32[7,8,1536]{2,1,0:T(8,128)S(1)}) custom-call(f32[1,7,1,8,1536]{4,3,2,1,0:T(8,128)S(1)} %copy-done.1, f32[1,1,8,1536]{3,2,1,0:T(8,128)S(1)} %copy-done, f32[7,8,1536]{2,1,0:T(8,128)S(1)} %shard_map.109.refs_0_.refs_1_, f32[1,7]{1,0:T(1,128)S(1)} %bitcast.6, f32[7,7]{1,0:T(8,128)S(1)} %copy-done.2), custom_call_target="tpu_custom_call" | custom-call | tf_op jit(solution)/shard_map/pallas_call | solution.py:595
  14.6 0.0 collective-permute-done.1.refs_2_.refs_0_
  14.7 0.8 %shard_map.111 = (f32[7,8,1536]{2,1,0:T(8,128)S(1)}, f32[16,1536]{1,0:T(8,128)S(1)}, f32[16,1536]{1,0:T(8,128)S(1)}) custom-call(f32[1,1,8,1536]{3,2,1,0:T(8,128)S(1)} %copy-done, f32[7,8,1536]{2,1,0:T(8,128)S(1)} %get-tuple-element.17.first, f32[7,8,1536]{2,1,0:T(8,128)S(1)} %get-tuple-element.18.refs_0_, f32[7,8,1536]{2,1,0:T(8,128)S(1)} %shard_map.109.refs_0_.refs_1_, ...), custom_call_target="tpu_custom_call" | custom-call | tf_op jit(solution)/shard_map/pallas_call | solution.py:595
  15.4 0.0 collective-permute-done.2.refs_1_.mate_row
  15.4 0.9 %collective-permute-done.3.refs_2_.next_row = f32[8,1536]{1,0:T(8,128)S(1)} collective-permute-done((f32[8,1536]{1,0:T(8,128)S(1)}, f32[8,1536]{1,0:T(8,128)S(1)}, u32[]{:S(2)}, u32[]{:S(2)}) %collective-permute-start.3) | collective-permute-done | bytes 49184 | tf_op jit(solution)/shard_map/ppermute | solution.py:574
  16.3 0.2 shard_map.114
  16.5 1.0 %collective-permute-start.5 = (f32[15,1536]{1,0:T(8,128)S(1)}, f32[15,1536]{1,0:T(8,128)S(1)}, u32[]{:S(2)}, u32[]{:S(2)}) collective-permute-start(f32[15,1536]{1,0:T(8,128)S(1)} %get-tuple-element.26), channel_id=1, source_target_pairs={{0,8},{1,2},{2,1},{3,4},{4,3},{5,6},{6,5},{7,15},{8,0},{9,10},{10,... | collective-permute-start | bytes 276488 | tf_op jit(solution)/shard_map/ppermute | solution.py:574
  17.4 0.1 collective-permute-start.4
  17.6 0.3 %all-to-all-done = f32[32,1,768]{2,1,0:T(1,128)S(1)} async-done(((f32[32,1,768]{2,1,0:T(1,128)}), f32[32,1,768]{2,1,0:T(1,128)S(1)}, u32[]{:S(2)}, u32[]{:S(2)}) %all-to-all-start) | async-done | bytes 98336 | tf_op jit(solution)/shard_map/all_to_all | solution.py:630
  17.9 0.0 copy-start.5
  17.9 0.0 copy-start.6
  17.9 0.0 copy-start.4
  17.9 0.3 %collective-permute-start.7 = (f32[2,1536]{1,0:T(2,128)S(1)}, f32[2,1536]{1,0:T(2,128)S(1)}, u32[]{:S(2)}, u32[]{:S(2)}) collective-permute-start(f32[2,1536]{1,0:T(2,128)S(1)} %get-tuple-element.28), channel_id=1, source_target_pairs={{0,1},{1,0},{2,3},{3,2},{4,5},{5,4},{6,7},{7,6},{8,24},{9,10},{10,... | collective-permute-start | bytes 36872 | tf_op jit(solution)/shard_map/ppermute | solution.py:591
  18.2 0.3 %collective-permute-start.6 = (f32[1,1536]{1,0:T(1,128)S(1)}, f32[1,1536]{1,0:T(1,128)S(1)}, u32[]{:S(2)}, u32[]{:S(2)}) collective-permute-start(f32[1,1536]{1,0:T(1,128)S(1)} %get-tuple-element.27), channel_id=1, source_target_pairs={{0,1},{1,0},{2,3},{3,2},{4,5},{5,4},{6,7},{7,6},{8,9},{9,8},{10,11... | collective-permute-start | bytes 18440 | tf_op jit(solution)/shard_map/ppermute | solution.py:591
  18.5 0.1 copy-done.5
  18.6 0.0 copy-done.6
  18.6 0.0 copy-done.4
  18.6 2.2 %shard_map.113.late = f32[7,8,1536]{2,1,0:T(8,128)S(1)} custom-call(f32[7,8,1536]{2,1,0:T(8,128)S(1)} %get-tuple-element.19.early, f32[192,128]{1,0:T(8,128)S(1)} %bitcast.5, f32[1,1,8,1536]{3,2,1,0:T(8,128)S(1)} %copy-done, f32[1,1,8,1536]{3,2,1,0:T(8,128)S(1)} %collective-permute-done.1.refs_2_.refs_0_, ...), custom_call_target="tpu_custom_call" | custom-call | tf_op jit(solution)/shard_map/pallas_call | solution.py:595
  20.9 0.0 collective-permute-done.6.refs_3_
  20.9 0.0 collective-permute-done.7.refs_4_
  20.9 0.0 collective-permute-done.4.refs_1_
  20.9 0.2 %collective-permute-done.5.refs_2_ = f32[15,1536]{1,0:T(8,128)S(1)} collective-permute-done((f32[15,1536]{1,0:T(8,128)S(1)}, f32[15,1536]{1,0:T(8,128)S(1)}, u32[]{:S(2)}, u32[]{:S(2)}) %collective-permute-start.5) | collective-permute-done | bytes 92192 | tf_op jit(solution)/shard_map/ppermute | solution.py:574
  21.1 1.0 %shard_map.116 = f32[1,7,1,8,1536]{4,3,2,1,0:T(8,128)} custom-call(f32[7,8,1536]{2,1,0:T(8,128)S(1)} %shard_map.113.late, f32[1,1,8,1536]{3,2,1,0:T(8,128)S(1)} %collective-permute-done.1.refs_2_.refs_0_, f32[14,1536]{1,0:T(8,128)S(1)} %collective-permute-done.4.refs_1_, f32[15,1536]{1,0:T(8,128)S(1)} %collective-permute-done.5.refs_2_, ...), custom_call_target="tpu_custom_call" | custom-call | tf_op jit(solution)/shard_map/pallas_call | solution.py:595
  (1 shorter events, 0.0 us)
Async XLA Ops:
  0.0 12.3 %collective-permute-start = (f32[1,7,1,8,1536]{4,3,2,1,0:T(8,128)}, f32[1,7,1,8,1536]{4,3,2,1,0:T(8,128)}, u32[]{:S(2)}, u32[]{:S(2)}) collective-permute-start(f32[1,7,1,8,1536]{4,3,2,1,0:T(8,128)} %refs_0_.1), channel_id=1, source_target_pairs={{0,8},{8,0},{1,9},{9,1},{2,10},{10,2},{3,11},{11,3},{4,12},{12,4},... | collective-permute-start | bytes 1032200 | tf_op jit(solution)/shard_map/ppermute | solution.py:613
  5.2 4.9 %copy-start = (f32[1,1,8,1536]{3,2,1,0:T(8,128)S(1)}, f32[1,1,8,1536]{3,2,1,0:T(8,128)}, u32[]{:S(2)}) copy-start(f32[1,1,8,1536]{3,2,1,0:T(8,128)} %cond.9) | copy-start | bytes 147460
  5.2 6.8 %copy-start.8 = (f32[8,1536]{1,0:T(8,128)S(1)}, f32[8,1536]{1,0:T(8,128)}, u32[]{:S(2)}) copy-start(f32[8,1536]{1,0:T(8,128)} %get-tuple-element.21) | copy-start | bytes 147460
  5.2 6.8 %copy-start.7 = (f32[8,1536]{1,0:T(8,128)S(1)}, f32[8,1536]{1,0:T(8,128)}, u32[]{:S(2)}) copy-start(f32[8,1536]{1,0:T(8,128)} %get-tuple-element.22) | copy-start | bytes 147460
  5.2 12.7 %all-to-all-start = ((f32[32,1,768]{2,1,0:T(1,128)}), f32[32,1,768]{2,1,0:T(1,128)S(1)}, u32[]{:S(2)}, u32[]{:S(2)}) async-start(f32[32,1,768]{2,1,0:T(1,128)} %bitcast.12), calls=%async_computation | async-start | bytes 196608 | tf_op jit(solution)/shard_map/all_to_all | solution.py:630
  10.1 4.5 %collective-permute-start.1 = (f32[1,1,8,1536]{3,2,1,0:T(8,128)S(1)}, f32[1,1,8,1536]{3,2,1,0:T(8,128)S(1)}, u32[]{:S(2)}, u32[]{:S(2)}) collective-permute-start(f32[1,1,8,1536]{3,2,1,0:T(8,128)S(1)} %copy-done), channel_id=1, source_target_pairs={{0,8},{8,0},{1,9},{9,1},{2,10},{10,2},{3,11},{11,3},{4,12},{12,4},... | collective-permute-start | bytes 147464 | tf_op jit(solution)/shard_map/ppermute | solution.py:613
  12.0 3.5 %collective-permute-start.2 = (f32[8,1536]{1,0:T(8,128)S(1)}, f32[8,1536]{1,0:T(8,128)S(1)}, u32[]{:S(2)}, u32[]{:S(2)}) collective-permute-start(f32[8,1536]{1,0:T(8,128)S(1)} %copy-done.8), channel_id=1, source_target_pairs={{0,1},{1,0},{2,3},{3,2},{4,5},{5,4},{6,7},{7,6},{8,9},{9,8},{10,11... | collective-permute-start | bytes 147464 | tf_op jit(solution)/shard_map/ppermute | solution.py:574
  12.0 1.4 %copy-start.1 = (f32[1,7,1,8,1536]{4,3,2,1,0:T(8,128)S(1)}, f32[1,7,1,8,1536]{4,3,2,1,0:T(8,128)}, u32[]{:S(2)}) copy-start(f32[1,7,1,8,1536]{4,3,2,1,0:T(8,128)} %refs_0_.1) | copy-start | bytes 1032196
  12.0 4.3 %collective-permute-start.3 = (f32[8,1536]{1,0:T(8,128)S(1)}, f32[8,1536]{1,0:T(8,128)S(1)}, u32[]{:S(2)}, u32[]{:S(2)}) collective-permute-start(f32[8,1536]{1,0:T(8,128)S(1)} %copy-done.7), channel_id=1, source_target_pairs={{0,8},{1,2},{2,1},{3,4},{4,3},{5,6},{6,5},{7,15},{8,0},{9,10},{10,... | collective-permute-start | bytes 147464 | tf_op jit(solution)/shard_map/ppermute | solution.py:574
  12.3 1.0 %copy-start.2 = (f32[7,7]{1,0:T(8,128)S(1)}, f32[7,7]{1,0:T(8,128)}, u32[]{:S(2)}) copy-start(f32[7,7]{1,0:T(8,128)} %refs_4_.5) | copy-start | bytes 592
  13.3 0.7 %copy-start.3 = (f32[7]{0:T(128)S(1)}, f32[7]{0:T(128)}, u32[]{:S(2)}) copy-start(f32[7]{0:T(128)} %refs_2_.3) | copy-start | bytes 88
  16.5 4.7 %collective-permute-start.5 = (f32[15,1536]{1,0:T(8,128)S(1)}, f32[15,1536]{1,0:T(8,128)S(1)}, u32[]{:S(2)}, u32[]{:S(2)}) collective-permute-start(f32[15,1536]{1,0:T(8,128)S(1)} %get-tuple-element.26), channel_id=1, source_target_pairs={{0,8},{1,2},{2,1},{3,4},{4,3},{5,6},{6,5},{7,15},{8,0},{9,10},{10,... | collective-permute-start | bytes 276488 | tf_op jit(solution)/shard_map/ppermute | solution.py:574
  17.4 3.5 %collective-permute-start.4 = (f32[14,1536]{1,0:T(8,128)S(1)}, f32[14,1536]{1,0:T(8,128)S(1)}, u32[]{:S(2)}, u32[]{:S(2)}) collective-permute-start(f32[14,1536]{1,0:T(8,128)S(1)} %get-tuple-element.25), channel_id=1, source_target_pairs={{0,1},{1,0},{2,3},{3,2},{4,5},{5,4},{6,7},{7,6},{8,9},{9,8},{10,11... | collective-permute-start | bytes 258056 | tf_op jit(solution)/shard_map/ppermute | solution.py:574
  17.9 0.7 %copy-start.5 = (s32[2,4,64]{2,1,0:T(4,128)S(1)}, s32[2,4,64]{2,1,0:T(4,128)}, u32[]{:S(2)}) copy-start(s32[2,4,64]{2,1,0:T(4,128)} %refs_6_.3) | copy-start | bytes 6148
  17.9 0.7 %copy-start.6 = (f32[2,4,64]{2,1,0:T(4,128)S(1)}, f32[2,4,64]{2,1,0:T(4,128)}, u32[]{:S(2)}) copy-start(f32[2,4,64]{2,1,0:T(4,128)} %refs_7_.1) | copy-start | bytes 6148
  17.9 0.7 %copy-start.4 = (s32[2,4,64]{2,1,0:T(4,128)S(1)}, s32[2,4,64]{2,1,0:T(4,128)}, u32[]{:S(2)}) copy-start(s32[2,4,64]{2,1,0:T(4,128)} %refs_5_.3) | copy-start | bytes 6148
  17.9 3.0 %collective-permute-start.7 = (f32[2,1536]{1,0:T(2,128)S(1)}, f32[2,1536]{1,0:T(2,128)S(1)}, u32[]{:S(2)}, u32[]{:S(2)}) collective-permute-start(f32[2,1536]{1,0:T(2,128)S(1)} %get-tuple-element.28), channel_id=1, source_target_pairs={{0,1},{1,0},{2,3},{3,2},{4,5},{5,4},{6,7},{7,6},{8,24},{9,10},{10,... | collective-permute-start | bytes 36872 | tf_op jit(solution)/shard_map/ppermute | solution.py:591
  18.2 2.7 %collective-permute-start.6 = (f32[1,1536]{1,0:T(1,128)S(1)}, f32[1,1536]{1,0:T(1,128)S(1)}, u32[]{:S(2)}, u32[]{:S(2)}) collective-permute-start(f32[1,1536]{1,0:T(1,128)S(1)} %get-tuple-element.27), channel_id=1, source_target_pairs={{0,1},{1,0},{2,3},{3,2},{4,5},{5,4},{6,7},{7,6},{8,9},{9,8},{10,11... | collective-permute-start | bytes 18440 | tf_op jit(solution)/shard_map/ppermute | solution.py:591

commit v9 on v8

--- a/solution.py
+++ b/solution.py
@@ -46,8 +46,13 @@
     return jnp.concatenate([tile] * (height // 16), axis=0)
 
 
-def matches(row, height):
-    return iota((height, row.shape[1]), 0).astype(F32).astype(BF16) == tall(row.astype(F32), height)
+def numbers(height, width):
+    return iota((height, width), 0).astype(F32).astype(BF16)
+
+
+def matches(row, height, rows=None):
+    rows = numbers(height, row.shape[1]) if rows is None else rows
+    return rows == tall(row.astype(F32), height)
 
 
 def onehot(index, height):
@@ -210,12 +215,11 @@
             stacked.append(recv[pl.ds(base(panel, rad) + z.edge_rows + side, z.tiles, stride=z.block), :])
     stacked.append(recv[pl.ds(base(*own) + z.feat_rows, z.tiles, stride=z.block), :])
     stacked = jnp.concatenate(stacked, axis=0)
-    width = 2 * SUBL * z.edge
-    lane = iota((LANES, width), 1)
+    lane = iota((1, 2 * SUBL * z.edge), 1)
     slot = lane // z.edge
     inner, plane = slot // SUBL, slot % SUBL
-    picks = (iota((LANES, width), 0) == (plane * 2 + inner) * z.rows + lane % z.rows).astype(F32)
-    moved = joint_dot(stacked, picks.astype(BF16), 3, (((1,), (0,)), ((), ())))
+    picks = onehot((plane * 2 + inner) * z.rows + lane % z.rows, LANES)
+    moved = joint_dot(stacked, picks, 3, (((1,), (0,)), ((), ())))
     lane = iota((height, z.edge), 1)
     keep = lane // z.rows == iota((height, z.edge), 0)
     out = []
@@ -278,18 +282,19 @@
 def dealt(z, values, highs, lows, height, spread_a, spread_b):
     width = spread_b.shape[0]
     sources = highs[0].shape[0]
-    zero, one = jnp.zeros((height, LANES), BF16), jnp.ones((width, LANES), BF16)
+    zero, none, one = jnp.zeros((height, LANES), BF16), jnp.zeros((width, LANES), BF16), jnp.ones((width, LANES), BF16)
+    rows_high, rows_low = numbers(height, LANES), numbers(width, LANES)
     for h in range(z.npr):
         parts = []
         for value in values[h]:
             parts += [part.astype(F32) for part in parts_of(value, 2)]
         for n in range(sources):
             at = (n * z.npr + h) * LANES
-            hit = matches(highs[h][n : n + 1], height)
+            hit = matches(highs[h][n : n + 1], height, rows_high)
             for k, part in enumerate(parts):
                 spread_a[k * height : (k + 1) * height, at : at + LANES] = jnp.where(hit, tall(part[n : n + 1], height), zero)
-            hit = matches(lows[h][n : n + 1], width)
-            spread_b[:, at : at + LANES] = jnp.where(hit, one, jnp.zeros_like(one))
+            hit = matches(lows[h][n : n + 1], width, rows_low)
+            spread_b[:, at : at + LANES] = jnp.where(hit, one, none)
     grid = lax.dot_general(spread_a[...], spread_b[...], NT_DIMS, preferred_element_type=F32)
     return [
         grid[2 * k * height : (2 * k + 1) * height] + grid[(2 * k + 1) * height : (2 * k + 2) * height]
@@ -654,7 +659,7 @@
         [],
         [cond, steps] + rows + [mate, next_],
     )
-    beyond = list(beside_rows(z, *links, "rad"))
+    beyond = list(beside_rows(z, *links, "panel"))
     points = z.rads * z.tiles * z.npr * LANES
     ends = 2 * (-(-z.cols // LANES // 16) * 16)
     ends = call(

time: 22.4 us -> 22.4 us (level)
  waiting for transfers between devices: 1.43 us -> 0.92 us
  starting transfers between devices: 11.7 us -> 12.2 us
    ppermute x4, starting transfers between devices: 1.45 us -> 1.9 us  [beside_rows(): return (lax.ppermute(mate, axes, pairs), lax.ppermute(next_, axes, links))]
    all_to_all x1, waiting for transfers between devices: 0.32 us -> 0.01 us  [body(): lax.all_to_all(pay, ('panel', 'rad', 'ang'), split_axis=0, concat_axis=0,...]
  transfers between devices with their start and end apart: 9 -> 9, of which waited for: 3 -> 1; matrix products, arithmetic and copies ran while one was open for 0% -> 0% of each run, Pallas kernels for 32% -> 32%
where the time goes in v9:
time: 22.4 us; the launch traced here: 22.1 us
  starting transfers between devices  12.2 us (54%)
  Pallas kernels  8.07 us (36%)
  waiting for transfers between devices  0.92 us (4%)
  local copies, waits for them, and re-layouts  0.71 us (3%)
    pallas_call x8, Pallas kernels, call(): pl.pallas_call(kernel, out_shape=[jax.ShapeDtypeStruct(shape, F32) for sh...  8.07 us
    all_to_all x1, starting transfers between devices, body(): lax.all_to_all(pay, ('panel', 'rad', 'ang'), split_axis=0, concat_axis=0,...  4.9 us
    ppermute x2, starting transfers between devices, body(): beside = [lax.ppermute(adj, 'rad', swap), lax.ppermute(cond, 'rad', swap)]  4.8 us
    ppermute x4, starting transfers between devices, beside_rows(): return (lax.ppermute(mate, axes, pairs), lax.ppermute(next_, axes, links))  1.9 us
    ppermute x4, waiting for transfers between devices, beside_rows(): return (lax.ppermute(mate, axes, pairs), lax.ppermute(next_, axes, links))  0.91 us
    unnamed x18, local copies, waits for them, and re-layouts  0.71 us
    ppermute x2, starting transfers between devices, outer_rows(): return (lax.ppermute(mate, axes, pairs), lax.ppermute(next_, axes, links))  0.63 us
  transfers between devices with their start and end apart: 9, of which 1 were waited for; matrix products, arithmetic and copies ran while one was open for 0% of the time, Pallas kernels for 32%

profile of v9, /device:TPU:0, one launch (start us, length us, event | category | flops | bytes accessed | tf_op | source)
XLA Modules:
  0.0 22.1 jit_solution(10262359301658797203)
XLA Ops:
  0.0 3.0 %collective-permute-start = (f32[1,7,1,8,1536]{4,3,2,1,0:T(8,128)}, f32[1,7,1,8,1536]{4,3,2,1,0:T(8,128)}, u32[]{:S(2)}, u32[]{:S(2)}) collective-permute-start(f32[1,7,1,8,1536]{4,3,2,1,0:T(8,128)} %refs_0_.1), channel_id=1, source_target_pairs={{0,8},{8,0},{1,9},{9,1},{2,10},{10,2},{3,11},{11,3},{4,12},{12,4},... | collective-permute-start | bytes 1032200 | tf_op jit(solution)/shard_map/ppermute | solution.py:618
  3.0 2.2 %shard_map.112 = (f32[192,128]{1,0:T(8,128)}, f32[8,1536]{1,0:T(8,128)}, f32[8,1536]{1,0:T(8,128)}) custom-call(f32[1,7,1,8,1536]{4,3,2,1,0:T(8,128)} %refs_0_.1, f32[1,1,8,1536]{3,2,1,0:T(8,128)} %cond.9, f32[7]{0:T(128)} %refs_2_.3, s32[1,256]{1,0:T(1,128)} %bitcast.13, s32[1,1,4,256]{3,2,1,0:T(4,128)} %refs_4_.4, f32[1,1,4,256]{3,2,1,0:T(4,128)} %refs_5_.2, ...), custom_call_target="tpu_custom_call" | custom-call | tf_op jit(solution)/shard_map/pallas_call | solution.py:600
  5.2 0.0 copy-start
  5.2 0.0 copy-start.8
  5.2 0.0 copy-start.7
  5.2 4.9 %all-to-all-start = ((f32[32,1,768]{2,1,0:T(1,128)}), f32[32,1,768]{2,1,0:T(1,128)S(1)}, u32[]{:S(2)}, u32[]{:S(2)}) async-start(f32[32,1,768]{2,1,0:T(1,128)} %bitcast.12), calls=%async_computation | async-start | bytes 196608 | tf_op jit(solution)/shard_map/all_to_all | solution.py:635
  10.1 0.0 copy-done
  10.1 1.8 %collective-permute-start.1 = (f32[1,1,8,1536]{3,2,1,0:T(8,128)S(1)}, f32[1,1,8,1536]{3,2,1,0:T(8,128)S(1)}, u32[]{:S(2)}, u32[]{:S(2)}) collective-permute-start(f32[1,1,8,1536]{3,2,1,0:T(8,128)S(1)} %copy-done), channel_id=1, source_target_pairs={{0,8},{8,0},{1,9},{9,1},{2,10},{10,2},{3,11},{11,3},{4,12},{12,4},... | collective-permute-start | bytes 147464 | tf_op jit(solution)/shard_map/ppermute | solution.py:618
  12.0 0.0 copy-done.8
  12.0 0.0 collective-permute-start.2
  12.0 0.0 copy-done.7
  12.0 0.0 copy-start.1
  12.0 0.3 %collective-permute-start.3 = (f32[8,1536]{1,0:T(8,128)S(1)}, f32[8,1536]{1,0:T(8,128)S(1)}, u32[]{:S(2)}, u32[]{:S(2)}) collective-permute-start(f32[8,1536]{1,0:T(8,128)S(1)} %copy-done.7), channel_id=1, source_target_pairs={{0,8},{1,2},{2,1},{3,4},{4,3},{5,6},{6,5},{7,15},{8,0},{9,10},{10,... | collective-permute-start | bytes 147464 | tf_op jit(solution)/shard_map/ppermute | solution.py:579
  12.3 0.0 collective-permute-done.adj2
  12.3 0.0 copy-start.2
  12.3 1.0 %shard_map.109.refs_0_.refs_1_ = f32[7,8,1536]{2,1,0:T(8,128)S(1)} custom-call(f32[1,7,1,8,1536]{4,3,2,1,0:T(8,128)} %collective-permute-done.adj2), custom_call_target="tpu_custom_call" | custom-call | bytes 16777216 | tf_op jit(solution)/shard_map/pallas_call | solution.py:600
  13.3 0.0 copy-start.3
  13.3 0.0 copy-done.1
  13.4 0.0 copy-done.2
  13.4 0.6 %copy-done.3 = f32[7]{0:T(128)S(1)} copy-done((f32[7]{0:T(128)S(1)}, f32[7]{0:T(128)}, u32[]{:S(2)}) %copy-start.3) | copy-done | bytes 52
  14.0 0.6 %shard_map.110 = (f32[7,8,1536]{2,1,0:T(8,128)S(1)}, f32[7,8,1536]{2,1,0:T(8,128)S(1)}) custom-call(f32[1,7,1,8,1536]{4,3,2,1,0:T(8,128)S(1)} %copy-done.1, f32[1,1,8,1536]{3,2,1,0:T(8,128)S(1)} %copy-done, f32[7,8,1536]{2,1,0:T(8,128)S(1)} %shard_map.109.refs_0_.refs_1_, f32[1,7]{1,0:T(1,128)S(1)} %bitcast.6, f32[7,7]{1,0:T(8,128)S(1)} %copy-done.2), custom_call_target="tpu_custom_call" | custom-call | tf_op jit(solution)/shard_map/pallas_call | solution.py:600
  14.6 0.0 collective-permute-done.1.refs_2_.refs_0_
  14.7 0.8 %shard_map.111 = (f32[7,8,1536]{2,1,0:T(8,128)S(1)}, f32[16,1536]{1,0:T(8,128)S(1)}, f32[16,1536]{1,0:T(8,128)S(1)}) custom-call(f32[1,1,8,1536]{3,2,1,0:T(8,128)S(1)} %copy-done, f32[7,8,1536]{2,1,0:T(8,128)S(1)} %get-tuple-element.17.first, f32[7,8,1536]{2,1,0:T(8,128)S(1)} %get-tuple-element.18.refs_0_, f32[7,8,1536]{2,1,0:T(8,128)S(1)} %shard_map.109.refs_0_.refs_1_, ...), custom_call_target="tpu_custom_call" | custom-call | tf_op jit(solution)/shard_map/pallas_call | solution.py:600
  15.4 0.0 collective-permute-done.2.refs_1_.mate_row
  15.4 0.9 %collective-permute-done.3.refs_2_.next_row = f32[8,1536]{1,0:T(8,128)S(1)} collective-permute-done((f32[8,1536]{1,0:T(8,128)S(1)}, f32[8,1536]{1,0:T(8,128)S(1)}, u32[]{:S(2)}, u32[]{:S(2)}) %collective-permute-start.3) | collective-permute-done | bytes 49184 | tf_op jit(solution)/shard_map/ppermute | solution.py:579
  16.3 0.2 shard_map.114
  16.5 1.6 %collective-permute-start.5 = (f32[15,1536]{1,0:T(8,128)S(1)}, f32[15,1536]{1,0:T(8,128)S(1)}, u32[]{:S(2)}, u32[]{:S(2)}) collective-permute-start(f32[15,1536]{1,0:T(8,128)S(1)} %get-tuple-element.26), channel_id=1, source_target_pairs={{0,16},{1,2},{2,1},{3,4},{4,3},{5,6},{6,5},{7,23},{8,24},{9,10},{1... | collective-permute-start | bytes 276488 | tf_op jit(solution)/shard_map/ppermute | solution.py:579
  18.0 0.0 collective-permute-start.4
  18.0 0.0 all-to-all-done
  18.0 0.0 copy-start.5
  18.0 0.0 copy-start.6
  18.1 0.0 copy-start.4
  18.1 0.6 %collective-permute-start.7 = (f32[2,1536]{1,0:T(2,128)S(1)}, f32[2,1536]{1,0:T(2,128)S(1)}, u32[]{:S(2)}, u32[]{:S(2)}) collective-permute-start(f32[2,1536]{1,0:T(2,128)S(1)} %get-tuple-element.28), channel_id=1, source_target_pairs={{0,1},{1,0},{2,3},{3,2},{4,5},{5,4},{6,7},{7,6},{8,24},{9,10},{10,... | collective-permute-start | bytes 36872 | tf_op jit(solution)/shard_map/ppermute | solution.py:596
  18.7 0.1 collective-permute-start.6
  18.7 0.0 copy-done.5
  18.7 0.0 copy-done.6
  18.7 0.0 copy-done.4
  18.8 2.3 %shard_map.113.late = f32[7,8,1536]{2,1,0:T(8,128)S(1)} custom-call(f32[7,8,1536]{2,1,0:T(8,128)S(1)} %get-tuple-element.19.early, f32[192,128]{1,0:T(8,128)S(1)} %bitcast.5, f32[1,1,8,1536]{3,2,1,0:T(8,128)S(1)} %copy-done, f32[1,1,8,1536]{3,2,1,0:T(8,128)S(1)} %collective-permute-done.1.refs_2_.refs_0_, ...), custom_call_target="tpu_custom_call" | custom-call | tf_op jit(solution)/shard_map/pallas_call | solution.py:600
  21.1 0.0 collective-permute-done.6.refs_3_
  21.1 0.0 collective-permute-done.7.refs_4_
  21.1 0.0 collective-permute-done.4.refs_1_
  21.1 0.0 collective-permute-done.5.refs_2_
  21.1 1.0 %shard_map.116 = f32[1,7,1,8,1536]{4,3,2,1,0:T(8,128)} custom-call(f32[7,8,1536]{2,1,0:T(8,128)S(1)} %shard_map.113.late, f32[1,1,8,1536]{3,2,1,0:T(8,128)S(1)} %collective-permute-done.1.refs_2_.refs_0_, f32[14,1536]{1,0:T(8,128)S(1)} %collective-permute-done.4.refs_1_, f32[15,1536]{1,0:T(8,128)S(1)} %collective-permute-done.5.refs_2_, ...), custom_call_target="tpu_custom_call" | custom-call | tf_op jit(solution)/shard_map/pallas_call | solution.py:600
  (1 shorter events, 0.0 us)
Async XLA Ops:
  0.0 12.3 %collective-permute-start = (f32[1,7,1,8,1536]{4,3,2,1,0:T(8,128)}, f32[1,7,1,8,1536]{4,3,2,1,0:T(8,128)}, u32[]{:S(2)}, u32[]{:S(2)}) collective-permute-start(f32[1,7,1,8,1536]{4,3,2,1,0:T(8,128)} %refs_0_.1), channel_id=1, source_target_pairs={{0,8},{8,0},{1,9},{9,1},{2,10},{10,2},{3,11},{11,3},{4,12},{12,4},... | collective-permute-start | bytes 1032200 | tf_op jit(solution)/shard_map/ppermute | solution.py:618
  5.2 4.9 %copy-start = (f32[1,1,8,1536]{3,2,1,0:T(8,128)S(1)}, f32[1,1,8,1536]{3,2,1,0:T(8,128)}, u32[]{:S(2)}) copy-start(f32[1,1,8,1536]{3,2,1,0:T(8,128)} %cond.9) | copy-start | bytes 147460
  5.2 6.8 %copy-start.8 = (f32[8,1536]{1,0:T(8,128)S(1)}, f32[8,1536]{1,0:T(8,128)}, u32[]{:S(2)}) copy-start(f32[8,1536]{1,0:T(8,128)} %get-tuple-element.21) | copy-start | bytes 147460
  5.2 6.8 %copy-start.7 = (f32[8,1536]{1,0:T(8,128)S(1)}, f32[8,1536]{1,0:T(8,128)}, u32[]{:S(2)}) copy-start(f32[8,1536]{1,0:T(8,128)} %get-tuple-element.22) | copy-start | bytes 147460
  5.2 12.8 %all-to-all-start = ((f32[32,1,768]{2,1,0:T(1,128)}), f32[32,1,768]{2,1,0:T(1,128)S(1)}, u32[]{:S(2)}, u32[]{:S(2)}) async-start(f32[32,1,768]{2,1,0:T(1,128)} %bitcast.12), calls=%async_computation | async-start | bytes 196608 | tf_op jit(solution)/shard_map/all_to_all | solution.py:635
  10.1 4.5 %collective-permute-start.1 = (f32[1,1,8,1536]{3,2,1,0:T(8,128)S(1)}, f32[1,1,8,1536]{3,2,1,0:T(8,128)S(1)}, u32[]{:S(2)}, u32[]{:S(2)}) collective-permute-start(f32[1,1,8,1536]{3,2,1,0:T(8,128)S(1)} %copy-done), channel_id=1, source_target_pairs={{0,8},{8,0},{1,9},{9,1},{2,10},{10,2},{3,11},{11,3},{4,12},{12,4},... | collective-permute-start | bytes 147464 | tf_op jit(solution)/shard_map/ppermute | solution.py:618
  12.0 3.5 %collective-permute-start.2 = (f32[8,1536]{1,0:T(8,128)S(1)}, f32[8,1536]{1,0:T(8,128)S(1)}, u32[]{:S(2)}, u32[]{:S(2)}) collective-permute-start(f32[8,1536]{1,0:T(8,128)S(1)} %copy-done.8), channel_id=1, source_target_pairs={{0,1},{1,0},{2,3},{3,2},{4,5},{5,4},{6,7},{7,6},{8,9},{9,8},{10,11... | collective-permute-start | bytes 147464 | tf_op jit(solution)/shard_map/ppermute | solution.py:579
  12.0 1.4 %copy-start.1 = (f32[1,7,1,8,1536]{4,3,2,1,0:T(8,128)S(1)}, f32[1,7,1,8,1536]{4,3,2,1,0:T(8,128)}, u32[]{:S(2)}) copy-start(f32[1,7,1,8,1536]{4,3,2,1,0:T(8,128)} %refs_0_.1) | copy-start | bytes 1032196
  12.0 4.3 %collective-permute-start.3 = (f32[8,1536]{1,0:T(8,128)S(1)}, f32[8,1536]{1,0:T(8,128)S(1)}, u32[]{:S(2)}, u32[]{:S(2)}) collective-permute-start(f32[8,1536]{1,0:T(8,128)S(1)} %copy-done.7), channel_id=1, source_target_pairs={{0,8},{1,2},{2,1},{3,4},{4,3},{5,6},{6,5},{7,15},{8,0},{9,10},{10,... | collective-permute-start | bytes 147464 | tf_op jit(solution)/shard_map/ppermute | solution.py:579
  12.3 1.0 %copy-start.2 = (f32[7,7]{1,0:T(8,128)S(1)}, f32[7,7]{1,0:T(8,128)}, u32[]{:S(2)}) copy-start(f32[7,7]{1,0:T(8,128)} %refs_4_.5) | copy-start | bytes 592
  13.3 0.7 %copy-start.3 = (f32[7]{0:T(128)S(1)}, f32[7]{0:T(128)}, u32[]{:S(2)}) copy-start(f32[7]{0:T(128)} %refs_2_.3) | copy-start | bytes 88
  16.5 4.7 %collective-permute-start.5 = (f32[15,1536]{1,0:T(8,128)S(1)}, f32[15,1536]{1,0:T(8,128)S(1)}, u32[]{:S(2)}, u32[]{:S(2)}) collective-permute-start(f32[15,1536]{1,0:T(8,128)S(1)} %get-tuple-element.26), channel_id=1, source_target_pairs={{0,16},{1,2},{2,1},{3,4},{4,3},{5,6},{6,5},{7,23},{8,24},{9,10},{1... | collective-permute-start | bytes 276488 | tf_op jit(solution)/shard_map/ppermute | solution.py:579
  18.0 3.1 %collective-permute-start.4 = (f32[14,1536]{1,0:T(8,128)S(1)}, f32[14,1536]{1,0:T(8,128)S(1)}, u32[]{:S(2)}, u32[]{:S(2)}) collective-permute-start(f32[14,1536]{1,0:T(8,128)S(1)} %get-tuple-element.25), channel_id=1, source_target_pairs={{0,1},{1,0},{2,3},{3,2},{4,5},{5,4},{6,7},{7,6},{8,9},{9,8},{10,11... | collective-permute-start | bytes 258056 | tf_op jit(solution)/shard_map/ppermute | solution.py:579
  18.0 0.7 %copy-start.5 = (s32[2,4,64]{2,1,0:T(4,128)S(1)}, s32[2,4,64]{2,1,0:T(4,128)}, u32[]{:S(2)}) copy-start(s32[2,4,64]{2,1,0:T(4,128)} %refs_6_.3) | copy-start | bytes 6148
  18.0 0.7 %copy-start.6 = (f32[2,4,64]{2,1,0:T(4,128)S(1)}, f32[2,4,64]{2,1,0:T(4,128)}, u32[]{:S(2)}) copy-start(f32[2,4,64]{2,1,0:T(4,128)} %refs_7_.1) | copy-start | bytes 6148
  18.1 0.7 %copy-start.4 = (s32[2,4,64]{2,1,0:T(4,128)S(1)}, s32[2,4,64]{2,1,0:T(4,128)}, u32[]{:S(2)}) copy-start(s32[2,4,64]{2,1,0:T(4,128)} %refs_5_.3) | copy-start | bytes 6148
  18.1 3.0 %collective-permute-start.7 = (f32[2,1536]{1,0:T(2,128)S(1)}, f32[2,1536]{1,0:T(2,128)S(1)}, u32[]{:S(2)}, u32[]{:S(2)}) collective-permute-start(f32[2,1536]{1,0:T(2,128)S(1)} %get-tuple-element.28), channel_id=1, source_target_pairs={{0,1},{1,0},{2,3},{3,2},{4,5},{5,4},{6,7},{7,6},{8,24},{9,10},{10,... | collective-permute-start | bytes 36872 | tf_op jit(solution)/shard_map/ppermute | solution.py:596
  18.7 2.4 %collective-permute-start.6 = (f32[1,1536]{1,0:T(1,128)S(1)}, f32[1,1536]{1,0:T(1,128)S(1)}, u32[]{:S(2)}, u32[]{:S(2)}) collective-permute-start(f32[1,1536]{1,0:T(1,128)S(1)} %get-tuple-element.27), channel_id=1, source_target_pairs={{0,1},{1,0},{2,3},{3,2},{4,5},{5,4},{6,7},{7,6},{8,9},{9,8},{10,11... | collective-permute-start | bytes 18440 | tf_op jit(solution)/shard_map/ppermute | solution.py:596
